TPU v7x, 256 devices: a whole 4x4x8 slice. The times are simulated.
256 devices in a mesh: segment: 2 (over z_hi), space: 16 (over z_lo, x), chan: 8 (over y, core).
Axes of the slice: x: 4, y: 4, z: 8 (z_hi: 2, z_lo: 4; z = z_hi * 4 + z_lo), core: 2. Of those that a mesh axis runs over, the one named last changes fastest.
Arguments:
- acts: float32 [2, 1, 768, 18432], P('segment', None, 'chan', 'space'), may hold values from -6 to 6
- cotangent: float32 [1, 768, 18432], P(None, 'chan', 'space'), may hold values from -6 to 6
- w_in: float32 [2, 2, 8, 96, 96], P('segment', None, 'chan'), may hold values from -0.4375 to 0.4375
- w_out: float32 [2, 2, 8, 96, 96], P('segment', None, 'chan'), may hold values from -0.4375 to 0.4375
- b_in: float32 [2, 2, 768], P('segment', None, 'chan'), may hold values from -3 to 3
- b_out: float32 [2, 2, 768], P('segment', None, 'chan'), may hold values from -3 to 3
Outputs:
- adjoints: float32 [2, 1, 768, 18432], P('segment', None, 'chan', 'space')
- grad_w_in: float32 [2, 2, 8, 96, 96], P('segment', None, 'chan')
- grad_w_out: float32 [2, 2, 8, 96, 96], P('segment', None, 'chan')
- grad_b_in: float32 [2, 2, 768], P('segment', None, 'chan')
- grad_b_out: float32 [2, 2, 768], P('segment', None, 'chan')
All inputs are finite; a program needn't handle non-finite values.
Results may differ from a plain program's by a relative error of at most 0.0059.
Values sent between devices are 32-bit elements; how exact they have to be, the bound alone decides.
No kernel may reach another device: no remote copies, remote signals or barrier semaphores. Data moves between devices by JAX's collectives and lax.ppermute only.
A program may use at most 64 MiB of HBM per device.

v0:
```python
import math

import jax
import jax.numpy as jnp
from jax import lax
from jax.sharding import PartitionSpec as P

H = 96
W = 192


exact = lax.Precision.HIGHEST
shrink = 0.3


def shifted(block, axis, distance):
    devices = range(lax.axis_size(axis))
    route = [(i - distance, i) for i in devices if i - distance in devices]
    return lax.ppermute(block, axis, route)


def dft_tables(length):
    counter = jnp.arange(length, dtype=jnp.int32)
    product = counter[:, None] * counter[None, :] % length
    phase = product.astype(jnp.float32) * (2.0 * math.pi / length)
    factor = 1.0 / math.sqrt(length)
    return (jnp.cos(phase) * factor, jnp.sin(phase) * factor)


def along_width(field, dft_table):
    return jnp.einsum("...chw,wv->...chv", field, dft_table, precision=exact)


def along_height(dft_table, field):
    return jnp.einsum("uh,chv->cuv", dft_table, field, precision=exact)


def split_groups(field, group_size):
    return field.reshape((field.shape[0] // group_size, group_size) + field.shape[1:])


def complex_mix(real_part, imag_part, weight, offsets):
    group_size = weight.shape[2]
    real_split = split_groups(real_part, group_size)
    imag_split = split_groups(imag_part, group_size)
    out_real = jnp.einsum("giuv,gij->gjuv", real_split, weight[0], precision=exact) - jnp.einsum(
        "giuv,gij->gjuv", imag_split, weight[1], precision=exact
    )
    out_imag = jnp.einsum("giuv,gij->gjuv", real_split, weight[1], precision=exact) + jnp.einsum(
        "giuv,gij->gjuv", imag_split, weight[0], precision=exact
    )
    return (
        out_real.reshape(real_part.shape) + offsets[0][:, None, None],
        out_imag.reshape(real_part.shape) + offsets[1][:, None, None],
    )


def mix_adjoint(real_part, imag_part, weight, grad_real, grad_imag):
    group_size = weight.shape[2]
    real_split = split_groups(real_part, group_size)
    imag_split = split_groups(imag_part, group_size)
    gr_split = split_groups(grad_real, group_size)
    gi_split = split_groups(grad_imag, group_size)
    weight_zero = jnp.einsum("giuv,gjuv->gij", real_split, gr_split, precision=exact) + jnp.einsum(
        "giuv,gjuv->gij", imag_split, gi_split, precision=exact
    )
    weight_one = jnp.einsum("giuv,gjuv->gij", real_split, gi_split, precision=exact) - jnp.einsum(
        "giuv,gjuv->gij", imag_split, gr_split, precision=exact
    )
    offset_grad = jnp.stack([jnp.sum(grad_real, axis=(1, 2)), jnp.sum(grad_imag, axis=(1, 2))])
    in_real = jnp.einsum("gjuv,gij->giuv", gr_split, weight[0], precision=exact) + jnp.einsum(
        "gjuv,gij->giuv", gi_split, weight[1], precision=exact
    )
    in_imag = jnp.einsum("gjuv,gij->giuv", gi_split, weight[0], precision=exact) - jnp.einsum(
        "gjuv,gij->giuv", gr_split, weight[1], precision=exact
    )
    return (
        jnp.stack([weight_zero, weight_one]),
        offset_grad,
        in_real.reshape(real_part.shape),
        in_imag.reshape(real_part.shape),
    )


def section_adjoint(spec_r, spec_i, upstream, params, tables):
    weight_one, weight_two, offset_one, offset_two = params
    cos_w, sin_w, cos_h, sin_h = tables
    freq_r = along_height(cos_h, spec_r) + along_height(sin_h, spec_i)
    freq_i = along_height(cos_h, spec_i) - along_height(sin_h, spec_r)
    hid_r, hid_i = complex_mix(freq_r, freq_i, weight_one, offset_one)
    act_r = jax.nn.relu(hid_r)
    act_i = jax.nn.relu(hid_i)
    out_r, out_i = complex_mix(act_r, act_i, weight_two, offset_two)
    back_r, back_i = (
        lax.all_to_all(
            along_width(upstream, cos_w), "space", split_axis=2, concat_axis=1, tiled=True
        ),
        lax.all_to_all(
            -along_width(upstream, sin_w), "space", split_axis=2, concat_axis=1, tiled=True
        ),
    )
    shr_r = along_height(cos_h, back_r) + along_height(sin_h, back_i)
    shr_i = along_height(cos_h, back_i) - along_height(sin_h, back_r)
    grad_out_r = jnp.where(jnp.abs(out_r) > shrink, shr_r, 0.0)
    grad_out_i = jnp.where(jnp.abs(out_i) > shrink, shr_i, 0.0)
    grad_two, grad_off_two, grad_act_r, grad_act_i = mix_adjoint(
        act_r, act_i, weight_two, grad_out_r, grad_out_i
    )
    grad_hid_r = jnp.where(hid_r > 0.0, grad_act_r, 0.0)
    grad_hid_i = jnp.where(hid_i > 0.0, grad_act_i, 0.0)
    grad_one, grad_off_one, grad_freq_r, grad_freq_i = mix_adjoint(
        freq_r, freq_i, weight_one, grad_hid_r, grad_hid_i
    )
    grad_spec_r = along_height(cos_h, grad_freq_r) - along_height(sin_h, grad_freq_i)
    grad_spec_i = along_height(sin_h, grad_freq_r) + along_height(cos_h, grad_freq_i)
    rows_r, rows_i = (
        lax.all_to_all(grad_spec_r, "space", split_axis=1, concat_axis=2, tiled=True),
        lax.all_to_all(grad_spec_i, "space", split_axis=1, concat_axis=2, tiled=True),
    )
    field_grad = upstream + along_width(rows_r, cos_w) - along_width(rows_i, sin_w)
    return (field_grad, (grad_one, grad_two, grad_off_one, grad_off_two))


def shards(acts, cotangent, w_in, w_out, b_in, b_out):
    segment_idx = lax.axis_index("segment")
    segments = lax.axis_size("segment")
    flat_inputs = acts[0]
    micro_count = flat_inputs.shape[0]
    channels = flat_inputs.shape[1]
    row_count = H // lax.axis_size("space")
    inputs = flat_inputs.reshape(micro_count, channels, row_count, W)
    cos_w, sin_w = dft_tables(W)
    cos_h, sin_h = dft_tables(H)
    tables = (cos_w, sin_w, cos_h, sin_h)
    params = (w_in[0], w_out[0], b_in[0], b_out[0])
    totals = (
        jnp.zeros(w_in[0].shape, jnp.float32),
        jnp.zeros(w_out[0].shape, jnp.float32),
        jnp.zeros(b_in[0].shape, jnp.float32),
        jnp.zeros(b_out[0].shape, jnp.float32),
    )
    carried = jnp.zeros(inputs.shape[1:], jnp.float32)
    adjoints = jnp.zeros(flat_inputs.shape, jnp.float32)
    turns = micro_count + segments - 1
    for position in range(turns):
        micro = position - (segments - 1) + segment_idx
        active_mask = (micro >= 0) & (micro < micro_count)
        micro_index = jnp.clip(micro, 0, micro_count - 1)
        given_adjoint = lax.dynamic_index_in_dim(cotangent, micro_index, 0, keepdims=False).reshape(
            inputs.shape[1:]
        )
        upstream = jnp.where(segment_idx == segments - 1, given_adjoint, carried)
        block_input = lax.dynamic_index_in_dim(inputs, micro_index, 0, keepdims=False)
        spec_r, spec_i = (
            lax.all_to_all(
                along_width(block_input, cos_w), "space", split_axis=2, concat_axis=1, tiled=True
            ),
            lax.all_to_all(
                -along_width(block_input, sin_w), "space", split_axis=2, concat_axis=1, tiled=True
            ),
        )
        field_grad, gradients = section_adjoint(spec_r, spec_i, upstream, params, tables)
        scale_factor = jnp.where(active_mask, 1.0, 0.0).astype(jnp.float32)
        gradients = tuple((scale_factor * entry for entry in gradients))
        gradients = lax.psum(gradients, "space")
        totals = tuple((total + entry for total, entry in zip(totals, gradients)))
        flat_grad = field_grad.reshape(channels, row_count * W)
        adjoints = jnp.where(
            active_mask,
            lax.dynamic_update_index_in_dim(adjoints, flat_grad, micro_index, 0),
            adjoints,
        )
        if position + 1 < turns:
            carried = shifted(field_grad, "segment", -1)
    return (adjoints[None], totals[0][None], totals[1][None], totals[2][None], totals[3][None])


def solution(mesh):
    placed = (
        P("segment", None, "chan", "space"),
        P(None, "chan", "space"),
        P("segment", None, "chan", None, None),
        P("segment", None, "chan", None, None),
        P("segment", None, "chan"),
        P("segment", None, "chan"),
    )
    return jax.shard_map(
        shards,
        mesh=mesh,
        in_specs=placed,
        out_specs=(
            P("segment", None, "chan", "space"),
            P("segment", None, "chan", None, None),
            P("segment", None, "chan", None, None),
            P("segment", None, "chan"),
            P("segment", None, "chan"),
        ),
        check_vma=False,
    )
```

profile of v0, /device:TPU:8, one launch (start us, length us, event | category | flops | bytes accessed | tf_op | source)
XLA Modules:
  0.0 501.4 jit_solution(9098200548360277567)
XLA Ops:
  8.4 1.4 convolution_bitcast_fusion
  11.2 8.5 %all-to-all-start = ((f32[96,6,192]{0,1,2:T(8,128)}), f32[96,6,192]{0,1,2:T(8,128)S(1)}, u32[]{:S(2)}, u32[]{:S(2)}) async-start(f32[96,6,192]{0,1,2:T(8,128)} %copy.150), calls=%async_computation | async-start | bytes 1572864 | tf_op jit(solution)/shard_map/all_to_all | solution.py:155
  19.6 1.4 fusion.30
  22.9 16.8 %all-to-all-done = f32[96,6,192]{0,1,2:T(8,128)S(1)} async-done(((f32[96,6,192]{0,1,2:T(8,128)}), f32[96,6,192]{0,1,2:T(8,128)S(1)}, u32[]{:S(2)}, u32[]{:S(2)}) %all-to-all-start) | async-done | bytes 442400 | tf_op jit(solution)/shard_map/all_to_all | solution.py:155
  39.7 5.3 %all-to-all-start.1 = ((f32[96,6,192]{0,1,2:T(8,128)}), f32[96,6,192]{0,1,2:T(8,128)}, u32[]{:S(2)}, u32[]{:S(2)}) async-start(f32[96,6,192]{0,1,2:T(8,128)} %copy.156), calls=%async_computation.1 | async-start | bytes 1572864 | tf_op jit(solution)/shard_map/all_to_all | solution.py:158
  53.1 10.9 %all-to-all-done.1 = f32[96,6,192]{0,1,2:T(8,128)} async-done(((f32[96,6,192]{0,1,2:T(8,128)}), f32[96,6,192]{0,1,2:T(8,128)}, u32[]{:S(2)}, u32[]{:S(2)}) %all-to-all-start.1) | async-done | bytes 442400 | tf_op jit(solution)/shard_map/all_to_all | solution.py:158
  64.0 5.5 %all-to-all-start.3 = ((f32[96,6,192]{0,1,2:T(8,128)}), f32[96,6,192]{0,1,2:T(8,128)}, u32[]{:S(2)}, u32[]{:S(2)}) async-start(f32[96,6,192]{0,1,2:T(8,128)} %copy.170), calls=%async_computation.3 | async-start | bytes 1572864 | tf_op jit(solution)/shard_map/all_to_all | solution.py:98
  69.6 2.1 copy.158
  82.8 5.7 %all-to-all-done.3 = f32[96,6,192]{0,1,2:T(8,128)} async-done(((f32[96,6,192]{0,1,2:T(8,128)}), f32[96,6,192]{0,1,2:T(8,128)}, u32[]{:S(2)}, u32[]{:S(2)}) %all-to-all-start.3) | async-done | bytes 442400 | tf_op jit(solution)/shard_map/all_to_all | solution.py:98
  88.5 5.8 %all-to-all-start.2 = ((f32[96,6,192]{0,1,2:T(8,128)}), f32[96,6,192]{0,1,2:T(8,128)}, u32[]{:S(2)}, u32[]{:S(2)}) async-start(f32[96,6,192]{0,1,2:T(8,128)} %copy.166), calls=%async_computation.2 | async-start | bytes 1572864 | tf_op jit(solution)/shard_map/all_to_all | solution.py:95
  95.1 2.1 copy.172
  98.4 1.7 fusion.231
  102.9 10.0 %all-to-all-done.2 = f32[96,6,192]{0,1,2:T(8,128)} async-done(((f32[96,6,192]{0,1,2:T(8,128)}), f32[96,6,192]{0,1,2:T(8,128)}, u32[]{:S(2)}, u32[]{:S(2)}) %all-to-all-start.2) | async-done | bytes 442400 | tf_op jit(solution)/shard_map/all_to_all | solution.py:95
  112.9 2.1 copy.168
  115.0 2.0 all_to_all.151
  117.1 2.0 fusion.233
  131.2 2.0 fusion.12
  133.3 2.3 copy.184
  135.5 5.3 %all-to-all-start.5 = ((f32[96,96,12]{0,2,1:T(8,128)}), f32[96,96,12]{0,2,1:T(8,128)}, u32[]{:S(2)}, u32[]{:S(2)}) async-start(f32[96,96,12]{0,2,1:T(8,128)} %copy.184), calls=%async_computation.5 | async-start | bytes 1572864 | tf_op jit(solution)/shard_map/all_to_all | solution.py:118
  140.9 2.3 fusion.229
  143.2 2.0 fusion.13
  145.2 2.3 copy.178
  147.5 12.4 %all-to-all-done.5 = f32[96,96,12]{0,2,1:T(8,128)} async-done(((f32[96,96,12]{0,2,1:T(8,128)}), f32[96,96,12]{0,2,1:T(8,128)}, u32[]{:S(2)}, u32[]{:S(2)}) %all-to-all-start.5) | async-done | bytes 442400 | tf_op jit(solution)/shard_map/all_to_all | solution.py:118
  159.9 5.4 %all-to-all-start.4 = ((f32[96,96,12]{0,2,1:T(8,128)}), f32[96,96,12]{0,2,1:T(8,128)}, u32[]{:S(2)}, u32[]{:S(2)}) async-start(f32[96,96,12]{0,2,1:T(8,128)} %copy.178), calls=%async_computation.4 | async-start | bytes 1572864 | tf_op jit(solution)/shard_map/all_to_all | solution.py:117
  165.2 2.1 copy.186
  167.3 2.0 all_to_all.163
  169.3 14.9 %all-to-all-done.4 = f32[96,96,12]{0,2,1:T(8,128)} async-done(((f32[96,96,12]{0,2,1:T(8,128)}), f32[96,96,12]{0,2,1:T(8,128)}, u32[]{:S(2)}, u32[]{:S(2)}) %all-to-all-start.4) | async-done | bytes 442400 | tf_op jit(solution)/shard_map/all_to_all | solution.py:117
  184.2 2.1 copy.180
  186.3 2.0 all_to_all.159
  188.4 3.0 convolution_add_fusion.6
  191.4 2.7 convolution_subtract_fusion.4
  195.4 16.7 %collective-permute-done = f32[96,6,192]{2,0,1:T(8,128)} collective-permute-done((f32[96,6,192]{2,0,1:T(8,128)}, f32[96,6,192]{2,0,1:T(8,128)}, u32[]{:S(2)}, u32[]{:S(2)}) %collective-permute-start) | collective-permute-done | bytes 442400 | tf_op jit(solution)/shard_map/ppermute | solution.py:19
  216.6 20.1 %all-to-all-start.7 = ((f32[96,6,192]{0,1,2:T(8,128)}), f32[96,6,192]{0,1,2:T(8,128)}, u32[]{:S(2)}, u32[]{:S(2)}) async-start(f32[96,6,192]{0,1,2:T(8,128)} %copy.193), calls=%async_computation.7 | async-start | bytes 1572864 | tf_op jit(solution)/shard_map/all_to_all | solution.py:98
  237.9 1.7 convolution_bitcast_fusion.7
  239.6 1.4 convolution_bitcast_fusion.15
  241.1 1.7 fusion.46
  242.8 2.2 fusion.127
  245.0 2.3 copy.189
  247.2 9.8 %all-to-all-done.7 = f32[96,6,192]{0,1,2:T(8,128)} async-done(((f32[96,6,192]{0,1,2:T(8,128)}), f32[96,6,192]{0,1,2:T(8,128)}, u32[]{:S(2)}, u32[]{:S(2)}) %all-to-all-start.7) | async-done | bytes 442400 | tf_op jit(solution)/shard_map/all_to_all | solution.py:98
  257.0 5.7 %all-to-all-start.6 = ((f32[96,6,192]{0,1,2:T(8,128)}), f32[96,6,192]{0,1,2:T(8,128)}, u32[]{:S(2)}, u32[]{:S(2)}) async-start(f32[96,6,192]{0,1,2:T(8,128)} %copy.189), calls=%async_computation.6 | async-start | bytes 1572864 | tf_op jit(solution)/shard_map/all_to_all | solution.py:95
  263.6 1.7 fusion.44
  268.2 2.1 copy.195
  271.5 1.7 fusion.224
  273.2 8.2 %all-to-all-done.6 = f32[96,6,192]{0,1,2:T(8,128)} async-done(((f32[96,6,192]{0,1,2:T(8,128)}), f32[96,6,192]{0,1,2:T(8,128)}, u32[]{:S(2)}, u32[]{:S(2)}) %all-to-all-start.6) | async-done | bytes 442400 | tf_op jit(solution)/shard_map/all_to_all | solution.py:95
  281.4 2.1 copy.191
  286.7 2.6 fusion.488
  289.3 1.5 fusion.489
  298.1 2.0 fusion.222
  301.5 2.0 fusion
  303.6 2.3 copy.207
  305.8 5.4 %all-to-all-start.9 = ((f32[96,96,12]{0,2,1:T(8,128)}), f32[96,96,12]{0,2,1:T(8,128)}, u32[]{:S(2)}, u32[]{:S(2)}) async-start(f32[96,96,12]{0,2,1:T(8,128)} %copy.207), calls=%async_computation.9 | async-start | bytes 1572864 | tf_op jit(solution)/shard_map/all_to_all | solution.py:118
  311.2 3.2 fusion.3
  314.5 2.3 copy.201
  316.7 2.2 convolution_bitcast_fusion.1
  320.0 1.4 convolution_bitcast_fusion.11
  321.5 1.7 fusion.48
  323.2 1.7 fusion.50
  324.9 5.3 %all-to-all-done.9 = f32[96,96,12]{0,2,1:T(8,128)} async-done(((f32[96,96,12]{0,2,1:T(8,128)}), f32[96,96,12]{0,2,1:T(8,128)}, u32[]{:S(2)}, u32[]{:S(2)}) %all-to-all-start.9) | async-done | bytes 442400 | tf_op jit(solution)/shard_map/all_to_all | solution.py:118
  330.2 5.4 %all-to-all-start.8 = ((f32[96,96,12]{0,2,1:T(8,128)}), f32[96,96,12]{0,2,1:T(8,128)}, u32[]{:S(2)}, u32[]{:S(2)}) async-start(f32[96,96,12]{0,2,1:T(8,128)} %copy.201), calls=%async_computation.8 | async-start | bytes 1572864 | tf_op jit(solution)/shard_map/all_to_all | solution.py:117
  339.8 44.3 %all-reduce = (f32[2,96]{1,0:T(2,128)}, f32[2,96]{1,0:T(2,128)}) all-reduce(f32[2,96]{1,0:T(2,128)S(1)} %get-tuple-element.50, f32[2,96]{1,0:T(2,128)S(1)} %get-tuple-element.51), channel_id=1, replica_groups=mesh['segment'=2,'space'=16,'chan'=8] {'space'}, use_global_device_ids=true, to_apply=%region_6.7 | all-reduce | flops 384 | bytes 3072 | tf_op jit(solution)/shard_map/psum | solution.py:165
  385.4 1.9 fusion.120
  389.6 1.9 fusion.2
  392.7 99.4 %all-reduce.4.cloned.1.call-done = (f32[2,1,96,96]{3,2,1,0:T(8,128)}, f32[2,1,96,96]{3,2,1,0:T(8,128)}) async-done(((f32[2,1,96,96]{3,2,1,0:T(8,128)}, f32[2,1,96,96]{3,2,1,0:T(8,128)}), (f32[2,1,96,96]{3,2,1,0:T(8,128)}, f32[2,1,96,96]{3,2,1,0:T(8,128)})) %all-reduce.4.cloned.1.call-update) | async-done | bytes 147472 | tf_op jit(solution)/shard_map/psum | solution.py:165
  492.1 1.6 copy.329
  (190 shorter events, 74.4 us)
Async XLA Ops:
  11.2 28.5 %all-to-all-start = ((f32[96,6,192]{0,1,2:T(8,128)}), f32[96,6,192]{0,1,2:T(8,128)S(1)}, u32[]{:S(2)}, u32[]{:S(2)}) async-start(f32[96,6,192]{0,1,2:T(8,128)} %copy.150), calls=%async_computation | async-start | bytes 1572864 | tf_op jit(solution)/shard_map/all_to_all | solution.py:155
  21.1 1.3 copy-start.40
  39.7 24.4 %all-to-all-start.1 = ((f32[96,6,192]{0,1,2:T(8,128)}), f32[96,6,192]{0,1,2:T(8,128)}, u32[]{:S(2)}, u32[]{:S(2)}) async-start(f32[96,6,192]{0,1,2:T(8,128)} %copy.156), calls=%async_computation.1 | async-start | bytes 1572864 | tf_op jit(solution)/shard_map/all_to_all | solution.py:158
  49.0 1.3 copy-start.55
  64.0 24.5 %all-to-all-start.3 = ((f32[96,6,192]{0,1,2:T(8,128)}), f32[96,6,192]{0,1,2:T(8,128)}, u32[]{:S(2)}, u32[]{:S(2)}) async-start(f32[96,6,192]{0,1,2:T(8,128)} %copy.170), calls=%async_computation.3 | async-start | bytes 1572864 | tf_op jit(solution)/shard_map/all_to_all | solution.py:98
  76.4 1.2 copy-start.21
  88.5 24.4 %all-to-all-start.2 = ((f32[96,6,192]{0,1,2:T(8,128)}), f32[96,6,192]{0,1,2:T(8,128)}, u32[]{:S(2)}, u32[]{:S(2)}) async-start(f32[96,6,192]{0,1,2:T(8,128)} %copy.166), calls=%async_computation.2 | async-start | bytes 1572864 | tf_op jit(solution)/shard_map/all_to_all | solution.py:95
  98.4 1.7 copy-start.24
  117.1 2.0 copy-start.25
  117.1 2.0 copy-start.39
  119.8 1.0 copy-start.34
  120.8 4.2 copy-start
  120.8 1.3 copy-start.38
  122.1 1.1 copy-start.19
  122.1 1.2 copy-start.28
  123.3 1.0 copy-start.36
  124.4 2.6 copy-start.5
  124.4 1.1 copy-start.30
  125.4 0.9 copy-start.22
  126.1 3.1 copy-start.2
  126.3 0.9 copy-start.32
  129.2 2.0 copy-start.15
  129.9 1.4 copy-start.18
  135.5 24.3 %all-to-all-start.5 = ((f32[96,96,12]{0,2,1:T(8,128)}), f32[96,96,12]{0,2,1:T(8,128)}, u32[]{:S(2)}, u32[]{:S(2)}) async-start(f32[96,96,12]{0,2,1:T(8,128)} %copy.184), calls=%async_computation.5 | async-start | bytes 1572864 | tf_op jit(solution)/shard_map/all_to_all | solution.py:118
  140.9 2.3 copy-start.16
  159.9 24.3 %all-to-all-start.4 = ((f32[96,96,12]{0,2,1:T(8,128)}), f32[96,96,12]{0,2,1:T(8,128)}, u32[]{:S(2)}, u32[]{:S(2)}) async-start(f32[96,96,12]{0,2,1:T(8,128)} %copy.178), calls=%async_computation.4 | async-start | bytes 1572864 | tf_op jit(solution)/shard_map/all_to_all | solution.py:117
  188.4 3.0 copy-start.27
  194.1 18.0 %collective-permute-start = (f32[96,6,192]{2,0,1:T(8,128)}, f32[96,6,192]{2,0,1:T(8,128)}, u32[]{:S(2)}, u32[]{:S(2)}) collective-permute-start(f32[96,6,192]{2,0,1:T(8,128)} %convolution_subtract_fusion.4), channel_id=1, source_target_pairs={{128,0},{129,1},{130,2},{131,3},{132,4},{133,5},{134,6},{135,7},{1... | collective-permute-start | bytes 1327112 | tf_op jit(solution)/shard_map/ppermute | solution.py:19
  213.2 0.8 copy-start.12
  216.6 20.1 %copy-start.1 = (f32[96,96,12]{0,1,2:T(8,128)S(1)}, f32[96,96,12]{0,1,2:T(8,128)}, u32[]{:S(2)}) copy-start(f32[96,96,12]{0,1,2:T(8,128)} %copy-done) | copy-start | bytes 1327108
  216.6 40.4 %all-to-all-start.7 = ((f32[96,6,192]{0,1,2:T(8,128)}), f32[96,6,192]{0,1,2:T(8,128)}, u32[]{:S(2)}, u32[]{:S(2)}) async-start(f32[96,6,192]{0,1,2:T(8,128)} %copy.193), calls=%async_computation.7 | async-start | bytes 1572864 | tf_op jit(solution)/shard_map/all_to_all | solution.py:98
  236.7 1.1 copy-start.6
  237.9 1.7 copy-start.3
  241.1 1.7 copy-start.13
  257.0 24.4 %all-to-all-start.6 = ((f32[96,6,192]{0,1,2:T(8,128)}), f32[96,6,192]{0,1,2:T(8,128)}, u32[]{:S(2)}, u32[]{:S(2)}) async-start(f32[96,6,192]{0,1,2:T(8,128)} %copy.189), calls=%async_computation.6 | async-start | bytes 1572864 | tf_op jit(solution)/shard_map/all_to_all | solution.py:95
  262.8 0.8 copy-start.43
  263.6 1.7 copy-start.42
  265.3 1.4 copy-start.4
  284.8 0.8 copy-start.20
  285.6 1.1 copy-start.29
  285.6 1.1 copy-start.37
  286.7 2.6 copy-start.35
  289.3 1.5 copy-start.26
  290.8 2.8 copy-start.10
  291.5 0.9 copy-start.33
  292.4 1.2 copy-start.31
  293.6 1.2 copy-start.23
  294.8 1.3 copy-start.7
  300.7 0.8 copy-start.17
  305.8 24.3 %all-to-all-start.9 = ((f32[96,96,12]{0,2,1:T(8,128)}), f32[96,96,12]{0,2,1:T(8,128)}, u32[]{:S(2)}, u32[]{:S(2)}) async-start(f32[96,96,12]{0,2,1:T(8,128)} %copy.207), calls=%async_computation.9 | async-start | bytes 1572864 | tf_op jit(solution)/shard_map/all_to_all | solution.py:118
  318.9 1.1 copy-start.8
  320.0 1.5 copy-start.11
  330.2 57.1 %all-to-all-start.8 = ((f32[96,96,12]{0,2,1:T(8,128)}), f32[96,96,12]{0,2,1:T(8,128)}, u32[]{:S(2)}, u32[]{:S(2)}) async-start(f32[96,96,12]{0,2,1:T(8,128)} %copy.201), calls=%async_computation.8 | async-start | bytes 1572864 | tf_op jit(solution)/shard_map/all_to_all | solution.py:117
  335.5 1.1 copy-start.9
  335.6 156.6 %all-reduce.4.cloned.1.call-start = ((), (), s32[]{:S(2)}) async-start(), calls=%async_computation.10 | async-start | bytes 393216 | tf_op jit(solution)/shard_map/psum | solution.py:165
  336.6 0.8 copy-start.41
  337.5 0.9 copy-start.44
  337.5 0.9 copy-start.45
  337.5 0.9 copy-start.46
  337.5 0.9 copy-start.47
  337.5 0.9 copy-start.48
  337.5 0.9 copy-start.49
  388.5 1.1 copy-start.14
  492.1 1.6 copy-start.50
  (5 other events, 3.4 us)
Sparse Core Ops, SparseCore 0:
  339.7 152.4 all-reduce.3
where the time goes:
time: 510 us; the launch traced here: 501 us
  waiting for transfers between devices  210 us (41%)
  matrix products  93.9 us (18%)
  starting transfers between devices  73.8 us (14%)
  local copies, waits for them, and re-layouts  60.6 us (12%)
  blocking collectives  44.3 us (9%)
  between operations  15.3 us (3%)
    psum x1, waiting for transfers between devices, shards(): gradients = lax.psum(gradients, 'space')  99.4 us
    psum x1, blocking collectives, shards(): gradients = lax.psum(gradients, 'space')  44.3 us
    dot_general x20, matrix products, along_height(): return jnp.einsum('uh,chv->cuv', dft_table, field, precision=exact)  33.2 us
    all_to_all x2, starting transfers between devices, section_adjoint(): lax.all_to_all(-along_width(upstream, sin_w), 'space', split_axis=2, conc...  25.6 us
    dot_general x10, matrix products, along_width(): return jnp.einsum('...chw,wv->...chv', field, dft_table, precision=exact)  18.7 us
    all_to_all x2, waiting for transfers between devices, section_adjoint(): lax.all_to_all(along_width(upstream, cos_w), 'space', split_axis=2, conca...  18.2 us
    all_to_all x2, waiting for transfers between devices, section_adjoint(): lax.all_to_all(grad_spec_i, 'space', split_axis=1, concat_axis=2, tiled=T...  17.7 us
    all_to_all x1, waiting for transfers between devices, shards(): lax.all_to_all(along_width(block_input, cos_w), 'space', split_axis=2, co...  16.8 us
  transfers between devices with their start and end apart: 12, of which 11 were waited for; matrix products, arithmetic and copies ran while one was open for 16% of the time, Pallas kernels for 0%

commit v1 on v0

v1 whole, which is shorter than its diff:
```python
import math

import jax
import jax.numpy as jnp
import ml_dtypes
import numpy as np
from jax import lax
from jax.experimental import pallas as pl
from jax.experimental.pallas import tpu as pltpu
from jax.sharding import PartitionSpec as P

H = 96
W = 192
CH = 96
LANES = 128
N_SPACE = 16
N_SEG = 2
N_DEST = N_SPACE * N_SEG
ROWS = H // N_SPACE
COLS = W // 2 // N_DEST
BLOCK = 48
SHRINK = 0.3
BF16 = jnp.bfloat16
F32 = jnp.float32
VMEM_LIMIT = 40 * 1024 * 1024


def split_table(table, count):
    parts = []
    for _ in range(count):
        parts.append(table.astype(np.float32).astype(ml_dtypes.bfloat16))
        table = table - parts[-1].astype(np.float64)
    return np.stack(parts)


def dft(length):
    index = np.arange(length)
    phase = 2.0 * math.pi * (np.outer(index, index) % length) / length
    return np.cos(phase) / math.sqrt(length), np.sin(phase) / math.sqrt(length)


def width_table():
    cos_w, sin_w = dft(W)
    half = W // 2
    real, imag = cos_w[:half].copy(), -sin_w[:half].copy()
    imag[0] = cos_w[half]
    both = np.stack([real, imag])
    return both.reshape(2, N_DEST, COLS, W).transpose(0, 2, 1, 3)


def height_tables():
    cos_h, sin_h = dft(H)
    order = np.array([ROWS * p + r for r in range(ROWS) for p in range(N_SPACE)])
    cos_h, sin_h = cos_h[:, order], sin_h[:, order]
    zero = np.zeros_like(cos_h)
    plain = np.block([[cos_h, sin_h], [-sin_h, cos_h]])
    mirror = np.block([[cos_h, sin_h], [sin_h, -cos_h]])
    special = np.block([[cos_h, zero], [-sin_h, zero], [zero, cos_h], [zero, -sin_h]])
    return plain, np.stack([np.concatenate([plain, mirror]), special])


def row_pair_tables():
    table = width_table()
    flat = table.reshape(2 * COLS * N_DEST, W)
    zero = np.zeros_like(flat)
    both = np.block([[flat, zero], [zero, flat]])
    parts = []
    for part in range(2):
        one = table[part].reshape(COLS * N_DEST, W)
        none = np.zeros_like(one)
        parts.append(np.block([[one, none], [none, one]]))
    return both, np.stack(parts)


def cut(value, count):
    parts = []
    for n in range(count):
        parts.append(value.astype(BF16))
        if n < count - 1:
            value = value - parts[-1].astype(F32)
    return parts


def halves(value):
    return cut(value, 2)


def thirds(value):
    return cut(value, 3)


def product(a, b, contract, parts=2):
    dims = (contract, ((), ()))
    total = None
    for order in reversed(range(parts)):
        for n in range(order + 1):
            one = lax.dot_general(a[n], b[order - n], dims, preferred_element_type=F32)
            total = one if total is None else total + one
    return total


NN = ((1,), (0,))
NT = ((1,), (1,))
TN = ((0,), (0,))


def lane_index(rows):
    return lax.broadcasted_iota(jnp.int32, (rows, LANES), 1)


def slot(part, c, r):
    return (part * COLS + c) * ROWS + r


N_FIELD = 2 * COLS * ROWS


def pack_rows(put, count, values):
    lane = lane_index(count)
    for q in range(BLOCK):
        third, extra = divmod(q, 16)
        value = values.get(q)
        packed = values.get(BLOCK + extra)
        if value is None:
            value = jnp.zeros((count, LANES), F32)
        if packed is not None:
            value = jnp.where(lane < CH, value, pltpu.roll(packed, CH - 32 * third, 1))
        put(q, value)


def unpack_row(get, count, q):
    if q < BLOCK:
        return get(q)
    lane = lane_index(count)
    extra = q - BLOCK
    value = jnp.zeros((count, LANES), F32)
    for third in range(3):
        moved = pltpu.roll(get(extra + 16 * third), (32 * third - CH) % LANES, 1)
        value = jnp.where((lane >= 32 * third) & (lane < 32 * third + 32), moved, value)
    return value


def ahead_kernel(seg_ref, x_ref, g_ref, both_ref, part_ref, out_ref):
    segment = seg_ref[0]
    pad = jnp.zeros((LANES - CH, 2 * W), F32)
    values = {}
    both = [both_ref[n] for n in range(3)]
    part = [part_ref[n, segment] for n in range(2)]
    for j in range(ROWS // 2):
        lanes = pl.ds(2 * W * j, 2 * W)
        field = product(both, thirds(jnp.concatenate([x_ref[:, lanes], pad], axis=0)), NT, 3)
        adjoint = product(part, halves(jnp.concatenate([g_ref[:, lanes], pad], axis=0)), NT)
        for rr in range(2):
            for c in range(COLS):
                for of in range(2):
                    base = ((rr * 2 + of) * COLS + c) * N_DEST
                    values[slot(of, c, 2 * j + rr)] = field[base : base + N_DEST]
                base = (rr * COLS + c) * N_DEST
                values[N_FIELD + c * ROWS + 2 * j + rr] = adjoint[base : base + N_DEST]

    def put(q, value):
        out_ref[pl.ds(q, N_DEST, stride=BLOCK), :] = value

    pack_rows(put, N_DEST, values)


def middle_kernel(flag_ref, got_ref, w_ref, b_ref, plain_ref, plain_t_ref, first_ref, first_t_ref, out_ref, grads_ref):
    flag = flag_ref[0]
    plain = [plain_ref[n] for n in range(3)]
    plain_t = [plain_t_ref[n] for n in range(2)]
    first = [first_ref[n, flag] for n in range(3)]
    first_t = [first_t_ref[n, flag] for n in range(2)]
    scale = jnp.where(flag == 1, 1.0, 0.5).astype(F32)

    def row(source, q):
        def get(at):
            return got_ref[pl.ds(source * N_SPACE * BLOCK + at, N_SPACE, stride=BLOCK), :]

        return unpack_row(get, N_SPACE, q)

    def field_column(s, c):
        return jnp.concatenate([row(s, slot(of, c, r)) for of in range(2) for r in range(ROWS)], axis=0)

    def adjoint_column(c):
        return jnp.concatenate([row(of, N_FIELD + c * ROWS + r) for of in range(2) for r in range(ROWS)], axis=0)

    def ordinary(column):
        r, i = column[:H], column[H:]
        return [jnp.concatenate([r, i], axis=1), jnp.concatenate([r, -i], axis=1)]

    def special(column):
        return [
            jnp.concatenate([column[:H], column[H : 2 * H]], axis=1),
            jnp.concatenate([column[2 * H : 3 * H], column[3 * H :]], axis=1),
        ]

    adjoint_first = adjoint_column(0)
    head = product(first, thirds(jnp.concatenate([field_column(s, 0) for s in range(2)], axis=1)), NN, 3)
    rest = product(
        plain, thirds(jnp.concatenate([field_column(s, c) for s in range(2) for c in (1, 2)], axis=1)), NN, 3
    )
    adjoint_head = product(first, halves(adjoint_first), NN)
    adjoint_rest = product(plain, halves(jnp.concatenate([adjoint_column(c) for c in (1, 2)], axis=1)), NN)

    def block(value, n):
        return value[:, LANES * n : LANES * (n + 1)]

    weights = [thirds(w_ref[n]) for n in range(4)]

    forward = []
    for s in range(2):
        x = jnp.concatenate(
            special(block(head, s)) + ordinary(block(rest, 2 * s)) + ordinary(block(rest, 2 * s + 1)), axis=0
        )
        x = thirds(x)
        hid = product(x, weights[2 * s], NN, 3) + b_ref[2 * s : 2 * s + 1, :]
        act = thirds(jnp.maximum(hid, 0.0))
        out = product(act, weights[2 * s + 1], NN, 3) + b_ref[2 * s + 1 : 2 * s + 2, :]
        forward.append((x, hid, act, out))

    def backward(s, upstream):
        x, hid, act, out = forward[s]
        grad_out = jnp.where(jnp.abs(out) > SHRINK, upstream, 0.0)
        grad_out_halves = halves(grad_out)
        grad_hid = jnp.where(hid > 0.0, product(grad_out_halves, weights[2 * s + 1], NT), 0.0)
        grad_hid_halves = halves(grad_hid)
        grad_x = product(grad_hid_halves, weights[2 * s], NT)
        pairs = []
        for n, (left, right) in enumerate(((x, grad_hid_halves), (act, grad_out_halves))):
            full = product(left, right, TN)
            grads_ref[pl.ds((2 * n) * CH, CH), :] = full[:CH, :LANES] + full[LANES : LANES + CH, LANES:]
            grads_ref[pl.ds((2 * n + 1) * CH, CH), :] = full[:CH, LANES:] - full[LANES : LANES + CH, :LANES]
        offsets = []
        for value in (grad_hid, grad_out):
            total = jnp.sum(value, axis=0, keepdims=True)
            offsets += [total[:, :LANES], total[:, LANES:]]
        sums = []
        for c in (1, 2):
            one, two = grad_x[2 * c * H : (2 * c + 1) * H], grad_x[(2 * c + 1) * H : (2 * c + 2) * H]
            sums.append(
                jnp.concatenate([one[:, :LANES] + two[:, :LANES], one[:, LANES:] - two[:, LANES:]], axis=0)
            )
        lead = jnp.concatenate(
            [grad_x[:H, :LANES], grad_x[:H, LANES:], grad_x[H : 2 * H, :LANES], grad_x[H : 2 * H, LANES:]], axis=0
        )
        head_back = product(first_t, halves(lead), NN)
        rest_back = product(plain_t, halves(jnp.concatenate(sums, axis=1)), NN)
        return [head_back, block(rest_back, 0), block(rest_back, 1)], sums, offsets

    def emit(s, columns, offsets):
        values = {}
        for c in range(COLS):
            for of in range(2):
                for r in range(ROWS):
                    base = (of * ROWS + r) * N_SPACE
                    values[slot(of, c, r)] = columns[c][base : base + N_SPACE]
        share = 4 * CH // N_SPACE
        for j in range(share):
            values[N_FIELD + j] = grads_ref[pl.ds(j, N_SPACE, stride=share), :]
        for j in range(4):
            values[N_FIELD + share + j] = jnp.broadcast_to(offsets[j], (N_SPACE, LANES))

        def put(q, value):
            out_ref[pl.ds(s * N_SPACE * BLOCK + q, N_SPACE, stride=BLOCK), :] = value

        pack_rows(put, N_SPACE, values)

    upstream = jnp.concatenate(
        special(adjoint_head) + ordinary(block(adjoint_rest, 0)) + ordinary(block(adjoint_rest, 1)), axis=0
    )
    columns_one, sums, offsets = backward(1, upstream)
    emit(1, columns_one, offsets)

    head_next = product(first, halves(adjoint_first + scale * columns_one[0]), NN)
    upstream = jnp.concatenate(
        special(head_next)
        + ordinary(block(adjoint_rest, 0) + 0.5 * sums[0])
        + ordinary(block(adjoint_rest, 1) + 0.5 * sums[1]),
        axis=0,
    )
    columns_zero, sums, offsets = backward(0, upstream)
    emit(0, [one + zero for one, zero in zip(columns_one, columns_zero)], offsets)


def total_kernel(got_ref, share_ref, offset_ref):
    total = got_ref[pl.ds(0, BLOCK), :]
    for d in range(1, N_DEST):
        total = total + got_ref[pl.ds(d * BLOCK, BLOCK), :]
    share = 4 * CH // N_SPACE
    lane = lane_index(16)
    late = jnp.zeros((16, LANES), F32)
    for third in range(3):
        moved = pltpu.roll(total[16 * third : 16 * third + 16], (32 * third - CH) % LANES, 1)
        late = jnp.where((lane >= 32 * third) & (lane < 32 * third + 32), moved, late)
    early = BLOCK - N_FIELD
    for p in range(N_SPACE):
        share_ref[pl.ds(p * share, early), :] = total[N_FIELD:BLOCK]
        share_ref[pl.ds(p * share + early, share - early), :] = late[: share - early]
    offset_ref[...] = late[share - early : 16]


def after_kernel(got_ref, g_ref, pair_ref, out_ref):
    for j in range(ROWS // 2):
        rows = []
        for rr in range(2):
            for of in range(2):
                for c in range(COLS):
                    rows.append(got_ref[pl.ds(slot(of, c, 2 * j + rr), N_DEST, stride=BLOCK), :])
        spectrum = halves(jnp.concatenate(rows, axis=0))
        back = product(spectrum, [pair_ref[n] for n in range(2)], TN)
        lanes = pl.ds(2 * W * j, 2 * W)
        out_ref[:, lanes] = g_ref[:, lanes] + back[:CH]


def vmem(count):
    return [pl.BlockSpec(memory_space=pltpu.VMEM)] * count


def smem():
    return [pl.BlockSpec(memory_space=pltpu.SMEM)]


PARAMS = pltpu.CompilerParams(vmem_limit_bytes=VMEM_LIMIT)


def shards(acts, cotangent, w_in, w_out, b_in, b_out):
    segment = lax.axis_index("segment")
    space = lax.axis_index("space")
    everyone = ("segment", "space")
    block_input, given = acts[0, 0], cotangent[0]

    pair, part = row_pair_tables()
    plain, heads = height_tables()
    pair_parts = split_table(pair, 3)
    part_parts = split_table(part, 2)
    plain_parts = split_table(plain, 3)
    plain_t_parts = split_table(plain.T, 2)
    head_parts = split_table(heads, 3)
    head_t_parts = split_table(heads.transpose(0, 2, 1), 2)

    sent = pl.pallas_call(
        ahead_kernel,
        out_shape=jax.ShapeDtypeStruct((N_DEST * BLOCK, LANES), F32),
        in_specs=smem() + vmem(4),
        out_specs=pl.BlockSpec(memory_space=pltpu.VMEM),
        compiler_params=PARAMS,
        name="ahead",
    )(segment.astype(jnp.int32).reshape(1), block_input, given, pair_parts, part_parts)
    got = lax.all_to_all(sent.reshape(N_DEST, BLOCK, LANES), everyone, 0, 0, tiled=True)

    own_w = jnp.concatenate([w_in[0, :, 0], w_out[0, :, 0]])
    own_b = jnp.concatenate([b_in[0], b_out[0]])
    swap = [(0, 1), (1, 0)]
    other_w = lax.ppermute(own_w, "segment", swap)
    other_b = lax.ppermute(own_b, "segment", swap)
    is_zero = segment == 0
    all_w = jnp.concatenate([jnp.where(is_zero, own_w, other_w), jnp.where(is_zero, other_w, own_w)])
    all_b = jnp.concatenate([jnp.where(is_zero, own_b, other_b), jnp.where(is_zero, other_b, own_b)])
    all_w = jnp.pad(all_w, ((0, 0), (0, LANES - CH), (0, LANES - CH))).reshape(4, 2, LANES, LANES)
    w0, w1 = all_w[:, 0], all_w[:, 1]
    full_w = jnp.concatenate(
        [jnp.concatenate([w0, w1], axis=2), jnp.concatenate([-w1, w0], axis=2)], axis=1
    )
    full_b = jnp.pad(all_b, ((0, 0), (0, LANES - CH))).reshape(4, 2 * LANES)
    full_b = jnp.pad(full_b, ((0, 4), (0, 0)))

    flag = ((segment == 0) & (space == 0)).astype(jnp.int32).reshape(1)
    sent = pl.pallas_call(
        middle_kernel,
        out_shape=jax.ShapeDtypeStruct((N_DEST * BLOCK, LANES), F32),
        in_specs=smem() + vmem(7),
        out_specs=pl.BlockSpec(memory_space=pltpu.VMEM),
        scratch_shapes=[pltpu.VMEM((4 * CH, LANES), F32)],
        compiler_params=PARAMS,
        name="middle",
    )(flag, got.reshape(N_DEST * BLOCK, LANES), full_w, full_b, plain_parts, plain_t_parts, head_parts, head_t_parts)
    got = lax.all_to_all(sent.reshape(N_DEST, BLOCK, LANES), everyone, 0, 0, tiled=True)
    got = got.reshape(N_DEST * BLOCK, LANES)

    share = 4 * CH // N_SPACE
    mine, offsets = pl.pallas_call(
        total_kernel,
        out_shape=(
            jax.ShapeDtypeStruct((N_SPACE * share, LANES), F32),
            jax.ShapeDtypeStruct((4, LANES), F32),
        ),
        in_specs=vmem(1),
        out_specs=tuple(vmem(2)),
        compiler_params=PARAMS,
        name="total",
    )(got)
    whole = lax.all_to_all(mine.reshape(N_SPACE, share, LANES), "space", 0, 0, tiled=True)

    adjoint = pl.pallas_call(
        after_kernel,
        out_shape=jax.ShapeDtypeStruct((CH, ROWS * W), F32),
        in_specs=vmem(3),
        out_specs=pl.BlockSpec(memory_space=pltpu.VMEM),
        compiler_params=PARAMS,
        name="after",
    )(got, given, pair_parts[:2])

    whole = whole.reshape(4, CH, LANES)[:, :, :CH]
    offsets = offsets[:, :CH]
    return (
        adjoint[None, None],
        whole[:2].reshape(w_in.shape),
        whole[2:].reshape(w_out.shape),
        offsets[:2].reshape(b_in.shape),
        offsets[2:].reshape(b_out.shape),
    )


def solution(mesh):
    placed = (
        P("segment", None, "chan", "space"),
        P(None, "chan", "space"),
        P("segment", None, "chan", None, None),
        P("segment", None, "chan", None, None),
        P("segment", None, "chan"),
        P("segment", None, "chan"),
    )
    return jax.shard_map(
        shards,
        mesh=mesh,
        in_specs=placed,
        out_specs=(
            P("segment", None, "chan", "space"),
            P("segment", None, "chan", None, None),
            P("segment", None, "chan", None, None),
            P("segment", None, "chan"),
            P("segment", None, "chan"),
        ),
        check_vma=False,
    )
```

time: 510 us -> 104 us (0.20); the launches traced: 501 us -> 103 us
  waiting for transfers between devices: 210 us -> 29.1 us
  matrix products: 93.9 us -> 0 us
  local copies, waits for them, and re-layouts: 60.6 us -> 7.91 us
  starting transfers between devices: 73.8 us -> 21.7 us
  between operations: 15.3 us -> 0.83 us
  blocking collectives: 44.3 us -> 30.5 us
  Pallas kernels: 0 us -> 13.2 us
    psum x1 -> x0, waiting for transfers between devices: 99.4 us -> none  [shards(): gradients = lax.psum(gradients, 'space')]
    dot_general x70 -> x0, matrix products: 93.9 us -> none  [the longest x20 33.2 us: along_height(): return jnp.einsum('uh,chv->cuv', dft_table, field, precision=exact)]
    all_to_all x10 -> x2, waiting for transfers between devices: 93.9 us -> 7.29 us  [the longest x1 7.28 us: shards(): lax.all_to_all(mine.reshape(N_SPACE, share, LANES), 'space', 0, 0, tiled=...]
    all_to_all x10 -> x2, starting transfers between devices: 72.3 us -> 15.6 us  [the longest x1 11.5 us: shards(): lax.all_to_all(sent.reshape(N_DEST, BLOCK, LANES), everyone, 0, 0, tiled=...]
    psum x1 -> x0, blocking collectives: 44.3 us -> none  [shards(): gradients = lax.psum(gradients, 'space')]
    all_to_all x0 -> x1, blocking collectives: none -> 30.5 us  [shards(): lax.all_to_all(sent.reshape(N_DEST, BLOCK, LANES), everyone, 0, 0, tiled=...]
    all_to_all x20 -> x0, local copies, waits for them, and re-layouts: 30.3 us -> none  [the longest x4 7.51 us: section_adjoint(): lax.all_to_all(along_width(upstream, cos_w), 'space', split_axis=2, conca...]
    pallas_call x0 -> x4, Pallas kernels: none -> 13.2 us  [the longest x1 7.69 us: shards(): pl.pallas_call(middle_kernel, out_shape=jax.ShapeDtypeStruct((N_DEST * BL...]
  transfers between devices with their start and end apart: 12 -> 4, of which waited for: 11 -> 3; matrix products, arithmetic and copies ran while one was open for 16% -> 1% of each run, Pallas kernels for 0% -> 2%
where the time goes in v1:
time: 104 us; the launch traced here: 103 us
  blocking collectives  30.5 us (29%)
  waiting for transfers between devices  29.1 us (28%)
  starting transfers between devices  21.7 us (21%)
  Pallas kernels  13.2 us (13%)
  local copies, waits for them, and re-layouts  7.91 us (8%)
    all_to_all x1, blocking collectives, shards(): lax.all_to_all(sent.reshape(N_DEST, BLOCK, LANES), everyone, 0, 0, tiled=...  30.5 us
    ppermute x1, waiting for transfers between devices, shards(): other_b = lax.ppermute(own_b, 'segment', swap)  16.9 us
    all_to_all x1, starting transfers between devices, shards(): lax.all_to_all(sent.reshape(N_DEST, BLOCK, LANES), everyone, 0, 0, tiled=...  11.5 us
    pallas_call x1, Pallas kernels, shards(): pl.pallas_call(middle_kernel, out_shape=jax.ShapeDtypeStruct((N_DEST * BL...  7.69 us
    all_to_all x1, waiting for transfers between devices, shards(): lax.all_to_all(mine.reshape(N_SPACE, share, LANES), 'space', 0, 0, tiled=...  7.28 us
    unnamed x28, local copies, waits for them, and re-layouts  6.6 us
    ppermute x1, starting transfers between devices, shards(): other_b = lax.ppermute(own_b, 'segment', swap)  5.79 us
    ppermute x1, waiting for transfers between devices, shards(): other_w = lax.ppermute(own_w, 'segment', swap)  4.85 us
  transfers between devices with their start and end apart: 4, of which 3 were waited for; matrix products, arithmetic and copies ran while one was open for 1% of the time, Pallas kernels for 2%

profile of v1, /device:TPU:8, one launch (start us, length us, event | category | flops | bytes accessed | tf_op | source)
XLA Modules:
  0.0 103.5 jit_solution(13143385560036813594)
XLA Ops:
  0.6 0.0 copy-start
  0.6 1.0 copy-done
  1.7 0.0 copy-start.3
  1.7 1.2 %copy-done.3 = bf16[3,384,384]{2,1,0:T(8,128)(2,1)S(1)} copy-done((bf16[3,384,384]{2,1,0:T(8,128)(2,1)S(1)}, bf16[3,384,384]{2,1,0:T(8,128)(2,1)}, u32[]{:S(2)}) %copy-start.3) | copy-done | bytes 884760
  2.8 0.0 copy-start.6
  2.8 1.1 %copy-done.6 = bf16[2,2,192,384]{3,2,1,0:T(8,128)(2,1)S(1)} copy-done((bf16[2,2,192,384]{3,2,1,0:T(8,128)(2,1)S(1)}, bf16[2,2,192,384]{3,2,1,0:T(8,128)(2,1)}, u32[]{:S(2)}) %copy-start.6) | copy-done | bytes 589848
  3.9 0.0 copy-start.7
  3.9 1.0 copy-done.7
  4.9 3.1 %ahead.1 = f32[1536,128]{1,0:T(8,128)} custom-call(s32[1]{0:T(128)} %bitcast.1.seg_ref, f32[96,1152]{1,0:T(8,128)S(1)} %bitcast.40, f32[96,1152]{1,0:T(8,128)S(1)} %bitcast.38, bf16[3,384,384]{2,1,0:T(8,128)(2,1)S(1)} %copy-done.3, bf16[2,2,192,384]{3,2,1,0:T(8,128)(2,1)S(1)} %copy-done.6), custom_call_target="tpu_custom_call" | custom-call | tf_op jit(solution)/shard_map/ahead/pallas_call | solution.py:341
  8.0 0.0 copy-start.12
  8.0 0.0 copy-start.13
  8.0 0.0 copy-start.10
  8.0 0.0 copy-start.11
  8.0 11.5 %all-to-all-start = ((f32[32,48,128]{2,1,0:T(8,128)}), f32[32,48,128]{2,1,0:T(8,128)S(1)}, u32[]{:S(2)}, u32[]{:S(2)}) async-start(f32[32,48,128]{2,1,0:T(8,128)} %bitcast.4), calls=%async_computation | async-start | bytes 1572864 | tf_op jit(solution)/shard_map/all_to_all | solution.py:349
  19.5 0.0 copy-done.12
  19.5 0.0 copy-done.13
  19.5 5.8 %collective-permute-start.1 = (f32[4,96]{1,0:T(4,128)S(1)}, f32[4,96]{1,0:T(4,128)S(1)}, u32[]{:S(2)}, u32[]{:S(2)}) collective-permute-start(f32[4,96]{1,0:T(4,128)S(1)} %pad_maximum_fusion.1), channel_id=1, source_target_pairs={{0,128},{128,0},{1,129},{129,1},{2,130},{130,2},{3,131},{131,3},{4... | collective-permute-start | bytes 4616 | tf_op jit(solution)/shard_map/ppermute | solution.py:355
  25.3 0.0 copy-done.10
  25.3 0.0 copy-done.11
  25.3 0.3 collective-permute-start
  25.6 16.9 %collective-permute-done.1 = f32[4,96]{1,0:T(4,128)S(1)} collective-permute-done((f32[4,96]{1,0:T(4,128)S(1)}, f32[4,96]{1,0:T(4,128)S(1)}, u32[]{:S(2)}, u32[]{:S(2)}) %collective-permute-start.1) | collective-permute-done | bytes 1568 | tf_op jit(solution)/shard_map/ppermute | solution.py:355
  42.6 4.8 %collective-permute-done = f32[4,96,96]{2,1,0:T(8,128)S(1)} collective-permute-done((f32[4,96,96]{2,1,0:T(8,128)S(1)}, f32[4,96,96]{2,1,0:T(8,128)S(1)}, u32[]{:S(2)}, u32[]{:S(2)}) %collective-permute-start) | collective-permute-done | bytes 147488 | tf_op jit(solution)/shard_map/ppermute | solution.py:354
  47.6 0.0 copy-start.2
  47.6 0.0 copy-start.8
  47.6 0.0 copy-start.9
  47.6 0.1 maximum_maximum_fusion.w_ref
  47.7 0.0 all-to-all-done
  47.7 1.1 %copy-done.2 = bf16[3,2,384,192]{3,2,1,0:T(8,128)(2,1)S(1)} copy-done((bf16[3,2,384,192]{3,2,1,0:T(8,128)(2,1)S(1)}, bf16[3,2,384,192]{3,2,1,0:T(8,128)(2,1)}, u32[]{:S(2)}) %copy-start.2) | copy-done | bytes 884760
  48.9 0.0 copy-done.8
  48.9 0.1 copy-done.9
  49.0 0.0 copy-start.4
  49.0 1.1 %copy-done.4 = bf16[2,2,192,384]{3,2,1,0:T(8,128)(2,1)S(1)} copy-done((bf16[2,2,192,384]{3,2,1,0:T(8,128)(2,1)S(1)}, bf16[2,2,192,384]{3,2,1,0:T(8,128)(2,1)}, u32[]{:S(2)}) %copy-start.4) | copy-done | bytes 589848
  50.0 7.7 %middle.1 = f32[1536,128]{1,0:T(8,128)S(1)} custom-call(s32[1]{0:T(128)} %bitcast.flag_ref, f32[1536,128]{1,0:T(8,128)S(1)} %bitcast.36, f32[4,256,256]{2,1,0:T(8,128)S(1)} %maximum_maximum_fusion.w_ref, f32[8,256]{1,0:T(8,128)S(1)} %pad.14.b_ref, bf16[3,192,192]{2,1,0:T(8,128)(2,1)S(1)} %copy-done.8, bf16[2,192,192]{2,1,0:T(8,128)(2,1)S(1)} %copy-done.9, ...), custom_call_target="tpu_custom_call" | custom-call | tf_op jit(solution)/shard_map/middle/pallas_call | solution.py:368
  57.7 0.0 copy-start.1
  57.8 0.0 copy-start.5
  57.8 30.5 %all_to_all.15 = f32[32,48,128]{2,1,0:T(8,128)S(1)} all-to-all(f32[32,48,128]{2,1,0:T(8,128)S(1)} %bitcast.37), channel_id=1, replica_groups=mesh['segment'=2,'space'=16,'chan'=8] {'segment','space'}, dimensions={0} | all-to-all | bytes 1572864 | tf_op jit(solution)/shard_map/all_to_all | solution.py:377
  88.3 0.8 total.1
  89.1 4.2 %all-to-all-start.2 = ((f32[16,24,128]{2,1,0:T(8,128)}), f32[16,24,128]{2,1,0:T(8,128)S(1)}, u32[]{:S(2)}, u32[]{:S(2)}) async-start(f32[16,24,128]{2,1,0:T(8,128)} %bitcast.16), calls=%async_computation.2 | async-start | bytes 393216 | tf_op jit(solution)/shard_map/all_to_all | solution.py:392
  93.3 0.0 copy-done.1
  93.3 0.0 copy-done.5
  93.3 1.6 %after.1 = f32[96,1152]{1,0:T(8,128)} custom-call(f32[1536,128]{1,0:T(8,128)S(1)} %bitcast.35, f32[96,1152]{1,0:T(8,128)S(1)} %bitcast.39, bf16[2,384,384]{2,1,0:T(8,128)(2,1)S(1)} %copy-done.5), custom_call_target="tpu_custom_call" | custom-call | tf_op jit(solution)/shard_map/after/pallas_call | solution.py:394
  94.9 0.6 slice_bitcast_fusion.4
  95.5 7.3 %all-to-all-done.2 = f32[16,24,128]{2,1,0:T(8,128)S(1)} async-done(((f32[16,24,128]{2,1,0:T(8,128)}), f32[16,24,128]{2,1,0:T(8,128)S(1)}, u32[]{:S(2)}, u32[]{:S(2)}) %all-to-all-start.2) | async-done | bytes 196640 | tf_op jit(solution)/shard_map/all_to_all | solution.py:392
  102.8 0.7 slice_bitcast_fusion.2
  (10 shorter events, 0.2 us)
Async XLA Ops:
  0.6 1.0 copy-start
  1.7 1.2 %copy-start.3 = (bf16[3,384,384]{2,1,0:T(8,128)(2,1)S(1)}, bf16[3,384,384]{2,1,0:T(8,128)(2,1)}, u32[]{:S(2)}) copy-start(bf16[3,384,384]{2,1,0:T(8,128)(2,1)} %constant.30.clone.both_ref) | copy-start | bytes 2654212
  2.8 1.1 %copy-start.6 = (bf16[2,2,192,384]{3,2,1,0:T(8,128)(2,1)S(1)}, bf16[2,2,192,384]{3,2,1,0:T(8,128)(2,1)}, u32[]{:S(2)}) copy-start(bf16[2,2,192,384]{3,2,1,0:T(8,128)(2,1)} %constant.31.clone.part_ref) | copy-start | bytes 1769476
  3.9 1.0 copy-start.7
  8.0 11.5 %copy-start.12 = (f32[1,2,96]{2,1,0:T(2,128)S(1)}, f32[1,2,96]{2,1,0:T(2,128)}, u32[]{:S(2)}) copy-start(f32[1,2,96]{2,1,0:T(2,128)} %param.18) | copy-start | bytes 2308
  8.0 11.5 %copy-start.13 = (f32[1,2,96]{2,1,0:T(2,128)S(1)}, f32[1,2,96]{2,1,0:T(2,128)}, u32[]{:S(2)}) copy-start(f32[1,2,96]{2,1,0:T(2,128)} %param.17) | copy-start | bytes 2308
  8.0 17.3 %copy-start.10 = (f32[1,2,1,96,96]{4,3,2,1,0:T(8,128)S(1)}, f32[1,2,1,96,96]{4,3,2,1,0:T(8,128)}, u32[]{:S(2)}) copy-start(f32[1,2,1,96,96]{4,3,2,1,0:T(8,128)} %param.16) | copy-start | bytes 221188
  8.0 17.3 %copy-start.11 = (f32[1,2,1,96,96]{4,3,2,1,0:T(8,128)S(1)}, f32[1,2,1,96,96]{4,3,2,1,0:T(8,128)}, u32[]{:S(2)}) copy-start(f32[1,2,1,96,96]{4,3,2,1,0:T(8,128)} %param.15) | copy-start | bytes 221188
  8.0 39.7 %all-to-all-start = ((f32[32,48,128]{2,1,0:T(8,128)}), f32[32,48,128]{2,1,0:T(8,128)S(1)}, u32[]{:S(2)}, u32[]{:S(2)}) async-start(f32[32,48,128]{2,1,0:T(8,128)} %bitcast.4), calls=%async_computation | async-start | bytes 1572864 | tf_op jit(solution)/shard_map/all_to_all | solution.py:349
  19.5 23.1 %collective-permute-start.1 = (f32[4,96]{1,0:T(4,128)S(1)}, f32[4,96]{1,0:T(4,128)S(1)}, u32[]{:S(2)}, u32[]{:S(2)}) collective-permute-start(f32[4,96]{1,0:T(4,128)S(1)} %pad_maximum_fusion.1), channel_id=1, source_target_pairs={{0,128},{128,0},{1,129},{129,1},{2,130},{130,2},{3,131},{131,3},{4... | collective-permute-start | bytes 4616 | tf_op jit(solution)/shard_map/ppermute | solution.py:355
  25.3 22.1 %collective-permute-start = (f32[4,96,96]{2,1,0:T(8,128)S(1)}, f32[4,96,96]{2,1,0:T(8,128)S(1)}, u32[]{:S(2)}, u32[]{:S(2)}) collective-permute-start(f32[4,96,96]{2,1,0:T(8,128)S(1)} %pad_maximum_fusion), channel_id=1, source_target_pairs={{0,128},{128,0},{1,129},{129,1},{2,130},{130,2},{3,131},{131,3},{4... | collective-permute-start | bytes 442376 | tf_op jit(solution)/shard_map/ppermute | solution.py:354
  47.6 1.3 %copy-start.2 = (bf16[3,2,384,192]{3,2,1,0:T(8,128)(2,1)S(1)}, bf16[3,2,384,192]{3,2,1,0:T(8,128)(2,1)}, u32[]{:S(2)}) copy-start(bf16[3,2,384,192]{3,2,1,0:T(8,128)(2,1)} %constant.34.clone.first_ref) | copy-start | bytes 2654212
  47.6 1.3 %copy-start.8 = (bf16[3,192,192]{2,1,0:T(8,128)(2,1)S(1)}, bf16[3,192,192]{2,1,0:T(8,128)(2,1)}, u32[]{:S(2)}) copy-start(bf16[3,192,192]{2,1,0:T(8,128)(2,1)} %constant.32.clone.plain_ref) | copy-start | bytes 663556
  47.6 1.3 %copy-start.9 = (bf16[2,192,192]{2,1,0:T(8,128)(2,1)S(1)}, bf16[2,192,192]{2,1,0:T(8,128)(2,1)}, u32[]{:S(2)}) copy-start(bf16[2,192,192]{2,1,0:T(8,128)(2,1)} %constant.33.clone.plain_t_ref) | copy-start | bytes 442372
  49.0 1.1 %copy-start.4 = (bf16[2,2,192,384]{3,2,1,0:T(8,128)(2,1)S(1)}, bf16[2,2,192,384]{3,2,1,0:T(8,128)(2,1)}, u32[]{:S(2)}) copy-start(bf16[2,2,192,384]{3,2,1,0:T(8,128)(2,1)} %constant.35.clone.first_t_ref) | copy-start | bytes 1769476
  57.7 35.6 %copy-start.1 = (f32[1,96,1152]{2,1,0:T(8,128)S(1)}, f32[1,96,1152]{2,1,0:T(8,128)}, u32[]{:S(2)}) copy-start(f32[1,96,1152]{2,1,0:T(8,128)} %param.14) | copy-start | bytes 1327108
  57.8 35.6 %copy-start.5 = (bf16[2,384,384]{2,1,0:T(8,128)(2,1)S(1)}, bf16[2,384,384]{2,1,0:T(8,128)(2,1)}, u32[]{:S(2)}) copy-start(bf16[2,384,384]{2,1,0:T(8,128)(2,1)} %constant.36.clone.pair_ref) | copy-start | bytes 1769476
  89.1 13.6 %all-to-all-start.2 = ((f32[16,24,128]{2,1,0:T(8,128)}), f32[16,24,128]{2,1,0:T(8,128)S(1)}, u32[]{:S(2)}, u32[]{:S(2)}) async-start(f32[16,24,128]{2,1,0:T(8,128)} %bitcast.16), calls=%async_computation.2 | async-start | bytes 393216 | tf_op jit(solution)/shard_map/all_to_all | solution.py:392

commit v2 on v1

--- a/solution.py
+++ b/solution.py
@@ -22,7 +22,8 @@
 SHRINK = 0.3
 BF16 = jnp.bfloat16
 F32 = jnp.float32
-VMEM_LIMIT = 40 * 1024 * 1024
+VMEM_LIMIT = 24 * 1024 * 1024
+AHEAD_VMEM = 56 * 1024 * 1024
 
 
 def split_table(table, count):
@@ -59,17 +60,10 @@
     return plain, np.stack([np.concatenate([plain, mirror]), special])
 
 
-def row_pair_tables():
-    table = width_table()
-    flat = table.reshape(2 * COLS * N_DEST, W)
+def row_pair_table():
+    flat = width_table().reshape(2 * COLS * N_DEST, W)
     zero = np.zeros_like(flat)
-    both = np.block([[flat, zero], [zero, flat]])
-    parts = []
-    for part in range(2):
-        one = table[part].reshape(COLS * N_DEST, W)
-        none = np.zeros_like(one)
-        parts.append(np.block([[one, none], [none, one]]))
-    return both, np.stack(parts)
+    return np.block([[flat, zero], [zero, flat]])
 
 
 def cut(value, count):
@@ -113,6 +107,7 @@
 
 
 N_FIELD = 2 * COLS * ROWS
+OFFSET_ROW = N_FIELD + COLS * ROWS
 
 
 def pack_rows(put, count, values):
@@ -140,23 +135,47 @@
     return value
 
 
-def ahead_kernel(seg_ref, x_ref, g_ref, both_ref, part_ref, out_ref):
+def ahead_kernel(
+    seg_ref, x_hbm, g_hbm, b_in_hbm, b_out_hbm, table_hbm, out_ref, x_ref, g_ref, b_in_ref, b_out_ref, table_ref, sems
+):
     segment = seg_ref[0]
-    pad = jnp.zeros((LANES - CH, 2 * W), F32)
+    pairs = [
+        (table_hbm, table_ref),
+        (x_hbm, x_ref),
+        (g_hbm, g_ref),
+        (b_in_hbm, b_in_ref),
+        (b_out_hbm, b_out_ref),
+    ]
+    copies = [pltpu.make_async_copy(src, dst, sems.at[n]) for n, (src, dst) in enumerate(pairs)]
+    for copy in copies:
+        copy.start()
+    pad = jnp.zeros((LANES - CH, W), F32)
     values = {}
-    both = [both_ref[n] for n in range(3)]
-    part = [part_ref[n, segment] for n in range(2)]
-    for j in range(ROWS // 2):
-        lanes = pl.ds(2 * W * j, 2 * W)
-        field = product(both, thirds(jnp.concatenate([x_ref[:, lanes], pad], axis=0)), NT, 3)
+    copies[0].wait()
+    table = [table_ref[n].reshape(2 * COLS * N_DEST, W) for n in range(3)]
+    part = [table_ref[n, segment] for n in range(2)]
+    copies[1].wait()
+    for r in range(ROWS):
+        lanes = pl.ds(W * r, W)
+        field = product(table, thirds(jnp.concatenate([x_ref[:, lanes], pad], axis=0)), NT, 3)
+        for of in range(2):
+            for c in range(COLS):
+                base = (of * COLS + c) * N_DEST
+                values[slot(of, c, r)] = field[base : base + N_DEST]
+    copies[2].wait()
+    for r in range(ROWS):
+        lanes = pl.ds(W * r, W)
         adjoint = product(part, halves(jnp.concatenate([g_ref[:, lanes], pad], axis=0)), NT)
-        for rr in range(2):
-            for c in range(COLS):
-                for of in range(2):
-                    base = ((rr * 2 + of) * COLS + c) * N_DEST
-                    values[slot(of, c, 2 * j + rr)] = field[base : base + N_DEST]
-                base = (rr * COLS + c) * N_DEST
-                values[N_FIELD + c * ROWS + 2 * j + rr] = adjoint[base : base + N_DEST]
+        for c in range(COLS):
+            base = c * N_DEST
+            values[N_FIELD + c * ROWS + r] = adjoint[base : base + N_DEST]
+    copies[3].wait()
+    copies[4].wait()
+    fill = jnp.zeros((1, LANES - CH), F32)
+    for n, ref in enumerate((b_in_ref, b_out_ref)):
+        for of in range(2):
+            one = jnp.concatenate([ref[of : of + 1, :], fill], axis=1)
+            values[OFFSET_ROW + 2 * n + of] = jnp.broadcast_to(one, (N_DEST, LANES))
 
     def put(q, value):
         out_ref[pl.ds(q, N_DEST, stride=BLOCK), :] = value
@@ -164,12 +183,13 @@
     pack_rows(put, N_DEST, values)
 
 
-def middle_kernel(flag_ref, got_ref, w_ref, b_ref, plain_ref, plain_t_ref, first_ref, first_t_ref, out_ref, grads_ref):
+def middle_kernel(flag_ref, got_ref, w_ref, plain_ref, plain_t_ref, first_ref, first_t_hbm, out_ref, grads_ref, first_t_ref, sem):
     flag = flag_ref[0]
+    fetch = pltpu.make_async_copy(first_t_hbm.at[flag], first_t_ref, sem)
+    fetch.start()
     plain = [plain_ref[n] for n in range(3)]
     plain_t = [plain_t_ref[n] for n in range(2)]
     first = [first_ref[n, flag] for n in range(3)]
-    first_t = [first_t_ref[n, flag] for n in range(2)]
     scale = jnp.where(flag == 1, 1.0, 0.5).astype(F32)
 
     def row(source, q):
@@ -206,6 +226,12 @@
         return value[:, LANES * n : LANES * (n + 1)]
 
     weights = [thirds(w_ref[n]) for n in range(4)]
+
+    def offset(s, n):
+        def get(at):
+            return got_ref[pl.ds(s * N_SPACE * BLOCK + at, 1), :]
+
+        return jnp.concatenate([unpack_row(get, 1, OFFSET_ROW + 2 * n + of) for of in range(2)], axis=1)
 
     forward = []
     for s in range(2):
@@ -213,9 +239,9 @@
             special(block(head, s)) + ordinary(block(rest, 2 * s)) + ordinary(block(rest, 2 * s + 1)), axis=0
         )
         x = thirds(x)
-        hid = product(x, weights[2 * s], NN, 3) + b_ref[2 * s : 2 * s + 1, :]
+        hid = product(x, weights[2 * s], NN, 3) + offset(s, 0)
         act = thirds(jnp.maximum(hid, 0.0))
-        out = product(act, weights[2 * s + 1], NN, 3) + b_ref[2 * s + 1 : 2 * s + 2, :]
+        out = product(act, weights[2 * s + 1], NN, 3) + offset(s, 1)
         forward.append((x, hid, act, out))
 
     def backward(s, upstream):
@@ -265,6 +291,8 @@
 
         pack_rows(put, N_SPACE, values)
 
+    fetch.wait()
+    first_t = [first_t_ref[n] for n in range(2)]
     upstream = jnp.concatenate(
         special(adjoint_head) + ordinary(block(adjoint_rest, 0)) + ordinary(block(adjoint_rest, 1)), axis=0
     )
@@ -329,51 +357,55 @@
     everyone = ("segment", "space")
     block_input, given = acts[0, 0], cotangent[0]
 
-    pair, part = row_pair_tables()
     plain, heads = height_tables()
-    pair_parts = split_table(pair, 3)
-    part_parts = split_table(part, 2)
+    table_parts = split_table(width_table().reshape(2, COLS * N_DEST, W), 3)
+    pair_parts = split_table(row_pair_table(), 2)
     plain_parts = split_table(plain, 3)
     plain_t_parts = split_table(plain.T, 2)
     head_parts = split_table(heads, 3)
-    head_t_parts = split_table(heads.transpose(0, 2, 1), 2)
-
+    head_t_parts = split_table(heads.transpose(0, 2, 1), 2).swapaxes(0, 1)
+
+    swap = [(0, 1), (1, 0)]
+    own_w = [w_in[0, :, 0], w_out[0, :, 0]]
+    other_w = [lax.ppermute(w, "segment", swap) for w in own_w]
+
+    given_arrays = (block_input, given, b_in[0], b_out[0], table_parts)
     sent = pl.pallas_call(
         ahead_kernel,
         out_shape=jax.ShapeDtypeStruct((N_DEST * BLOCK, LANES), F32),
-        in_specs=smem() + vmem(4),
+        in_specs=smem() + [pl.BlockSpec(memory_space=pl.ANY)] * len(given_arrays),
         out_specs=pl.BlockSpec(memory_space=pltpu.VMEM),
-        compiler_params=PARAMS,
+        scratch_shapes=[pltpu.VMEM(a.shape, a.dtype) for a in given_arrays]
+        + [pltpu.SemaphoreType.DMA((len(given_arrays),))],
+        compiler_params=pltpu.CompilerParams(vmem_limit_bytes=AHEAD_VMEM),
         name="ahead",
-    )(segment.astype(jnp.int32).reshape(1), block_input, given, pair_parts, part_parts)
+    )(segment.astype(jnp.int32).reshape(1), *given_arrays)
+    sent, other_w = lax.optimization_barrier((sent, other_w))
     got = lax.all_to_all(sent.reshape(N_DEST, BLOCK, LANES), everyone, 0, 0, tiled=True)
 
-    own_w = jnp.concatenate([w_in[0, :, 0], w_out[0, :, 0]])
-    own_b = jnp.concatenate([b_in[0], b_out[0]])
-    swap = [(0, 1), (1, 0)]
-    other_w = lax.ppermute(own_w, "segment", swap)
-    other_b = lax.ppermute(own_b, "segment", swap)
+    own_w, other_w = jnp.concatenate(own_w), jnp.concatenate(other_w)
     is_zero = segment == 0
     all_w = jnp.concatenate([jnp.where(is_zero, own_w, other_w), jnp.where(is_zero, other_w, own_w)])
-    all_b = jnp.concatenate([jnp.where(is_zero, own_b, other_b), jnp.where(is_zero, other_b, own_b)])
     all_w = jnp.pad(all_w, ((0, 0), (0, LANES - CH), (0, LANES - CH))).reshape(4, 2, LANES, LANES)
     w0, w1 = all_w[:, 0], all_w[:, 1]
     full_w = jnp.concatenate(
         [jnp.concatenate([w0, w1], axis=2), jnp.concatenate([-w1, w0], axis=2)], axis=1
     )
-    full_b = jnp.pad(all_b, ((0, 0), (0, LANES - CH))).reshape(4, 2 * LANES)
-    full_b = jnp.pad(full_b, ((0, 4), (0, 0)))
 
     flag = ((segment == 0) & (space == 0)).astype(jnp.int32).reshape(1)
     sent = pl.pallas_call(
         middle_kernel,
         out_shape=jax.ShapeDtypeStruct((N_DEST * BLOCK, LANES), F32),
-        in_specs=smem() + vmem(7),
+        in_specs=smem() + vmem(5) + [pl.BlockSpec(memory_space=pl.ANY)],
         out_specs=pl.BlockSpec(memory_space=pltpu.VMEM),
-        scratch_shapes=[pltpu.VMEM((4 * CH, LANES), F32)],
+        scratch_shapes=[
+            pltpu.VMEM((4 * CH, LANES), F32),
+            pltpu.VMEM(head_t_parts.shape[1:], BF16),
+            pltpu.SemaphoreType.DMA,
+        ],
         compiler_params=PARAMS,
         name="middle",
-    )(flag, got.reshape(N_DEST * BLOCK, LANES), full_w, full_b, plain_parts, plain_t_parts, head_parts, head_t_parts)
+    )(flag, got.reshape(N_DEST * BLOCK, LANES), full_w, plain_parts, plain_t_parts, head_parts, head_t_parts)
     got = lax.all_to_all(sent.reshape(N_DEST, BLOCK, LANES), everyone, 0, 0, tiled=True)
     got = got.reshape(N_DEST * BLOCK, LANES)
 
@@ -398,7 +430,7 @@
         out_specs=pl.BlockSpec(memory_space=pltpu.VMEM),
         compiler_params=PARAMS,
         name="after",
-    )(got, given, pair_parts[:2])
+    )(got, given, pair_parts)
 
     whole = whole.reshape(4, CH, LANES)[:, :, :CH]
     offsets = offsets[:, :CH]

time: 104 us -> 99 us (0.952)
  waiting for transfers between devices: 29.1 us -> 34.7 us
  local copies, waits for them, and re-layouts: 7.91 us -> 2.42 us
  blocking collectives: 30.5 us -> 26.2 us
  starting transfers between devices: 21.7 us -> 19.8 us
  Pallas kernels: 13.2 us -> 14.4 us
    all_to_all x1, waiting for transfers between devices: 0.01 us -> 21.5 us  [shards(): lax.all_to_all(sent.reshape(N_DEST, BLOCK, LANES), everyone, 0, 0, tiled=...]
    ppermute x2, waiting for transfers between devices: 21.8 us -> 5.95 us  [shards(): other_w = [lax.ppermute(w, 'segment', swap) for w in own_w]]
    unnamed x28 -> x17, local copies, waits for them, and re-layouts: 6.6 us -> 1.11 us
    all_to_all x1, blocking collectives: 30.5 us -> 26.2 us  [shards(): lax.all_to_all(sent.reshape(N_DEST, BLOCK, LANES), everyone, 0, 0, tiled=...]
    all_to_all x1, starting transfers between devices: 11.5 us -> 8.5 us  [shards(): lax.all_to_all(sent.reshape(N_DEST, BLOCK, LANES), everyone, 0, 0, tiled=...]
    ppermute x2, starting transfers between devices: 6.11 us -> 7.38 us  [shards(): other_w = [lax.ppermute(w, 'segment', swap) for w in own_w]]
  transfers between devices with their start and end apart: 4 -> 4, of which waited for: 3 -> 4; matrix products, arithmetic and copies ran while one was open for 1% -> 1% of each run, Pallas kernels for 2% -> 6%
where the time goes in v2:
time: 99 us; the launch traced here: 98.6 us
  waiting for transfers between devices  34.7 us (35%)
  blocking collectives  26.2 us (26%)
  starting transfers between devices  19.8 us (20%)
  Pallas kernels  14.4 us (15%)
  local copies, waits for them, and re-layouts  2.42 us (2%)
    all_to_all x1, blocking collectives, shards(): lax.all_to_all(sent.reshape(N_DEST, BLOCK, LANES), everyone, 0, 0, tiled=...  26.2 us
    all_to_all x1, waiting for transfers between devices, shards(): lax.all_to_all(sent.reshape(N_DEST, BLOCK, LANES), everyone, 0, 0, tiled=...  21.5 us
    all_to_all x1, starting transfers between devices, shards(): lax.all_to_all(sent.reshape(N_DEST, BLOCK, LANES), everyone, 0, 0, tiled=...  8.5 us
    pallas_call x1, Pallas kernels, shards(): pl.pallas_call(middle_kernel, out_shape=jax.ShapeDtypeStruct((N_DEST * BL...  7.94 us
    ppermute x2, starting transfers between devices, shards(): other_w = [lax.ppermute(w, 'segment', swap) for w in own_w]  7.38 us
    all_to_all x1, waiting for transfers between devices, shards(): lax.all_to_all(mine.reshape(N_SPACE, share, LANES), 'space', 0, 0, tiled=...  7.28 us
    ppermute x2, waiting for transfers between devices, shards(): other_w = [lax.ppermute(w, 'segment', swap) for w in own_w]  5.95 us
    pallas_call x1, Pallas kernels, shards(): pl.pallas_call(ahead_kernel, out_shape=jax.ShapeDtypeStruct((N_DEST * BLO...  4.07 us
  transfers between devices with their start and end apart: 4, of which 4 were waited for; matrix products, arithmetic and copies ran while one was open for 1% of the time, Pallas kernels for 6%

profile of v2, /device:TPU:8, one launch (start us, length us, event | category | flops | bytes accessed | tf_op | source)
XLA Modules:
  0.0 98.6 jit_solution(8782123137388110087)
XLA Ops:
  0.6 7.3 %collective-permute-start = (f32[2,96,96]{2,1,0:T(8,128)}, f32[2,96,96]{2,1,0:T(8,128)S(1)}, u32[]{:S(2)}, u32[]{:S(2)}) collective-permute-start(f32[2,96,96]{2,1,0:T(8,128)} %bitcast.46), channel_id=1, source_target_pairs={{0,128},{128,0},{1,129},{129,1},{2,130},{130,2},{3,131},{131,3},{4... | collective-permute-start | bytes 221192 | tf_op jit(solution)/shard_map/ppermute | solution.py:370
  7.9 0.1 collective-permute-start.1
  8.0 4.1 %ahead.1 = f32[1536,128]{1,0:T(8,128)} custom-call(s32[1]{0:T(128)} %bitcast.1.seg_ref, f32[96,1152]{1,0:T(8,128)} %bitcast.44, f32[96,1152]{1,0:T(8,128)} %bitcast.38, f32[2,96]{1,0:T(2,128)} %bitcast.50, f32[2,96]{1,0:T(2,128)} %bitcast.51, bf16[3,2,96,192]{3,2,1,0:T(8,128)(2,1)} %constant.28.clone.table_hbm), custom_call_target="tpu_custom_call" | custom-call | tf_op jit(solution)/shard_map/ahead/pallas_call | solution.py:373
  12.1 0.0 copy-start.6
  12.1 0.0 copy-start.7
  12.1 1.6 %collective-permute-done = f32[2,96,96]{2,1,0:T(8,128)S(1)} collective-permute-done((f32[2,96,96]{2,1,0:T(8,128)}, f32[2,96,96]{2,1,0:T(8,128)S(1)}, u32[]{:S(2)}, u32[]{:S(2)}) %collective-permute-start) | collective-permute-done | bytes 73760 | tf_op jit(solution)/shard_map/ppermute | solution.py:370
  13.7 4.3 %collective-permute-done.1 = f32[2,96,96]{2,1,0:T(8,128)S(1)} collective-permute-done((f32[2,96,96]{2,1,0:T(8,128)}, f32[2,96,96]{2,1,0:T(8,128)S(1)}, u32[]{:S(2)}, u32[]{:S(2)}) %collective-permute-start.1) | collective-permute-done | bytes 73760 | tf_op jit(solution)/shard_map/ppermute | solution.py:370
  18.1 8.5 %all-to-all-start = ((f32[32,48,128]{2,1,0:T(8,128)}), f32[32,48,128]{2,1,0:T(8,128)S(1)}, u32[]{:S(2)}, u32[]{:S(2)}) async-start(f32[32,48,128]{2,1,0:T(8,128)} %bitcast.42), calls=%async_computation | async-start | bytes 1572864 | tf_op jit(solution)/shard_map/all_to_all | solution.py:384
  26.6 0.0 copy-done.6
  26.6 0.0 copy-done.7
  26.8 0.0 copy-start.1
  26.8 0.0 copy-start.4
  26.8 0.0 copy-start.5
  26.8 0.1 maximum_maximum_fusion.w_ref
  26.9 21.5 %all-to-all-done = f32[32,48,128]{2,1,0:T(8,128)S(1)} async-done(((f32[32,48,128]{2,1,0:T(8,128)}), f32[32,48,128]{2,1,0:T(8,128)S(1)}, u32[]{:S(2)}, u32[]{:S(2)}) %all-to-all-start) | async-done | bytes 786464 | tf_op jit(solution)/shard_map/all_to_all | solution.py:384
  48.4 0.0 copy-done.1
  48.4 0.0 copy-done.4
  48.4 0.0 copy-done.5
  48.4 0.0 copy-start.2
  48.5 1.1 %copy-done.2 = bf16[2,2,192,384]{3,2,1,0:T(8,128)(2,1)S(1)} copy-done((bf16[2,2,192,384]{3,2,1,0:T(8,128)(2,1)S(1)}, bf16[2,2,192,384]{3,2,1,0:T(8,128)(2,1)}, u32[]{:S(2)}) %copy-start.2) | copy-done | bytes 589848
  49.5 7.9 %middle.1 = f32[1536,128]{1,0:T(8,128)S(1)} custom-call(s32[1]{0:T(128)} %bitcast.flag_ref, f32[1536,128]{1,0:T(8,128)S(1)} %bitcast.36, f32[4,256,256]{2,1,0:T(8,128)S(1)} %maximum_maximum_fusion.w_ref, bf16[3,192,192]{2,1,0:T(8,128)(2,1)S(1)} %copy-done.4, bf16[2,192,192]{2,1,0:T(8,128)(2,1)S(1)} %copy-done.5, bf16[3,2,384,192]{3,2,1,0:T(8,128)(2,1)S(1)} %copy-done.1, ...), custom_call_target="tpu_custom_call" | custom-call | tf_op jit(solution)/shard_map/middle/pallas_call | solution.py:396
  57.5 0.0 copy-start
  57.5 0.0 copy-start.3
  57.5 26.2 %all_to_all.15 = f32[32,48,128]{2,1,0:T(8,128)S(1)} all-to-all(f32[32,48,128]{2,1,0:T(8,128)S(1)} %bitcast.37), channel_id=1, replica_groups=mesh['segment'=2,'space'=16,'chan'=8] {'segment','space'}, dimensions={0} | all-to-all | bytes 1572864 | tf_op jit(solution)/shard_map/all_to_all | solution.py:409
  83.7 0.8 total.1
  84.5 4.0 %all-to-all-start.2 = ((f32[16,24,128]{2,1,0:T(8,128)}), f32[16,24,128]{2,1,0:T(8,128)S(1)}, u32[]{:S(2)}, u32[]{:S(2)}) async-start(f32[16,24,128]{2,1,0:T(8,128)} %bitcast.16), calls=%async_computation.2 | async-start | bytes 393216 | tf_op jit(solution)/shard_map/all_to_all | solution.py:424
  88.5 0.0 copy-done
  88.5 0.0 copy-done.3
  88.5 1.6 %after.1 = f32[96,1152]{1,0:T(8,128)} custom-call(f32[1536,128]{1,0:T(8,128)S(1)} %bitcast.35, f32[96,1152]{1,0:T(8,128)S(1)} %bitcast.39, bf16[2,384,384]{2,1,0:T(8,128)(2,1)S(1)} %copy-done.3), custom_call_target="tpu_custom_call" | custom-call | tf_op jit(solution)/shard_map/after/pallas_call | solution.py:426
  90.1 0.6 slice_bitcast_fusion.4
  90.6 7.3 %all-to-all-done.2 = f32[16,24,128]{2,1,0:T(8,128)S(1)} async-done(((f32[16,24,128]{2,1,0:T(8,128)}), f32[16,24,128]{2,1,0:T(8,128)S(1)}, u32[]{:S(2)}, u32[]{:S(2)}) %all-to-all-start.2) | async-done | bytes 196640 | tf_op jit(solution)/shard_map/all_to_all | solution.py:424
  97.9 0.7 slice_bitcast_fusion.2
  (6 shorter events, 0.2 us)
Async XLA Ops:
  0.6 13.1 %collective-permute-start = (f32[2,96,96]{2,1,0:T(8,128)}, f32[2,96,96]{2,1,0:T(8,128)S(1)}, u32[]{:S(2)}, u32[]{:S(2)}) collective-permute-start(f32[2,96,96]{2,1,0:T(8,128)} %bitcast.46), channel_id=1, source_target_pairs={{0,128},{128,0},{1,129},{129,1},{2,130},{130,2},{3,131},{131,3},{4... | collective-permute-start | bytes 221192 | tf_op jit(solution)/shard_map/ppermute | solution.py:370
  7.9 10.2 %collective-permute-start.1 = (f32[2,96,96]{2,1,0:T(8,128)}, f32[2,96,96]{2,1,0:T(8,128)S(1)}, u32[]{:S(2)}, u32[]{:S(2)}) collective-permute-start(f32[2,96,96]{2,1,0:T(8,128)} %bitcast.48), channel_id=1, source_target_pairs={{0,128},{128,0},{1,129},{129,1},{2,130},{130,2},{3,131},{131,3},{4... | collective-permute-start | bytes 221192 | tf_op jit(solution)/shard_map/ppermute | solution.py:370
  12.1 14.5 %copy-start.6 = (f32[1,2,1,96,96]{4,3,2,1,0:T(8,128)S(1)}, f32[1,2,1,96,96]{4,3,2,1,0:T(8,128)}, u32[]{:S(2)}) copy-start(f32[1,2,1,96,96]{4,3,2,1,0:T(8,128)} %param.14) | copy-start | bytes 221188
  12.1 14.5 %copy-start.7 = (f32[1,2,1,96,96]{4,3,2,1,0:T(8,128)S(1)}, f32[1,2,1,96,96]{4,3,2,1,0:T(8,128)}, u32[]{:S(2)}) copy-start(f32[1,2,1,96,96]{4,3,2,1,0:T(8,128)} %param.15) | copy-start | bytes 221188
  18.1 30.4 %all-to-all-start = ((f32[32,48,128]{2,1,0:T(8,128)}), f32[32,48,128]{2,1,0:T(8,128)S(1)}, u32[]{:S(2)}, u32[]{:S(2)}) async-start(f32[32,48,128]{2,1,0:T(8,128)} %bitcast.42), calls=%async_computation | async-start | bytes 1572864 | tf_op jit(solution)/shard_map/all_to_all | solution.py:384
  26.8 21.6 %copy-start.1 = (bf16[3,2,384,192]{3,2,1,0:T(8,128)(2,1)S(1)}, bf16[3,2,384,192]{3,2,1,0:T(8,128)(2,1)}, u32[]{:S(2)}) copy-start(bf16[3,2,384,192]{3,2,1,0:T(8,128)(2,1)} %constant.31.clone.first_ref) | copy-start | bytes 2654212
  26.8 21.6 %copy-start.4 = (bf16[3,192,192]{2,1,0:T(8,128)(2,1)S(1)}, bf16[3,192,192]{2,1,0:T(8,128)(2,1)}, u32[]{:S(2)}) copy-start(bf16[3,192,192]{2,1,0:T(8,128)(2,1)} %constant.29.clone.plain_ref) | copy-start | bytes 663556
  26.8 21.6 %copy-start.5 = (bf16[2,192,192]{2,1,0:T(8,128)(2,1)S(1)}, bf16[2,192,192]{2,1,0:T(8,128)(2,1)}, u32[]{:S(2)}) copy-start(bf16[2,192,192]{2,1,0:T(8,128)(2,1)} %constant.30.clone.plain_t_ref) | copy-start | bytes 442372
  48.4 1.1 %copy-start.2 = (bf16[2,2,192,384]{3,2,1,0:T(8,128)(2,1)S(1)}, bf16[2,2,192,384]{3,2,1,0:T(8,128)(2,1)}, u32[]{:S(2)}) copy-start(bf16[2,2,192,384]{3,2,1,0:T(8,128)(2,1)} %constant.32.clone.first_t_hbm) | copy-start | bytes 1769476
  57.5 31.0 %copy-start = (f32[1,96,1152]{2,1,0:T(8,128)S(1)}, f32[1,96,1152]{2,1,0:T(8,128)}, u32[]{:S(2)}) copy-start(f32[1,96,1152]{2,1,0:T(8,128)} %param.13) | copy-start | bytes 1327108
  57.5 31.0 %copy-start.3 = (bf16[2,384,384]{2,1,0:T(8,128)(2,1)S(1)}, bf16[2,384,384]{2,1,0:T(8,128)(2,1)}, u32[]{:S(2)}) copy-start(bf16[2,384,384]{2,1,0:T(8,128)(2,1)} %constant.33.clone.pair_ref) | copy-start | bytes 1769476
  84.5 13.4 %all-to-all-start.2 = ((f32[16,24,128]{2,1,0:T(8,128)}), f32[16,24,128]{2,1,0:T(8,128)S(1)}, u32[]{:S(2)}, u32[]{:S(2)}) async-start(f32[16,24,128]{2,1,0:T(8,128)} %bitcast.16), calls=%async_computation.2 | async-start | bytes 393216 | tf_op jit(solution)/shard_map/all_to_all | solution.py:424

commit v3 on v2

--- a/solution.py
+++ b/solution.py
@@ -15,6 +15,7 @@
 LANES = 128
 N_SPACE = 16
 N_SEG = 2
+N_X = 4
 N_DEST = N_SPACE * N_SEG
 ROWS = H // N_SPACE
 COLS = W // 2 // N_DEST
@@ -49,15 +50,11 @@
     return both.reshape(2, N_DEST, COLS, W).transpose(0, 2, 1, 3)
 
 
-def height_tables():
+def height_table():
     cos_h, sin_h = dft(H)
     order = np.array([ROWS * p + r for r in range(ROWS) for p in range(N_SPACE)])
-    cos_h, sin_h = cos_h[:, order], sin_h[:, order]
-    zero = np.zeros_like(cos_h)
-    plain = np.block([[cos_h, sin_h], [-sin_h, cos_h]])
-    mirror = np.block([[cos_h, sin_h], [sin_h, -cos_h]])
-    special = np.block([[cos_h, zero], [-sin_h, zero], [zero, cos_h], [zero, -sin_h]])
-    return plain, np.stack([np.concatenate([plain, mirror]), special])
+    cos_h, sin_h = cos_h[np.ix_(order, order)], sin_h[np.ix_(order, order)]
+    return np.block([[cos_h, sin_h], [-sin_h, cos_h]])
 
 
 def row_pair_table():
@@ -151,24 +148,28 @@
         copy.start()
     pad = jnp.zeros((LANES - CH, W), F32)
     values = {}
+
+    def two_rows(ref, r):
+        return jnp.concatenate([ref[:, pl.ds(W * r, W)], pad, ref[:, pl.ds(W * (r + 1), W)], pad], axis=0)
+
     copies[0].wait()
     table = [table_ref[n].reshape(2 * COLS * N_DEST, W) for n in range(3)]
     part = [table_ref[n, segment] for n in range(2)]
     copies[1].wait()
-    for r in range(ROWS):
-        lanes = pl.ds(W * r, W)
-        field = product(table, thirds(jnp.concatenate([x_ref[:, lanes], pad], axis=0)), NT, 3)
-        for of in range(2):
+    for r in range(0, ROWS, 2):
+        field = product(table, thirds(two_rows(x_ref, r)), NT, 3)
+        for rr in range(2):
+            for of in range(2):
+                for c in range(COLS):
+                    base = (of * COLS + c) * N_DEST
+                    values[slot(of, c, r + rr)] = field[base : base + N_DEST, LANES * rr : LANES * (rr + 1)]
+    copies[2].wait()
+    for r in range(0, ROWS, 2):
+        adjoint = product(part, halves(two_rows(g_ref, r)), NT)
+        for rr in range(2):
             for c in range(COLS):
-                base = (of * COLS + c) * N_DEST
-                values[slot(of, c, r)] = field[base : base + N_DEST]
-    copies[2].wait()
-    for r in range(ROWS):
-        lanes = pl.ds(W * r, W)
-        adjoint = product(part, halves(jnp.concatenate([g_ref[:, lanes], pad], axis=0)), NT)
-        for c in range(COLS):
-            base = c * N_DEST
-            values[N_FIELD + c * ROWS + r] = adjoint[base : base + N_DEST]
+                base = c * N_DEST
+                values[N_FIELD + c * ROWS + r + rr] = adjoint[base : base + N_DEST, LANES * rr : LANES * (rr + 1)]
     copies[3].wait()
     copies[4].wait()
     fill = jnp.zeros((1, LANES - CH), F32)
@@ -183,14 +184,10 @@
     pack_rows(put, N_DEST, values)
 
 
-def middle_kernel(flag_ref, got_ref, w_ref, plain_ref, plain_t_ref, first_ref, first_t_hbm, out_ref, grads_ref, first_t_ref, sem):
-    flag = flag_ref[0]
-    fetch = pltpu.make_async_copy(first_t_hbm.at[flag], first_t_ref, sem)
-    fetch.start()
-    plain = [plain_ref[n] for n in range(3)]
-    plain_t = [plain_t_ref[n] for n in range(2)]
-    first = [first_ref[n, flag] for n in range(3)]
-    scale = jnp.where(flag == 1, 1.0, 0.5).astype(F32)
+def middle_kernel(flag_ref, got_ref, w_ref, table_ref, out_ref, grads_ref):
+    is_special = flag_ref[0] == 1
+    table = [table_ref[n] for n in range(3)]
+    scale = jnp.where(is_special, 1.0, 0.5).astype(F32)
 
     def row(source, q):
         def get(at):
@@ -204,26 +201,31 @@
     def adjoint_column(c):
         return jnp.concatenate([row(of, N_FIELD + c * ROWS + r) for of in range(2) for r in range(ROWS)], axis=0)
 
+    nothing = jnp.zeros((H, LANES), F32)
+
+    def block(value, n):
+        return value[:, LANES * n : LANES * (n + 1)]
+
+    def spread(first):
+        one = jnp.concatenate([first[:H], jnp.where(is_special, nothing, first[H:])], axis=0)
+        return [one, jnp.concatenate([first[H:], nothing], axis=0)]
+
     def ordinary(column):
         r, i = column[:H], column[H:]
         return [jnp.concatenate([r, i], axis=1), jnp.concatenate([r, -i], axis=1)]
 
-    def special(column):
-        return [
-            jnp.concatenate([column[:H], column[H : 2 * H]], axis=1),
-            jnp.concatenate([column[2 * H : 3 * H], column[3 * H :]], axis=1),
-        ]
+    def leading(one, two):
+        mirror = jnp.where(is_special, two, jnp.concatenate([one[:H], -one[H:]], axis=0))
+        return [jnp.concatenate([v[:H], v[H:]], axis=1) for v in (one, mirror)]
+
+    def transform(columns, parts):
+        return product(table, cut(jnp.concatenate(columns, axis=1), parts), NN, parts)
 
     adjoint_first = adjoint_column(0)
-    head = product(first, thirds(jnp.concatenate([field_column(s, 0) for s in range(2)], axis=1)), NN, 3)
-    rest = product(
-        plain, thirds(jnp.concatenate([field_column(s, c) for s in range(2) for c in (1, 2)], axis=1)), NN, 3
-    )
-    adjoint_head = product(first, halves(adjoint_first), NN)
-    adjoint_rest = product(plain, halves(jnp.concatenate([adjoint_column(c) for c in (1, 2)], axis=1)), NN)
-
-    def block(value, n):
-        return value[:, LANES * n : LANES * (n + 1)]
+    fields = transform(
+        [v for s in range(2) for v in spread(field_column(s, 0)) + [field_column(s, 1), field_column(s, 2)]], 3
+    )
+    adjoints = transform(spread(adjoint_first) + [adjoint_column(1), adjoint_column(2)], 2)
 
     weights = [thirds(w_ref[n]) for n in range(4)]
 
@@ -235,9 +237,8 @@
 
     forward = []
     for s in range(2):
-        x = jnp.concatenate(
-            special(block(head, s)) + ordinary(block(rest, 2 * s)) + ordinary(block(rest, 2 * s + 1)), axis=0
-        )
+        parts = [block(fields, 4 * s + n) for n in range(4)]
+        x = jnp.concatenate(leading(parts[0], parts[1]) + ordinary(parts[2]) + ordinary(parts[3]), axis=0)
         x = thirds(x)
         hid = product(x, weights[2 * s], NN, 3) + offset(s, 0)
         act = thirds(jnp.maximum(hid, 0.0))
@@ -261,17 +262,25 @@
             total = jnp.sum(value, axis=0, keepdims=True)
             offsets += [total[:, :LANES], total[:, LANES:]]
         sums = []
-        for c in (1, 2):
+        for c in range(COLS):
             one, two = grad_x[2 * c * H : (2 * c + 1) * H], grad_x[(2 * c + 1) * H : (2 * c + 2) * H]
-            sums.append(
-                jnp.concatenate([one[:, :LANES] + two[:, :LANES], one[:, LANES:] - two[:, LANES:]], axis=0)
-            )
-        lead = jnp.concatenate(
-            [grad_x[:H, :LANES], grad_x[:H, LANES:], grad_x[H : 2 * H, :LANES], grad_x[H : 2 * H, LANES:]], axis=0
+            sums.append((one[:, :LANES] + two[:, :LANES], one[:, LANES:] - two[:, LANES:]))
+        one = jnp.concatenate(
+            [
+                jnp.where(is_special, grad_x[:H, :LANES], sums[0][0]),
+                -jnp.where(is_special, grad_x[:H, LANES:], sums[0][1]),
+            ],
+            axis=0,
         )
-        head_back = product(first_t, halves(lead), NN)
-        rest_back = product(plain_t, halves(jnp.concatenate(sums, axis=1)), NN)
-        return [head_back, block(rest_back, 0), block(rest_back, 1)], sums, offsets
+        two = jnp.concatenate([grad_x[H : 2 * H, :LANES], -grad_x[H : 2 * H, LANES:]], axis=0)
+        back = transform([one, two] + [jnp.concatenate([r, -i], axis=0) for r, i in sums[1:]], 2)
+        columns = []
+        for n in (0, 2, 3):
+            low = -block(back, n)[H:]
+            if n == 0:
+                low = jnp.where(is_special, block(back, 1)[:H], low)
+            columns.append(jnp.concatenate([block(back, n)[:H], low], axis=0))
+        return columns, [jnp.concatenate(pair, axis=0) for pair in sums[1:]], offsets
 
     def emit(s, columns, offsets):
         values = {}
@@ -291,19 +300,16 @@
 
         pack_rows(put, N_SPACE, values)
 
-    fetch.wait()
-    first_t = [first_t_ref[n] for n in range(2)]
-    upstream = jnp.concatenate(
-        special(adjoint_head) + ordinary(block(adjoint_rest, 0)) + ordinary(block(adjoint_rest, 1)), axis=0
-    )
+    parts = [block(adjoints, n) for n in range(4)]
+    upstream = jnp.concatenate(leading(parts[0], parts[1]) + ordinary(parts[2]) + ordinary(parts[3]), axis=0)
     columns_one, sums, offsets = backward(1, upstream)
     emit(1, columns_one, offsets)
 
-    head_next = product(first, halves(adjoint_first + scale * columns_one[0]), NN)
+    lead = transform(spread(adjoint_first + scale * columns_one[0]), 2)
     upstream = jnp.concatenate(
-        special(head_next)
-        + ordinary(block(adjoint_rest, 0) + 0.5 * sums[0])
-        + ordinary(block(adjoint_rest, 1) + 0.5 * sums[1]),
+        leading(block(lead, 0), block(lead, 1))
+        + ordinary(parts[2] + 0.5 * sums[0])
+        + ordinary(parts[3] + 0.5 * sums[1]),
         axis=0,
     )
     columns_zero, sums, offsets = backward(0, upstream)
@@ -357,17 +363,14 @@
     everyone = ("segment", "space")
     block_input, given = acts[0, 0], cotangent[0]
 
-    plain, heads = height_tables()
     table_parts = split_table(width_table().reshape(2, COLS * N_DEST, W), 3)
     pair_parts = split_table(row_pair_table(), 2)
-    plain_parts = split_table(plain, 3)
-    plain_t_parts = split_table(plain.T, 2)
-    head_parts = split_table(heads, 3)
-    head_t_parts = split_table(heads.transpose(0, 2, 1), 2).swapaxes(0, 1)
-
-    swap = [(0, 1), (1, 0)]
+    height_parts = split_table(height_table(), 3)
+
+    depth = N_DEST // N_X
+    swap = [(z * N_X + x, (depth - 1 - z) * N_X + x) for z in range(depth) for x in range(N_X)]
     own_w = [w_in[0, :, 0], w_out[0, :, 0]]
-    other_w = [lax.ppermute(w, "segment", swap) for w in own_w]
+    other_w = [lax.ppermute(w, everyone, swap) for w in own_w]
 
     given_arrays = (block_input, given, b_in[0], b_out[0], table_parts)
     sent = pl.pallas_call(
@@ -396,16 +399,12 @@
     sent = pl.pallas_call(
         middle_kernel,
         out_shape=jax.ShapeDtypeStruct((N_DEST * BLOCK, LANES), F32),
-        in_specs=smem() + vmem(5) + [pl.BlockSpec(memory_space=pl.ANY)],
+        in_specs=smem() + vmem(3),
         out_specs=pl.BlockSpec(memory_space=pltpu.VMEM),
-        scratch_shapes=[
-            pltpu.VMEM((4 * CH, LANES), F32),
-            pltpu.VMEM(head_t_parts.shape[1:], BF16),
-            pltpu.SemaphoreType.DMA,
-        ],
+        scratch_shapes=[pltpu.VMEM((4 * CH, LANES), F32)],
         compiler_params=PARAMS,
         name="middle",
-    )(flag, got.reshape(N_DEST * BLOCK, LANES), full_w, plain_parts, plain_t_parts, head_parts, head_t_parts)
+    )(flag, got.reshape(N_DEST * BLOCK, LANES), full_w, height_parts)
     got = lax.all_to_all(sent.reshape(N_DEST, BLOCK, LANES), everyone, 0, 0, tiled=True)
     got = got.reshape(N_DEST * BLOCK, LANES)
 

time: 99 us -> 95.9 us (0.969)
  waiting for transfers between devices: 34.7 us -> 32.7 us
  starting transfers between devices: 19.8 us -> 18.4 us
    ppermute x2, starting transfers between devices: 7.38 us -> 6.04 us  [shards(): other_w = [lax.ppermute(w, everyone, swap) for w in own_w]]
    ppermute x2, waiting for transfers between devices: 5.95 us -> 4.94 us  [shards(): other_w = [lax.ppermute(w, everyone, swap) for w in own_w]]
where the time goes in v3:
time: 95.9 us; the launch traced here: 95.5 us
  waiting for transfers between devices  32.7 us (34%)
  blocking collectives  27.1 us (28%)
  starting transfers between devices  18.4 us (19%)
  Pallas kernels  14.2 us (15%)
  local copies, waits for them, and re-layouts  2.24 us (2%)
    all_to_all x1, blocking collectives, shards(): lax.all_to_all(sent.reshape(N_DEST, BLOCK, LANES), everyone, 0, 0, tiled=...  27.1 us
    all_to_all x1, waiting for transfers between devices, shards(): lax.all_to_all(sent.reshape(N_DEST, BLOCK, LANES), everyone, 0, 0, tiled=...  20.6 us
    all_to_all x1, starting transfers between devices, shards(): lax.all_to_all(sent.reshape(N_DEST, BLOCK, LANES), everyone, 0, 0, tiled=...  8.41 us
    pallas_call x1, Pallas kernels, shards(): pl.pallas_call(middle_kernel, out_shape=jax.ShapeDtypeStruct((N_DEST * BL...  7.42 us
    all_to_all x1, waiting for transfers between devices, shards(): lax.all_to_all(mine.reshape(N_SPACE, share, LANES), 'space', 0, 0, tiled=...  7.23 us
    ppermute x2, starting transfers between devices, shards(): other_w = [lax.ppermute(w, everyone, swap) for w in own_w]  6.04 us
    ppermute x2, waiting for transfers between devices, shards(): other_w = [lax.ppermute(w, everyone, swap) for w in own_w]  4.94 us
    pallas_call x1, Pallas kernels, shards(): pl.pallas_call(ahead_kernel, out_shape=jax.ShapeDtypeStruct((N_DEST * BLO...  4.28 us
  transfers between devices with their start and end apart: 4, of which 4 were waited for; matrix products, arithmetic and copies ran while one was open for 1% of the time, Pallas kernels for 6%

profile of v3, /device:TPU:8, one launch (start us, length us, event | category | flops | bytes accessed | tf_op | source)
XLA Modules:
  0.0 95.5 jit_solution(2314466214828544441)
XLA Ops:
  0.6 5.9 %collective-permute-start = (f32[2,96,96]{2,1,0:T(8,128)}, f32[2,96,96]{2,1,0:T(8,128)S(1)}, u32[]{:S(2)}, u32[]{:S(2)}) collective-permute-start(f32[2,96,96]{2,1,0:T(8,128)} %bitcast.46), channel_id=1, source_target_pairs={{0,224},{8,232},{16,240},{24,248},{32,192},{40,200},{48,208},{56,2... | collective-permute-start | bytes 221192 | tf_op jit(solution)/shard_map/ppermute | solution.py:373
  6.6 0.1 collective-permute-start.1
  6.7 4.3 %ahead.1 = f32[1536,128]{1,0:T(8,128)} custom-call(s32[1]{0:T(128)} %bitcast.1.seg_ref, f32[96,1152]{1,0:T(8,128)} %bitcast.44, f32[96,1152]{1,0:T(8,128)} %bitcast.38, f32[2,96]{1,0:T(2,128)} %bitcast.50, f32[2,96]{1,0:T(2,128)} %bitcast.51, bf16[3,2,96,192]{3,2,1,0:T(8,128)(2,1)} %constant.22.clone.table_hbm), custom_call_target="tpu_custom_call" | custom-call | tf_op jit(solution)/shard_map/ahead/pallas_call | solution.py:376
  11.0 3.2 %collective-permute-done = f32[2,96,96]{2,1,0:T(8,128)S(1)} collective-permute-done((f32[2,96,96]{2,1,0:T(8,128)}, f32[2,96,96]{2,1,0:T(8,128)S(1)}, u32[]{:S(2)}, u32[]{:S(2)}) %collective-permute-start) | collective-permute-done | bytes 73760 | tf_op jit(solution)/shard_map/ppermute | solution.py:373
  14.2 1.7 %collective-permute-done.1 = f32[2,96,96]{2,1,0:T(8,128)S(1)} collective-permute-done((f32[2,96,96]{2,1,0:T(8,128)}, f32[2,96,96]{2,1,0:T(8,128)S(1)}, u32[]{:S(2)}, u32[]{:S(2)}) %collective-permute-start.1) | collective-permute-done | bytes 73760 | tf_op jit(solution)/shard_map/ppermute | solution.py:373
  15.9 8.4 %all-to-all-start = ((f32[32,48,128]{2,1,0:T(8,128)}), f32[32,48,128]{2,1,0:T(8,128)S(1)}, u32[]{:S(2)}, u32[]{:S(2)}) async-start(f32[32,48,128]{2,1,0:T(8,128)} %bitcast.42), calls=%async_computation | async-start | bytes 1572864 | tf_op jit(solution)/shard_map/all_to_all | solution.py:387
  24.3 0.0 copy-start.3
  24.4 0.0 copy-start.4
  24.4 0.9 copy-done.3
  25.2 0.0 copy-done.4
  25.5 0.0 copy-start.2
  25.5 0.1 maximum_maximum_fusion.w_ref
  25.6 20.6 %all-to-all-done = f32[32,48,128]{2,1,0:T(8,128)S(1)} async-done(((f32[32,48,128]{2,1,0:T(8,128)}), f32[32,48,128]{2,1,0:T(8,128)S(1)}, u32[]{:S(2)}, u32[]{:S(2)}) %all-to-all-start) | async-done | bytes 786464 | tf_op jit(solution)/shard_map/all_to_all | solution.py:387
  46.1 0.0 copy-done.2
  46.1 7.4 %middle.1 = f32[1536,128]{1,0:T(8,128)S(1)} custom-call(s32[1]{0:T(128)} %bitcast.flag_ref, f32[1536,128]{1,0:T(8,128)S(1)} %bitcast.36, f32[4,256,256]{2,1,0:T(8,128)S(1)} %maximum_maximum_fusion.w_ref, bf16[3,192,192]{2,1,0:T(8,128)(2,1)S(1)} %copy-done.2), custom_call_target="tpu_custom_call" | custom-call | tf_op jit(solution)/shard_map/middle/pallas_call | solution.py:399
  53.6 27.1 %all_to_all.15 = f32[32,48,128]{2,1,0:T(8,128)S(1)} all-to-all(f32[32,48,128]{2,1,0:T(8,128)S(1)} %bitcast.37), channel_id=1, replica_groups=mesh['segment'=2,'space'=16,'chan'=8] {'segment','space'}, dimensions={0} | all-to-all | bytes 1572864 | tf_op jit(solution)/shard_map/all_to_all | solution.py:408
  80.6 0.0 copy-start
  80.6 0.0 copy-start.1
  80.6 0.8 total.1
  81.4 3.9 %all-to-all-start.2 = ((f32[16,24,128]{2,1,0:T(8,128)}), f32[16,24,128]{2,1,0:T(8,128)S(1)}, u32[]{:S(2)}, u32[]{:S(2)}) async-start(f32[16,24,128]{2,1,0:T(8,128)} %bitcast.16), calls=%async_computation.2 | async-start | bytes 393216 | tf_op jit(solution)/shard_map/all_to_all | solution.py:423
  85.4 0.0 copy-done
  85.4 0.0 copy-done.1
  85.4 1.6 %after.1 = f32[96,1152]{1,0:T(8,128)} custom-call(f32[1536,128]{1,0:T(8,128)S(1)} %bitcast.35, f32[96,1152]{1,0:T(8,128)S(1)} %bitcast.39, bf16[2,384,384]{2,1,0:T(8,128)(2,1)S(1)} %copy-done.1), custom_call_target="tpu_custom_call" | custom-call | tf_op jit(solution)/shard_map/after/pallas_call | solution.py:425
  87.0 0.6 slice_bitcast_fusion.4
  87.6 7.2 %all-to-all-done.2 = f32[16,24,128]{2,1,0:T(8,128)S(1)} async-done(((f32[16,24,128]{2,1,0:T(8,128)}), f32[16,24,128]{2,1,0:T(8,128)S(1)}, u32[]{:S(2)}, u32[]{:S(2)}) %all-to-all-start.2) | async-done | bytes 196640 | tf_op jit(solution)/shard_map/all_to_all | solution.py:423
  94.8 0.7 slice_bitcast_fusion.2
  (6 shorter events, 0.2 us)
Async XLA Ops:
  0.6 13.6 %collective-permute-start = (f32[2,96,96]{2,1,0:T(8,128)}, f32[2,96,96]{2,1,0:T(8,128)S(1)}, u32[]{:S(2)}, u32[]{:S(2)}) collective-permute-start(f32[2,96,96]{2,1,0:T(8,128)} %bitcast.46), channel_id=1, source_target_pairs={{0,224},{8,232},{16,240},{24,248},{32,192},{40,200},{48,208},{56,2... | collective-permute-start | bytes 221192 | tf_op jit(solution)/shard_map/ppermute | solution.py:373
  6.6 9.3 %collective-permute-start.1 = (f32[2,96,96]{2,1,0:T(8,128)}, f32[2,96,96]{2,1,0:T(8,128)S(1)}, u32[]{:S(2)}, u32[]{:S(2)}) collective-permute-start(f32[2,96,96]{2,1,0:T(8,128)} %bitcast.48), channel_id=1, source_target_pairs={{0,224},{8,232},{16,240},{24,248},{32,192},{40,200},{48,208},{56,2... | collective-permute-start | bytes 221192 | tf_op jit(solution)/shard_map/ppermute | solution.py:373
  15.9 30.2 %all-to-all-start = ((f32[32,48,128]{2,1,0:T(8,128)}), f32[32,48,128]{2,1,0:T(8,128)S(1)}, u32[]{:S(2)}, u32[]{:S(2)}) async-start(f32[32,48,128]{2,1,0:T(8,128)} %bitcast.42), calls=%async_computation | async-start | bytes 1572864 | tf_op jit(solution)/shard_map/all_to_all | solution.py:387
  24.3 0.9 copy-start.3
  24.4 0.9 copy-start.4
  25.5 20.7 %copy-start.2 = (bf16[3,192,192]{2,1,0:T(8,128)(2,1)S(1)}, bf16[3,192,192]{2,1,0:T(8,128)(2,1)}, u32[]{:S(2)}) copy-start(bf16[3,192,192]{2,1,0:T(8,128)(2,1)} %constant.23.clone.table_ref) | copy-start | bytes 663556
  80.6 4.8 %copy-start = (f32[1,96,1152]{2,1,0:T(8,128)S(1)}, f32[1,96,1152]{2,1,0:T(8,128)}, u32[]{:S(2)}) copy-start(f32[1,96,1152]{2,1,0:T(8,128)} %param.10) | copy-start | bytes 1327108
  80.6 4.8 %copy-start.1 = (bf16[2,384,384]{2,1,0:T(8,128)(2,1)S(1)}, bf16[2,384,384]{2,1,0:T(8,128)(2,1)}, u32[]{:S(2)}) copy-start(bf16[2,384,384]{2,1,0:T(8,128)(2,1)} %constant.24.clone.pair_ref) | copy-start | bytes 1769476
  81.4 13.4 %all-to-all-start.2 = ((f32[16,24,128]{2,1,0:T(8,128)}), f32[16,24,128]{2,1,0:T(8,128)S(1)}, u32[]{:S(2)}, u32[]{:S(2)}) async-start(f32[16,24,128]{2,1,0:T(8,128)} %bitcast.16), calls=%async_computation.2 | async-start | bytes 393216 | tf_op jit(solution)/shard_map/all_to_all | solution.py:423

commit v4 on v3

--- a/solution.py
+++ b/solution.py
@@ -15,11 +15,12 @@
 LANES = 128
 N_SPACE = 16
 N_SEG = 2
-N_X = 4
 N_DEST = N_SPACE * N_SEG
 ROWS = H // N_SPACE
 COLS = W // 2 // N_DEST
-BLOCK = 48
+EXTRA = 16
+BLOCK_IN = 56
+BLOCK_OUT = 48
 SHRINK = 0.3
 BF16 = jnp.bfloat16
 F32 = jnp.float32
@@ -104,102 +105,141 @@
 
 
 N_FIELD = 2 * COLS * ROWS
-OFFSET_ROW = N_FIELD + COLS * ROWS
-
-
-def pack_rows(put, count, values):
+WEIGHT_ROW = N_FIELD + 4
+SHARE = 4 * CH // N_SPACE
+
+
+def pack_rows(put, count, values, block):
     lane = lane_index(count)
-    for q in range(BLOCK):
-        third, extra = divmod(q, 16)
+    for q in range(block):
         value = values.get(q)
-        packed = values.get(BLOCK + extra)
         if value is None:
             value = jnp.zeros((count, LANES), F32)
-        if packed is not None:
+        third, extra = divmod(q, EXTRA)
+        packed = values.get(block + extra)
+        if packed is not None and third < 3:
             value = jnp.where(lane < CH, value, pltpu.roll(packed, CH - 32 * third, 1))
         put(q, value)
 
 
-def unpack_row(get, count, q):
-    if q < BLOCK:
-        return get(q)
-    lane = lane_index(count)
-    extra = q - BLOCK
-    value = jnp.zeros((count, LANES), F32)
-    for third in range(3):
-        moved = pltpu.roll(get(extra + 16 * third), (32 * third - CH) % LANES, 1)
+def join_thirds(thirds_of):
+    lane = lane_index(thirds_of[0].shape[0])
+    value = jnp.zeros(thirds_of[0].shape, F32)
+    for third, part in enumerate(thirds_of):
+        moved = pltpu.roll(part, (32 * third - CH) % LANES, 1)
         value = jnp.where((lane >= 32 * third) & (lane < 32 * third + 32), moved, value)
     return value
 
 
+def unpack_row(get, q, block):
+    if q < block:
+        return get(q)
+    return join_thirds([get(q - block + EXTRA * third) for third in range(3)])
+
+
 def ahead_kernel(
-    seg_ref, x_hbm, g_hbm, b_in_hbm, b_out_hbm, table_hbm, out_ref, x_ref, g_ref, b_in_ref, b_out_ref, table_ref, sems
+    place_ref, x_hbm, g_hbm, b_in_hbm, b_out_hbm, w_in_hbm, w_out_hbm, table_hbm,
+    out_ref, x_ref, g_ref, b_in_ref, b_out_ref, w_ref, table_ref, sems,
 ):
-    segment = seg_ref[0]
-    pairs = [
-        (table_hbm, table_ref),
-        (x_hbm, x_ref),
-        (g_hbm, g_ref),
-        (b_in_hbm, b_in_ref),
-        (b_out_hbm, b_out_ref),
-    ]
+    segment, space = place_ref[0], place_ref[1]
+    pairs = [(table_hbm, table_ref)]
+    for src, dst in ((x_hbm, x_ref), (g_hbm, g_ref)):
+        for j in range(ROWS // 2):
+            lanes = pl.ds(2 * W * j, 2 * W)
+            pairs.append((src.at[:, lanes], dst.at[:, lanes]))
+    pairs += [(b_in_hbm, b_in_ref), (b_out_hbm, b_out_ref), (w_in_hbm, w_ref.at[0:2]), (w_out_hbm, w_ref.at[2:4])]
     copies = [pltpu.make_async_copy(src, dst, sems.at[n]) for n, (src, dst) in enumerate(pairs)]
     for copy in copies:
         copy.start()
     pad = jnp.zeros((LANES - CH, W), F32)
-    values = {}
+    fields = [{} for _ in range(N_SEG)]
+    adjoints = {}
 
     def two_rows(ref, r):
         return jnp.concatenate([ref[:, pl.ds(W * r, W)], pad, ref[:, pl.ds(W * (r + 1), W)], pad], axis=0)
 
+    def cut_out(value, base, rr):
+        return value[base : base + N_SPACE, LANES * rr : LANES * (rr + 1)]
+
     copies[0].wait()
-    table = [table_ref[n].reshape(2 * COLS * N_DEST, W) for n in range(3)]
+    table = [table_ref[n].reshape(N_SEG * 2 * COLS * N_SPACE, W) for n in range(3)]
     part = [table_ref[n, segment] for n in range(2)]
-    copies[1].wait()
     for r in range(0, ROWS, 2):
+        copies[1 + r // 2].wait()
         field = product(table, thirds(two_rows(x_ref, r)), NT, 3)
+        for rr in range(2):
+            for s in range(N_SEG):
+                for of in range(2):
+                    for c in range(COLS):
+                        fields[s][slot(of, c, r + rr)] = cut_out(field, ((s * 2 + of) * COLS + c) * N_SPACE, rr)
+    for r in range(0, ROWS, 2):
+        copies[1 + ROWS // 2 + r // 2].wait()
+        adjoint = product(part, halves(two_rows(g_ref, r)), NT)
         for rr in range(2):
             for of in range(2):
                 for c in range(COLS):
-                    base = (of * COLS + c) * N_DEST
-                    values[slot(of, c, r + rr)] = field[base : base + N_DEST, LANES * rr : LANES * (rr + 1)]
-    copies[2].wait()
-    for r in range(0, ROWS, 2):
-        adjoint = product(part, halves(two_rows(g_ref, r)), NT)
-        for rr in range(2):
-            for c in range(COLS):
-                base = c * N_DEST
-                values[N_FIELD + c * ROWS + r + rr] = adjoint[base : base + N_DEST, LANES * rr : LANES * (rr + 1)]
-    copies[3].wait()
-    copies[4].wait()
+                    adjoints[N_FIELD + slot(of, c, r + rr)] = cut_out(adjoint, (of * COLS + c) * N_SPACE, rr)
+    for copy in copies[1 + ROWS :]:
+        copy.wait()
+    others = {}
+
+    def to_all(row):
+        return jnp.broadcast_to(row, (N_SPACE, LANES))
+
     fill = jnp.zeros((1, LANES - CH), F32)
     for n, ref in enumerate((b_in_ref, b_out_ref)):
         for of in range(2):
-            one = jnp.concatenate([ref[of : of + 1, :], fill], axis=1)
-            values[OFFSET_ROW + 2 * n + of] = jnp.broadcast_to(one, (N_DEST, LANES))
-
-    def put(q, value):
-        out_ref[pl.ds(q, N_DEST, stride=BLOCK), :] = value
-
-    pack_rows(put, N_DEST, values)
-
-
-def middle_kernel(flag_ref, got_ref, w_ref, table_ref, out_ref, grads_ref):
-    is_special = flag_ref[0] == 1
+            others[N_FIELD + 2 * n + of] = to_all(jnp.concatenate([ref[of : of + 1, :], fill], axis=1))
+    start = pl.multiple_of(lax.rem(space, 4) * SHARE, 8)
+    weights = w_ref[space // 4, pl.ds(start, SHARE), :]
+    weights = jnp.concatenate([weights, jnp.zeros((SHARE, LANES - CH), F32)], axis=1)
+    for j in range(SHARE):
+        others[WEIGHT_ROW + j] = to_all(weights[j : j + 1])
+    nothing = jnp.zeros((N_SPACE, LANES), F32)
+
+    for s in range(N_SEG):
+        values = dict(fields[s])
+        for q in range(N_FIELD, 2 * N_FIELD):
+            values[q] = jnp.where(segment == s, adjoints[q], others.get(q, nothing))
+
+        def put(q, value, s=s):
+            out_ref[pl.ds(s * N_SPACE * BLOCK_IN + q, N_SPACE, stride=BLOCK_IN), :] = value
+
+        pack_rows(put, N_SPACE, values, BLOCK_IN)
+
+
+def middle_kernel(place_ref, got_ref, own_w_ref, own_b_ref, table_ref, out_ref, grads_ref, w_ref, b_ref):
+    segment, space = place_ref[0], place_ref[1]
+    is_special = (segment == 0) & (space == 0)
     table = [table_ref[n] for n in range(3)]
     scale = jnp.where(is_special, 1.0, 0.5).astype(F32)
 
     def row(source, q):
         def get(at):
-            return got_ref[pl.ds(source * N_SPACE * BLOCK + at, N_SPACE, stride=BLOCK), :]
-
-        return unpack_row(get, N_SPACE, q)
+            return got_ref[pl.ds(source * N_SPACE * BLOCK_IN + at, N_SPACE, stride=BLOCK_IN), :]
+
+        return unpack_row(get, q, BLOCK_IN)
 
     def field_column(s, c):
         return jnp.concatenate([row(s, slot(of, c, r)) for of in range(2) for r in range(ROWS)], axis=0)
 
     def adjoint_column(c):
-        return jnp.concatenate([row(of, N_FIELD + c * ROWS + r) for of in range(2) for r in range(ROWS)], axis=0)
+        return jnp.concatenate(
+            [row(segment, N_FIELD + slot(of, c, r)) for of in range(2) for r in range(ROWS)], axis=0
+        )
+
+    other = 1 - segment
+    w_ref[segment] = own_w_ref[...]
+    b_ref[segment] = own_b_ref[...]
+    for n in range(4):
+        b_ref[other, n : n + 1, :] = row(other, N_FIELD + n)[:1]
+        for a in range(4):
+            base = pl.multiple_of((other * N_SPACE + 4 * n + a) * BLOCK_IN, 8)
+            main = got_ref[pl.ds(base + WEIGHT_ROW, BLOCK_IN - WEIGHT_ROW), :]
+            main = jnp.where(lane_index(BLOCK_IN - WEIGHT_ROW) < CH, main, 0.0)
+            rest = join_thirds([got_ref[pl.ds(base + EXTRA * third, 8), :] for third in range(3)])
+            w_ref[other, n, pl.ds(SHARE * a, BLOCK_IN - WEIGHT_ROW), :] = main
+            w_ref[other, n, pl.ds(SHARE * a + BLOCK_IN - WEIGHT_ROW, 8), :] = rest
 
     nothing = jnp.zeros((H, LANES), F32)
 
@@ -227,13 +267,16 @@
     )
     adjoints = transform(spread(adjoint_first) + [adjoint_column(1), adjoint_column(2)], 2)
 
-    weights = [thirds(w_ref[n]) for n in range(4)]
+    weights = []
+    gap = jnp.zeros((LANES - CH, 2 * LANES), F32)
+    for s in range(N_SEG):
+        for n in range(2):
+            real, imag = w_ref[s, 2 * n], w_ref[s, 2 * n + 1]
+            top, bottom = jnp.concatenate([real, imag], axis=1), jnp.concatenate([-imag, real], axis=1)
+            weights.append(thirds(jnp.concatenate([top, gap, bottom, gap], axis=0)))
 
     def offset(s, n):
-        def get(at):
-            return got_ref[pl.ds(s * N_SPACE * BLOCK + at, 1), :]
-
-        return jnp.concatenate([unpack_row(get, 1, OFFSET_ROW + 2 * n + of) for of in range(2)], axis=1)
+        return jnp.concatenate([b_ref[s, 2 * n + of : 2 * n + of + 1, :] for of in range(2)], axis=1)
 
     forward = []
     for s in range(2):
@@ -289,16 +332,15 @@
                 for r in range(ROWS):
                     base = (of * ROWS + r) * N_SPACE
                     values[slot(of, c, r)] = columns[c][base : base + N_SPACE]
-        share = 4 * CH // N_SPACE
-        for j in range(share):
-            values[N_FIELD + j] = grads_ref[pl.ds(j, N_SPACE, stride=share), :]
+        for j in range(SHARE):
+            values[N_FIELD + j] = grads_ref[pl.ds(j, N_SPACE, stride=SHARE), :]
         for j in range(4):
-            values[N_FIELD + share + j] = jnp.broadcast_to(offsets[j], (N_SPACE, LANES))
+            values[N_FIELD + SHARE + j] = jnp.broadcast_to(offsets[j], (N_SPACE, LANES))
 
         def put(q, value):
-            out_ref[pl.ds(s * N_SPACE * BLOCK + q, N_SPACE, stride=BLOCK), :] = value
-
-        pack_rows(put, N_SPACE, values)
+            out_ref[pl.ds(s * N_SPACE * BLOCK_OUT + q, N_SPACE, stride=BLOCK_OUT), :] = value
+
+        pack_rows(put, N_SPACE, values, BLOCK_OUT)
 
     parts = [block(adjoints, n) for n in range(4)]
     upstream = jnp.concatenate(leading(parts[0], parts[1]) + ordinary(parts[2]) + ordinary(parts[3]), axis=0)
@@ -317,20 +359,15 @@
 
 
 def total_kernel(got_ref, share_ref, offset_ref):
-    total = got_ref[pl.ds(0, BLOCK), :]
+    total = got_ref[pl.ds(0, BLOCK_OUT), :]
     for d in range(1, N_DEST):
-        total = total + got_ref[pl.ds(d * BLOCK, BLOCK), :]
-    share = 4 * CH // N_SPACE
-    lane = lane_index(16)
-    late = jnp.zeros((16, LANES), F32)
-    for third in range(3):
-        moved = pltpu.roll(total[16 * third : 16 * third + 16], (32 * third - CH) % LANES, 1)
-        late = jnp.where((lane >= 32 * third) & (lane < 32 * third + 32), moved, late)
-    early = BLOCK - N_FIELD
+        total = total + got_ref[pl.ds(d * BLOCK_OUT, BLOCK_OUT), :]
+    late = join_thirds([total[EXTRA * third : EXTRA * (third + 1)] for third in range(3)])
+    early = BLOCK_OUT - N_FIELD
     for p in range(N_SPACE):
-        share_ref[pl.ds(p * share, early), :] = total[N_FIELD:BLOCK]
-        share_ref[pl.ds(p * share + early, share - early), :] = late[: share - early]
-    offset_ref[...] = late[share - early : 16]
+        share_ref[pl.ds(p * SHARE, early), :] = total[N_FIELD:BLOCK_OUT]
+        share_ref[pl.ds(p * SHARE + early, SHARE - early), :] = late[: SHARE - early]
+    offset_ref[...] = late[SHARE - early : EXTRA]
 
 
 def after_kernel(got_ref, g_ref, pair_ref, out_ref):
@@ -339,7 +376,7 @@
         for rr in range(2):
             for of in range(2):
                 for c in range(COLS):
-                    rows.append(got_ref[pl.ds(slot(of, c, 2 * j + rr), N_DEST, stride=BLOCK), :])
+                    rows.append(got_ref[pl.ds(slot(of, c, 2 * j + rr), N_DEST, stride=BLOCK_OUT), :])
         spectrum = halves(jnp.concatenate(rows, axis=0))
         back = product(spectrum, [pair_ref[n] for n in range(2)], TN)
         lanes = pl.ds(2 * W * j, 2 * W)
@@ -363,56 +400,50 @@
     everyone = ("segment", "space")
     block_input, given = acts[0, 0], cotangent[0]
 
-    table_parts = split_table(width_table().reshape(2, COLS * N_DEST, W), 3)
+    by_owner = width_table().reshape(2, COLS, N_SEG, N_SPACE, W).transpose(2, 0, 1, 3, 4)
+    table_parts = split_table(by_owner.reshape(N_SEG, 2 * COLS * N_SPACE, W), 3)
     pair_parts = split_table(row_pair_table(), 2)
     height_parts = split_table(height_table(), 3)
 
-    depth = N_DEST // N_X
-    swap = [(z * N_X + x, (depth - 1 - z) * N_X + x) for z in range(depth) for x in range(N_X)]
-    own_w = [w_in[0, :, 0], w_out[0, :, 0]]
-    other_w = [lax.ppermute(w, everyone, swap) for w in own_w]
-
-    given_arrays = (block_input, given, b_in[0], b_out[0], table_parts)
+    place = jnp.stack([segment, space]).astype(jnp.int32)
+    given_arrays = (block_input, given, b_in[0], b_out[0], w_in[0, :, 0], w_out[0, :, 0], table_parts)
+    copied = [(CH, ROWS * W), (CH, ROWS * W), (2, CH), (2, CH), (4, CH, CH)]
     sent = pl.pallas_call(
         ahead_kernel,
-        out_shape=jax.ShapeDtypeStruct((N_DEST * BLOCK, LANES), F32),
+        out_shape=jax.ShapeDtypeStruct((N_DEST * BLOCK_IN, LANES), F32),
         in_specs=smem() + [pl.BlockSpec(memory_space=pl.ANY)] * len(given_arrays),
         out_specs=pl.BlockSpec(memory_space=pltpu.VMEM),
-        scratch_shapes=[pltpu.VMEM(a.shape, a.dtype) for a in given_arrays]
-        + [pltpu.SemaphoreType.DMA((len(given_arrays),))],
+        scratch_shapes=[pltpu.VMEM(shape, F32) for shape in copied]
+        + [pltpu.VMEM(table_parts.shape, BF16), pltpu.SemaphoreType.DMA((1 + ROWS + 4,))],
         compiler_params=pltpu.CompilerParams(vmem_limit_bytes=AHEAD_VMEM),
         name="ahead",
-    )(segment.astype(jnp.int32).reshape(1), *given_arrays)
-    sent, other_w = lax.optimization_barrier((sent, other_w))
-    got = lax.all_to_all(sent.reshape(N_DEST, BLOCK, LANES), everyone, 0, 0, tiled=True)
-
-    own_w, other_w = jnp.concatenate(own_w), jnp.concatenate(other_w)
-    is_zero = segment == 0
-    all_w = jnp.concatenate([jnp.where(is_zero, own_w, other_w), jnp.where(is_zero, other_w, own_w)])
-    all_w = jnp.pad(all_w, ((0, 0), (0, LANES - CH), (0, LANES - CH))).reshape(4, 2, LANES, LANES)
-    w0, w1 = all_w[:, 0], all_w[:, 1]
-    full_w = jnp.concatenate(
-        [jnp.concatenate([w0, w1], axis=2), jnp.concatenate([-w1, w0], axis=2)], axis=1
-    )
-
-    flag = ((segment == 0) & (space == 0)).astype(jnp.int32).reshape(1)
+    )(place, *given_arrays)
+    got = lax.all_to_all(sent.reshape(N_DEST, BLOCK_IN, LANES), everyone, 0, 0, tiled=True)
+
+    own_w = jnp.concatenate([w_in[0, :, 0], w_out[0, :, 0]])
+    own_w = jnp.pad(own_w, ((0, 0), (0, 0), (0, LANES - CH)))
+    own_b = jnp.pad(jnp.concatenate([b_in[0], b_out[0]]), ((0, 4), (0, LANES - CH)))
+
     sent = pl.pallas_call(
         middle_kernel,
-        out_shape=jax.ShapeDtypeStruct((N_DEST * BLOCK, LANES), F32),
-        in_specs=smem() + vmem(3),
+        out_shape=jax.ShapeDtypeStruct((N_DEST * BLOCK_OUT, LANES), F32),
+        in_specs=smem() + vmem(4),
         out_specs=pl.BlockSpec(memory_space=pltpu.VMEM),
-        scratch_shapes=[pltpu.VMEM((4 * CH, LANES), F32)],
+        scratch_shapes=[
+            pltpu.VMEM((4 * CH, LANES), F32),
+            pltpu.VMEM((N_SEG, 4, CH, LANES), F32),
+            pltpu.VMEM((N_SEG, 8, LANES), F32),
+        ],
         compiler_params=PARAMS,
         name="middle",
-    )(flag, got.reshape(N_DEST * BLOCK, LANES), full_w, height_parts)
-    got = lax.all_to_all(sent.reshape(N_DEST, BLOCK, LANES), everyone, 0, 0, tiled=True)
-    got = got.reshape(N_DEST * BLOCK, LANES)
-
-    share = 4 * CH // N_SPACE
+    )(place, got.reshape(N_DEST * BLOCK_IN, LANES), own_w, own_b, height_parts)
+    got = lax.all_to_all(sent.reshape(N_DEST, BLOCK_OUT, LANES), everyone, 0, 0, tiled=True)
+    got = got.reshape(N_DEST * BLOCK_OUT, LANES)
+
     mine, offsets = pl.pallas_call(
         total_kernel,
         out_shape=(
-            jax.ShapeDtypeStruct((N_SPACE * share, LANES), F32),
+            jax.ShapeDtypeStruct((N_SPACE * SHARE, LANES), F32),
             jax.ShapeDtypeStruct((4, LANES), F32),
         ),
         in_specs=vmem(1),
@@ -420,7 +451,7 @@
         compiler_params=PARAMS,
         name="total",
     )(got)
-    whole = lax.all_to_all(mine.reshape(N_SPACE, share, LANES), "space", 0, 0, tiled=True)
+    whole = lax.all_to_all(mine.reshape(N_SPACE, SHARE, LANES), "space", 0, 0, tiled=True)
 
     adjoint = pl.pallas_call(
         after_kernel,

time: 95.9 us -> 94.3 us (0.983)
  starting transfers between devices: 18.4 us -> 15.5 us
  Pallas kernels: 14.2 us -> 16.1 us
    ppermute x2 -> x0, starting transfers between devices: 6.04 us -> none  [shards(): other_w = [lax.ppermute(w, everyone, swap) for w in own_w]]
    ppermute x2 -> x0, waiting for transfers between devices: 4.94 us -> none  [shards(): other_w = [lax.ppermute(w, everyone, swap) for w in own_w]]
    all_to_all x2, waiting for transfers between devices: 27.8 us -> 32.7 us  [the longest x1 25.5 us: shards(): lax.all_to_all(sent.reshape(N_DEST, BLOCK_IN, LANES), everyone, 0, 0, til...]
    all_to_all x2, starting transfers between devices: 12.3 us -> 15.5 us  [the longest x1 11.5 us: shards(): lax.all_to_all(sent.reshape(N_DEST, BLOCK_IN, LANES), everyone, 0, 0, til...]
    pallas_call x1, Pallas kernels: 4.28 us -> 5.81 us  [shards(): pl.pallas_call(ahead_kernel, out_shape=jax.ShapeDtypeStruct((N_DEST * BLO...]
  transfers between devices with their start and end apart: 4 -> 2, of which waited for: 4 -> 2; matrix products, arithmetic and copies ran while one was open for 1% -> 1% of each run, Pallas kernels for 6% -> 2%
where the time goes in v4:
time: 94.3 us; the launch traced here: 94 us
  waiting for transfers between devices  32.7 us (35%)
  blocking collectives  26.9 us (29%)
  Pallas kernels  16.1 us (17%)
  starting transfers between devices  15.5 us (16%)
  local copies, waits for them, and re-layouts  1.3 us (1%)
    all_to_all x1, blocking collectives, shards(): lax.all_to_all(sent.reshape(N_DEST, BLOCK_OUT, LANES), everyone, 0, 0, ti...  26.9 us
    all_to_all x1, waiting for transfers between devices, shards(): lax.all_to_all(sent.reshape(N_DEST, BLOCK_IN, LANES), everyone, 0, 0, til...  25.5 us
    all_to_all x1, starting transfers between devices, shards(): lax.all_to_all(sent.reshape(N_DEST, BLOCK_IN, LANES), everyone, 0, 0, til...  11.5 us
    pallas_call x1, Pallas kernels, shards(): pl.pallas_call(middle_kernel, out_shape=jax.ShapeDtypeStruct((N_DEST * BL...  7.88 us
    all_to_all x1, waiting for transfers between devices, shards(): lax.all_to_all(mine.reshape(N_SPACE, SHARE, LANES), 'space', 0, 0, tiled=...  7.23 us
    pallas_call x1, Pallas kernels, shards(): pl.pallas_call(ahead_kernel, out_shape=jax.ShapeDtypeStruct((N_DEST * BLO...  5.81 us
    all_to_all x1, starting transfers between devices, shards(): lax.all_to_all(mine.reshape(N_SPACE, SHARE, LANES), 'space', 0, 0, tiled=...  4.02 us
  transfers between devices with their start and end apart: 2, of which 2 were waited for; matrix products, arithmetic and copies ran while one was open for 1% of the time, Pallas kernels for 2%

profile of v4, /device:TPU:8, one launch (start us, length us, event | category | flops | bytes accessed | tf_op | source)
XLA Modules:
  0.0 94.0 jit_solution(5682474956954409904)
XLA Ops:
  0.6 0.6 pad_add_fusion.place_ref
  1.2 5.8 %ahead.1 = f32[1792,128]{1,0:T(8,128)} custom-call(s32[2]{0:T(128)} %pad_add_fusion.place_ref, f32[96,1152]{1,0:T(8,128)} %bitcast.31, f32[96,1152]{1,0:T(8,128)} %bitcast.27, f32[2,96]{1,0:T(2,128)} %bitcast.37, f32[2,96]{1,0:T(2,128)} %bitcast.39, f32[2,96,96]{2,1,0:T(8,128)} %bitcast.33, f32[2,96,96]{2,1,0:T(8,128)} %bitcast.35, ...), custom_call_target="tpu_custom_call" | custom-call | tf_op jit(solution)/shard_map/ahead/pallas_call | solution.py:411
  7.0 0.0 copy-start.6
  7.0 0.0 copy-start.7
  7.1 0.0 copy-start.4
  7.1 0.0 copy-start.5
  7.1 11.5 %all-to-all-start = ((f32[32,56,128]{2,1,0:T(8,128)}), f32[32,56,128]{2,1,0:T(8,128)S(1)}, u32[]{:S(2)}, u32[]{:S(2)}) async-start(f32[32,56,128]{2,1,0:T(8,128)} %bitcast.29), calls=%async_computation | async-start | bytes 1835008 | tf_op jit(solution)/shard_map/all_to_all | solution.py:421
  18.5 0.0 copy-done.6
  18.6 0.0 copy-done.7
  18.6 0.0 copy-start.2
  18.6 0.0 copy-done.4
  18.6 0.0 copy-done.5
  18.6 0.0 copy-start.3
  18.7 25.5 %all-to-all-done = f32[32,56,128]{2,1,0:T(8,128)S(1)} async-done(((f32[32,56,128]{2,1,0:T(8,128)}), f32[32,56,128]{2,1,0:T(8,128)S(1)}, u32[]{:S(2)}, u32[]{:S(2)}) %all-to-all-start) | async-done | bytes 917536 | tf_op jit(solution)/shard_map/all_to_all | solution.py:421
  44.1 0.0 copy-done.2
  44.1 0.0 copy-done.3
  44.1 7.9 %middle.1 = f32[1536,128]{1,0:T(8,128)S(1)} custom-call(s32[2]{0:T(128)S(1)} %copy-done.3, f32[1792,128]{1,0:T(8,128)S(1)} %bitcast.25, f32[4,96,128]{2,1,0:T(8,128)S(1)} %select_maximum_fusion.own_w_ref, f32[8,128]{1,0:T(8,128)S(1)} %select_maximum_fusion.1.own_b_ref, bf16[3,192,192]{2,1,0:T(8,128)(2,1)S(1)} %copy-done.2), custom_call_target="tpu_custom_call" | custom-call | tf_op jit(solution)/shard_map/middle/pallas_call | solution.py:427
  52.0 26.9 %all_to_all.15 = f32[32,48,128]{2,1,0:T(8,128)S(1)} all-to-all(f32[32,48,128]{2,1,0:T(8,128)S(1)} %bitcast.26), channel_id=1, replica_groups=mesh['segment'=2,'space'=16,'chan'=8] {'segment','space'}, dimensions={0} | all-to-all | bytes 1572864 | tf_op jit(solution)/shard_map/all_to_all | solution.py:440
  79.0 0.0 copy-start
  79.0 0.0 copy-start.1
  79.0 0.8 total.1
  79.8 4.0 %all-to-all-start.2 = ((f32[16,24,128]{2,1,0:T(8,128)}), f32[16,24,128]{2,1,0:T(8,128)S(1)}, u32[]{:S(2)}, u32[]{:S(2)}) async-start(f32[16,24,128]{2,1,0:T(8,128)} %bitcast.13), calls=%async_computation.2 | async-start | bytes 393216 | tf_op jit(solution)/shard_map/all_to_all | solution.py:454
  83.8 0.0 copy-done
  83.8 0.0 copy-done.1
  83.8 1.6 %after.1 = f32[96,1152]{1,0:T(8,128)} custom-call(f32[1536,128]{1,0:T(8,128)S(1)} %bitcast.24, f32[96,1152]{1,0:T(8,128)S(1)} %bitcast.28, bf16[2,384,384]{2,1,0:T(8,128)(2,1)S(1)} %copy-done.1), custom_call_target="tpu_custom_call" | custom-call | tf_op jit(solution)/shard_map/after/pallas_call | solution.py:456
  85.5 0.6 slice_bitcast_fusion.2
  86.0 7.2 %all-to-all-done.2 = f32[16,24,128]{2,1,0:T(8,128)S(1)} async-done(((f32[16,24,128]{2,1,0:T(8,128)}), f32[16,24,128]{2,1,0:T(8,128)S(1)}, u32[]{:S(2)}, u32[]{:S(2)}) %all-to-all-start.2) | async-done | bytes 196640 | tf_op jit(solution)/shard_map/all_to_all | solution.py:454
  93.3 0.7 slice_bitcast_fusion
  (2 shorter events, 0.0 us)
Async XLA Ops:
  7.0 11.5 %copy-start.6 = (f32[1,2,96]{2,1,0:T(2,128)S(1)}, f32[1,2,96]{2,1,0:T(2,128)}, u32[]{:S(2)}) copy-start(f32[1,2,96]{2,1,0:T(2,128)} %param.13) | copy-start | bytes 2308
  7.0 11.5 %copy-start.7 = (f32[1,2,96]{2,1,0:T(2,128)S(1)}, f32[1,2,96]{2,1,0:T(2,128)}, u32[]{:S(2)}) copy-start(f32[1,2,96]{2,1,0:T(2,128)} %param.14) | copy-start | bytes 2308
  7.1 11.5 %copy-start.4 = (f32[1,2,1,96,96]{4,3,2,1,0:T(8,128)S(1)}, f32[1,2,1,96,96]{4,3,2,1,0:T(8,128)}, u32[]{:S(2)}) copy-start(f32[1,2,1,96,96]{4,3,2,1,0:T(8,128)} %param.11) | copy-start | bytes 221188
  7.1 11.5 %copy-start.5 = (f32[1,2,1,96,96]{4,3,2,1,0:T(8,128)S(1)}, f32[1,2,1,96,96]{4,3,2,1,0:T(8,128)}, u32[]{:S(2)}) copy-start(f32[1,2,1,96,96]{4,3,2,1,0:T(8,128)} %param.12) | copy-start | bytes 221188
  7.1 37.1 %all-to-all-start = ((f32[32,56,128]{2,1,0:T(8,128)}), f32[32,56,128]{2,1,0:T(8,128)S(1)}, u32[]{:S(2)}, u32[]{:S(2)}) async-start(f32[32,56,128]{2,1,0:T(8,128)} %bitcast.29), calls=%async_computation | async-start | bytes 1835008 | tf_op jit(solution)/shard_map/all_to_all | solution.py:421
  18.6 25.6 %copy-start.2 = (bf16[3,192,192]{2,1,0:T(8,128)(2,1)S(1)}, bf16[3,192,192]{2,1,0:T(8,128)(2,1)}, u32[]{:S(2)}) copy-start(bf16[3,192,192]{2,1,0:T(8,128)(2,1)} %constant.22.clone.table_ref) | copy-start | bytes 663556
  18.6 25.5 %copy-start.3 = (s32[2]{0:T(128)S(1)}, s32[2]{0:T(128)}, u32[]{:S(2)}) copy-start(s32[2]{0:T(128)} %pad_add_fusion.place_ref) | copy-start | bytes 28
  79.0 4.9 %copy-start = (f32[1,96,1152]{2,1,0:T(8,128)S(1)}, f32[1,96,1152]{2,1,0:T(8,128)}, u32[]{:S(2)}) copy-start(f32[1,96,1152]{2,1,0:T(8,128)} %param.10) | copy-start | bytes 1327108
  79.0 4.9 %copy-start.1 = (bf16[2,384,384]{2,1,0:T(8,128)(2,1)S(1)}, bf16[2,384,384]{2,1,0:T(8,128)(2,1)}, u32[]{:S(2)}) copy-start(bf16[2,384,384]{2,1,0:T(8,128)(2,1)} %constant.23.clone.pair_ref) | copy-start | bytes 1769476
  79.8 13.5 %all-to-all-start.2 = ((f32[16,24,128]{2,1,0:T(8,128)}), f32[16,24,128]{2,1,0:T(8,128)S(1)}, u32[]{:S(2)}, u32[]{:S(2)}) async-start(f32[16,24,128]{2,1,0:T(8,128)} %bitcast.13), calls=%async_computation.2 | async-start | bytes 393216 | tf_op jit(solution)/shard_map/all_to_all | solution.py:454

commit v5 on v4

--- a/solution.py
+++ b/solution.py
@@ -18,9 +18,8 @@
 N_DEST = N_SPACE * N_SEG
 ROWS = H // N_SPACE
 COLS = W // 2 // N_DEST
-EXTRA = 16
-BLOCK_IN = 56
-BLOCK_OUT = 48
+BLOCK_IN, EXTRA_IN = 51, 17
+BLOCK_OUT, EXTRA_OUT = 48, 16
 SHRINK = 0.3
 BF16 = jnp.bfloat16
 F32 = jnp.float32
@@ -105,20 +104,19 @@
 
 
 N_FIELD = 2 * COLS * ROWS
-WEIGHT_ROW = N_FIELD + 4
+OWN = 32
+OFFSET_ROW = 2 * N_FIELD - OWN
+WEIGHT_ROW = OFFSET_ROW + 4
 SHARE = 4 * CH // N_SPACE
 
 
-def pack_rows(put, count, values, block):
+def pack_rows(put, count, values, block, extras):
     lane = lane_index(count)
     for q in range(block):
-        value = values.get(q)
-        if value is None:
-            value = jnp.zeros((count, LANES), F32)
-        third, extra = divmod(q, EXTRA)
-        packed = values.get(block + extra)
-        if packed is not None and third < 3:
-            value = jnp.where(lane < CH, value, pltpu.roll(packed, CH - 32 * third, 1))
+        third, extra = divmod(q, extras)
+        value = values[q]
+        if third < 3:
+            value = jnp.where(lane < CH, value, pltpu.roll(values[block + extra], CH - 32 * third, 1))
         put(q, value)
 
 
@@ -131,17 +129,17 @@
     return value
 
 
-def unpack_row(get, q, block):
+def unpack_row(get, q, block, extras):
     if q < block:
         return get(q)
-    return join_thirds([get(q - block + EXTRA * third) for third in range(3)])
+    return join_thirds([get(q - block + extras * third) for third in range(3)])
 
 
 def ahead_kernel(
-    place_ref, x_hbm, g_hbm, b_in_hbm, b_out_hbm, w_in_hbm, w_out_hbm, table_hbm,
+    x_hbm, g_hbm, b_in_hbm, b_out_hbm, w_in_hbm, w_out_hbm, table_hbm,
     out_ref, x_ref, g_ref, b_in_ref, b_out_ref, w_ref, table_ref, sems,
 ):
-    segment, space = place_ref[0], place_ref[1]
+    segment, space = lax.axis_index("segment"), lax.axis_index("space")
     pairs = [(table_hbm, table_ref)]
     for src, dst in ((x_hbm, x_ref), (g_hbm, g_ref)):
         for j in range(ROWS // 2):
@@ -163,7 +161,11 @@
 
     copies[0].wait()
     table = [table_ref[n].reshape(N_SEG * 2 * COLS * N_SPACE, W) for n in range(3)]
-    part = [table_ref[n, segment] for n in range(2)]
+    last = (2 * COLS - 1) * N_SPACE
+    part = [
+        jnp.concatenate([table_ref[n, segment], table_ref[n, 1 - segment, last:, :]], axis=0) for n in range(2)
+    ]
+    others = {}
     for r in range(0, ROWS, 2):
         copies[1 + r // 2].wait()
         field = product(table, thirds(two_rows(x_ref, r)), NT, 3)
@@ -178,10 +180,13 @@
         for rr in range(2):
             for of in range(2):
                 for c in range(COLS):
-                    adjoints[N_FIELD + slot(of, c, r + rr)] = cut_out(adjoint, (of * COLS + c) * N_SPACE, rr)
+                    at = slot(of, c, r + rr)
+                    if at < OWN:
+                        adjoints[N_FIELD + at] = cut_out(adjoint, (of * COLS + c) * N_SPACE, rr)
+                    else:
+                        others[N_FIELD + at - OWN] = cut_out(adjoint, last + N_SPACE, rr)
     for copy in copies[1 + ROWS :]:
         copy.wait()
-    others = {}
 
     def to_all(row):
         return jnp.broadcast_to(row, (N_SPACE, LANES))
@@ -189,27 +194,26 @@
     fill = jnp.zeros((1, LANES - CH), F32)
     for n, ref in enumerate((b_in_ref, b_out_ref)):
         for of in range(2):
-            others[N_FIELD + 2 * n + of] = to_all(jnp.concatenate([ref[of : of + 1, :], fill], axis=1))
+            others[OFFSET_ROW + 2 * n + of] = to_all(jnp.concatenate([ref[of : of + 1, :], fill], axis=1))
     start = pl.multiple_of(lax.rem(space, 4) * SHARE, 8)
     weights = w_ref[space // 4, pl.ds(start, SHARE), :]
     weights = jnp.concatenate([weights, jnp.zeros((SHARE, LANES - CH), F32)], axis=1)
     for j in range(SHARE):
         others[WEIGHT_ROW + j] = to_all(weights[j : j + 1])
-    nothing = jnp.zeros((N_SPACE, LANES), F32)
 
     for s in range(N_SEG):
         values = dict(fields[s])
-        for q in range(N_FIELD, 2 * N_FIELD):
-            values[q] = jnp.where(segment == s, adjoints[q], others.get(q, nothing))
+        for q in range(N_FIELD, N_FIELD + OWN):
+            values[q] = jnp.where(segment == s, adjoints[q], others[q])
 
         def put(q, value, s=s):
             out_ref[pl.ds(s * N_SPACE * BLOCK_IN + q, N_SPACE, stride=BLOCK_IN), :] = value
 
-        pack_rows(put, N_SPACE, values, BLOCK_IN)
-
-
-def middle_kernel(place_ref, got_ref, own_w_ref, own_b_ref, table_ref, out_ref, grads_ref, w_ref, b_ref):
-    segment, space = place_ref[0], place_ref[1]
+        pack_rows(put, N_SPACE, values, BLOCK_IN, EXTRA_IN)
+
+
+def middle_kernel(got_ref, own_w_ref, own_b_ref, table_ref, out_ref, grads_ref, w_ref, b_ref):
+    segment, space = lax.axis_index("segment"), lax.axis_index("space")
     is_special = (segment == 0) & (space == 0)
     table = [table_ref[n] for n in range(3)]
     scale = jnp.where(is_special, 1.0, 0.5).astype(F32)
@@ -218,28 +222,26 @@
         def get(at):
             return got_ref[pl.ds(source * N_SPACE * BLOCK_IN + at, N_SPACE, stride=BLOCK_IN), :]
 
-        return unpack_row(get, q, BLOCK_IN)
+        return unpack_row(get, q, BLOCK_IN, EXTRA_IN)
 
     def field_column(s, c):
         return jnp.concatenate([row(s, slot(of, c, r)) for of in range(2) for r in range(ROWS)], axis=0)
 
+    other = 1 - segment
+
+    def adjoint_row(at):
+        return row(segment, N_FIELD + at) if at < OWN else row(other, N_FIELD + at - OWN)
+
     def adjoint_column(c):
-        return jnp.concatenate(
-            [row(segment, N_FIELD + slot(of, c, r)) for of in range(2) for r in range(ROWS)], axis=0
-        )
-
-    other = 1 - segment
-    w_ref[segment] = own_w_ref[...]
+        return jnp.concatenate([adjoint_row(slot(of, c, r)) for of in range(2) for r in range(ROWS)], axis=0)
+
+    w_ref[pl.ds(pl.multiple_of(segment * 4 * CH, 8), 4 * CH), :] = own_w_ref[...]
     b_ref[segment] = own_b_ref[...]
+    inside = lane_index(N_SPACE) < CH
     for n in range(4):
-        b_ref[other, n : n + 1, :] = row(other, N_FIELD + n)[:1]
-        for a in range(4):
-            base = pl.multiple_of((other * N_SPACE + 4 * n + a) * BLOCK_IN, 8)
-            main = got_ref[pl.ds(base + WEIGHT_ROW, BLOCK_IN - WEIGHT_ROW), :]
-            main = jnp.where(lane_index(BLOCK_IN - WEIGHT_ROW) < CH, main, 0.0)
-            rest = join_thirds([got_ref[pl.ds(base + EXTRA * third, 8), :] for third in range(3)])
-            w_ref[other, n, pl.ds(SHARE * a, BLOCK_IN - WEIGHT_ROW), :] = main
-            w_ref[other, n, pl.ds(SHARE * a + BLOCK_IN - WEIGHT_ROW, 8), :] = rest
+        b_ref[other, n : n + 1, :] = row(other, OFFSET_ROW + n)[:1]
+    for j in range(SHARE):
+        w_ref[pl.ds(other * 4 * CH + j, N_SPACE, stride=SHARE), :] = jnp.where(inside, row(other, WEIGHT_ROW + j), 0.0)
 
     nothing = jnp.zeros((H, LANES), F32)
 
@@ -271,7 +273,7 @@
     gap = jnp.zeros((LANES - CH, 2 * LANES), F32)
     for s in range(N_SEG):
         for n in range(2):
-            real, imag = w_ref[s, 2 * n], w_ref[s, 2 * n + 1]
+            real, imag = (w_ref[pl.ds((4 * s + 2 * n + of) * CH, CH), :] for of in range(2))
             top, bottom = jnp.concatenate([real, imag], axis=1), jnp.concatenate([-imag, real], axis=1)
             weights.append(thirds(jnp.concatenate([top, gap, bottom, gap], axis=0)))
 
@@ -340,7 +342,7 @@
         def put(q, value):
             out_ref[pl.ds(s * N_SPACE * BLOCK_OUT + q, N_SPACE, stride=BLOCK_OUT), :] = value
 
-        pack_rows(put, N_SPACE, values, BLOCK_OUT)
+        pack_rows(put, N_SPACE, values, BLOCK_OUT, EXTRA_OUT)
 
     parts = [block(adjoints, n) for n in range(4)]
     upstream = jnp.concatenate(leading(parts[0], parts[1]) + ordinary(parts[2]) + ordinary(parts[3]), axis=0)
@@ -362,12 +364,12 @@
     total = got_ref[pl.ds(0, BLOCK_OUT), :]
     for d in range(1, N_DEST):
         total = total + got_ref[pl.ds(d * BLOCK_OUT, BLOCK_OUT), :]
-    late = join_thirds([total[EXTRA * third : EXTRA * (third + 1)] for third in range(3)])
+    late = join_thirds([total[EXTRA_OUT * third : EXTRA_OUT * (third + 1)] for third in range(3)])
     early = BLOCK_OUT - N_FIELD
     for p in range(N_SPACE):
         share_ref[pl.ds(p * SHARE, early), :] = total[N_FIELD:BLOCK_OUT]
         share_ref[pl.ds(p * SHARE + early, SHARE - early), :] = late[: SHARE - early]
-    offset_ref[...] = late[SHARE - early : EXTRA]
+    offset_ref[...] = late[SHARE - early : EXTRA_OUT]
 
 
 def after_kernel(got_ref, g_ref, pair_ref, out_ref):
@@ -387,16 +389,10 @@
     return [pl.BlockSpec(memory_space=pltpu.VMEM)] * count
 
 
-def smem():
-    return [pl.BlockSpec(memory_space=pltpu.SMEM)]
-
-
 PARAMS = pltpu.CompilerParams(vmem_limit_bytes=VMEM_LIMIT)
 
 
 def shards(acts, cotangent, w_in, w_out, b_in, b_out):
-    segment = lax.axis_index("segment")
-    space = lax.axis_index("space")
     everyone = ("segment", "space")
     block_input, given = acts[0, 0], cotangent[0]
 
@@ -405,38 +401,37 @@
     pair_parts = split_table(row_pair_table(), 2)
     height_parts = split_table(height_table(), 3)
 
-    place = jnp.stack([segment, space]).astype(jnp.int32)
     given_arrays = (block_input, given, b_in[0], b_out[0], w_in[0, :, 0], w_out[0, :, 0], table_parts)
     copied = [(CH, ROWS * W), (CH, ROWS * W), (2, CH), (2, CH), (4, CH, CH)]
     sent = pl.pallas_call(
         ahead_kernel,
         out_shape=jax.ShapeDtypeStruct((N_DEST * BLOCK_IN, LANES), F32),
-        in_specs=smem() + [pl.BlockSpec(memory_space=pl.ANY)] * len(given_arrays),
+        in_specs=[pl.BlockSpec(memory_space=pl.ANY)] * len(given_arrays),
         out_specs=pl.BlockSpec(memory_space=pltpu.VMEM),
         scratch_shapes=[pltpu.VMEM(shape, F32) for shape in copied]
         + [pltpu.VMEM(table_parts.shape, BF16), pltpu.SemaphoreType.DMA((1 + ROWS + 4,))],
         compiler_params=pltpu.CompilerParams(vmem_limit_bytes=AHEAD_VMEM),
         name="ahead",
-    )(place, *given_arrays)
-    got = lax.all_to_all(sent.reshape(N_DEST, BLOCK_IN, LANES), everyone, 0, 0, tiled=True)
+    )(*given_arrays)
+    got = lax.all_to_all(sent.reshape(N_DEST, BLOCK_IN, 1, LANES), everyone, 0, 0, tiled=True)
 
     own_w = jnp.concatenate([w_in[0, :, 0], w_out[0, :, 0]])
-    own_w = jnp.pad(own_w, ((0, 0), (0, 0), (0, LANES - CH)))
+    own_w = jnp.pad(own_w, ((0, 0), (0, 0), (0, LANES - CH))).reshape(4 * CH, LANES)
     own_b = jnp.pad(jnp.concatenate([b_in[0], b_out[0]]), ((0, 4), (0, LANES - CH)))
 
     sent = pl.pallas_call(
         middle_kernel,
         out_shape=jax.ShapeDtypeStruct((N_DEST * BLOCK_OUT, LANES), F32),
-        in_specs=smem() + vmem(4),
+        in_specs=vmem(4),
         out_specs=pl.BlockSpec(memory_space=pltpu.VMEM),
         scratch_shapes=[
             pltpu.VMEM((4 * CH, LANES), F32),
-            pltpu.VMEM((N_SEG, 4, CH, LANES), F32),
+            pltpu.VMEM((N_SEG * 4 * CH, LANES), F32),
             pltpu.VMEM((N_SEG, 8, LANES), F32),
         ],
         compiler_params=PARAMS,
         name="middle",
-    )(place, got.reshape(N_DEST * BLOCK_IN, LANES), own_w, own_b, height_parts)
+    )(got.reshape(N_DEST * BLOCK_IN, LANES), own_w, own_b, height_parts)
     got = lax.all_to_all(sent.reshape(N_DEST, BLOCK_OUT, LANES), everyone, 0, 0, tiled=True)
     got = got.reshape(N_DEST * BLOCK_OUT, LANES)
 

time: 94.3 us -> 90.7 us (0.962)
  waiting for transfers between devices: 32.7 us -> 31.1 us
  Pallas kernels: 16.1 us -> 14.9 us
    all_to_all x1, waiting for transfers between devices: 25.5 us -> 23.8 us  [shards(): lax.all_to_all(sent.reshape(N_DEST, BLOCK_IN, 1, LANES), everyone, 0, 0,...]
where the time goes in v5:
time: 90.7 us; the launch traced here: 90.4 us
  waiting for transfers between devices  31.1 us (34%)
  blocking collectives  26.9 us (30%)
  starting transfers between devices  15.5 us (17%)
  Pallas kernels  14.9 us (16%)
  local copies, waits for them, and re-layouts  1.29 us (1%)
    all_to_all x1, blocking collectives, shards(): lax.all_to_all(sent.reshape(N_DEST, BLOCK_OUT, LANES), everyone, 0, 0, ti...  26.9 us
    all_to_all x1, waiting for transfers between devices, shards(): lax.all_to_all(sent.reshape(N_DEST, BLOCK_IN, 1, LANES), everyone, 0, 0,...  23.8 us
    all_to_all x1, starting transfers between devices, shards(): lax.all_to_all(sent.reshape(N_DEST, BLOCK_IN, 1, LANES), everyone, 0, 0,...  11.5 us
    pallas_call x1, Pallas kernels, shards(): pl.pallas_call(middle_kernel, out_shape=jax.ShapeDtypeStruct((N_DEST * BL...  7.31 us
    all_to_all x1, waiting for transfers between devices, shards(): lax.all_to_all(mine.reshape(N_SPACE, SHARE, LANES), 'space', 0, 0, tiled=...  7.23 us
    pallas_call x1, Pallas kernels, shards(): pl.pallas_call(ahead_kernel, out_shape=jax.ShapeDtypeStruct((N_DEST * BLO...  5.14 us
    all_to_all x1, starting transfers between devices, shards(): lax.all_to_all(mine.reshape(N_SPACE, SHARE, LANES), 'space', 0, 0, tiled=...  4.03 us
  transfers between devices with their start and end apart: 2, of which 2 were waited for; matrix products, arithmetic and copies ran while one was open for 1% of the time, Pallas kernels for 2%

profile of v5, /device:TPU:8, one launch (start us, length us, event | category | flops | bytes accessed | tf_op | source)
XLA Modules:
  0.0 90.4 jit_solution(8696646022844687909)
XLA Ops:
  0.6 5.1 %ahead.1 = f32[1632,128]{1,0:T(8,128)} custom-call(f32[96,1152]{1,0:T(8,128)} %bitcast.31, f32[96,1152]{1,0:T(8,128)} %bitcast.26, f32[2,96]{1,0:T(2,128)} %bitcast.37, f32[2,96]{1,0:T(2,128)} %bitcast.39, f32[2,96,96]{2,1,0:T(8,128)} %bitcast.33, f32[2,96,96]{2,1,0:T(8,128)} %bitcast.35, bf16[3,2,96,192]{3,2,1,0:T(8,128)(2,1)} %constant.9.clone.table_hbm), custom_call_target="tpu_custom_call" | custom-call | tf_op jit(solution)/shard_map/ahead/pallas_call | solution.py:406
  5.8 0.0 copy-start.5
  5.8 0.0 copy-start.6
  5.8 0.0 copy-start.3
  5.8 0.0 copy-start.4
  5.8 11.5 %all-to-all-start = ((f32[32,51,1,128]{3,2,1,0:T(1,128)}), f32[32,51,1,128]{3,2,1,0:T(1,128)S(1)}, u32[]{:S(2)}, u32[]{:S(2)}) async-start(f32[32,51,1,128]{3,2,1,0:T(1,128)} %bitcast.29), calls=%async_computation | async-start | bytes 1671168 | tf_op jit(solution)/shard_map/all_to_all | solution.py:416
  17.3 0.0 copy-done.5
  17.3 0.0 copy-done.6
  17.3 0.0 copy-start.2
  17.3 0.0 copy-done.3
  17.3 0.0 copy-done.4
  17.4 23.8 %all-to-all-done = f32[32,51,1,128]{3,2,1,0:T(1,128)S(1)} async-done(((f32[32,51,1,128]{3,2,1,0:T(1,128)}), f32[32,51,1,128]{3,2,1,0:T(1,128)S(1)}, u32[]{:S(2)}, u32[]{:S(2)}) %all-to-all-start) | async-done | bytes 835616 | tf_op jit(solution)/shard_map/all_to_all | solution.py:416
  41.2 0.0 copy-done.2
  41.2 7.3 %middle.1 = f32[1536,128]{1,0:T(8,128)S(1)} custom-call(f32[1632,128]{1,0:T(8,128)S(1)} %bitcast.24, f32[384,128]{1,0:T(8,128)S(1)} %bitcast.28, f32[8,128]{1,0:T(8,128)S(1)} %select_maximum_fusion.1.own_b_ref, bf16[3,192,192]{2,1,0:T(8,128)(2,1)S(1)} %copy-done.2), custom_call_target="tpu_custom_call" | custom-call | tf_op jit(solution)/shard_map/middle/pallas_call | solution.py:422
  48.5 26.9 %all_to_all.15 = f32[32,48,128]{2,1,0:T(8,128)S(1)} all-to-all(f32[32,48,128]{2,1,0:T(8,128)S(1)} %bitcast.25), channel_id=1, replica_groups=mesh['segment'=2,'space'=16,'chan'=8] {'segment','space'}, dimensions={0} | all-to-all | bytes 1572864 | tf_op jit(solution)/shard_map/all_to_all | solution.py:435
  75.4 0.0 copy-start
  75.4 0.0 copy-start.1
  75.4 0.8 total.1
  76.2 4.0 %all-to-all-start.2 = ((f32[16,24,128]{2,1,0:T(8,128)}), f32[16,24,128]{2,1,0:T(8,128)S(1)}, u32[]{:S(2)}, u32[]{:S(2)}) async-start(f32[16,24,128]{2,1,0:T(8,128)} %bitcast.12), calls=%async_computation.2 | async-start | bytes 393216 | tf_op jit(solution)/shard_map/all_to_all | solution.py:449
  80.3 0.0 copy-done
  80.3 0.0 copy-done.1
  80.3 1.6 %after.1 = f32[96,1152]{1,0:T(8,128)} custom-call(f32[1536,128]{1,0:T(8,128)S(1)} %bitcast.23, f32[96,1152]{1,0:T(8,128)S(1)} %bitcast.27, bf16[2,384,384]{2,1,0:T(8,128)(2,1)S(1)} %copy-done.1), custom_call_target="tpu_custom_call" | custom-call | tf_op jit(solution)/shard_map/after/pallas_call | solution.py:451
  81.9 0.6 slice_bitcast_fusion.2
  82.5 7.2 %all-to-all-done.2 = f32[16,24,128]{2,1,0:T(8,128)S(1)} async-done(((f32[16,24,128]{2,1,0:T(8,128)}), f32[16,24,128]{2,1,0:T(8,128)S(1)}, u32[]{:S(2)}, u32[]{:S(2)}) %all-to-all-start.2) | async-done | bytes 196640 | tf_op jit(solution)/shard_map/all_to_all | solution.py:449
  89.7 0.7 slice_bitcast_fusion
  (2 shorter events, 0.0 us)
Async XLA Ops:
  5.8 11.5 %copy-start.5 = (f32[1,2,96]{2,1,0:T(2,128)S(1)}, f32[1,2,96]{2,1,0:T(2,128)}, u32[]{:S(2)}) copy-start(f32[1,2,96]{2,1,0:T(2,128)} %param.13) | copy-start | bytes 2308
  5.8 11.5 %copy-start.6 = (f32[1,2,96]{2,1,0:T(2,128)S(1)}, f32[1,2,96]{2,1,0:T(2,128)}, u32[]{:S(2)}) copy-start(f32[1,2,96]{2,1,0:T(2,128)} %param.14) | copy-start | bytes 2308
  5.8 11.5 %copy-start.3 = (f32[1,2,1,96,96]{4,3,2,1,0:T(8,128)S(1)}, f32[1,2,1,96,96]{4,3,2,1,0:T(8,128)}, u32[]{:S(2)}) copy-start(f32[1,2,1,96,96]{4,3,2,1,0:T(8,128)} %param.11) | copy-start | bytes 221188
  5.8 11.5 %copy-start.4 = (f32[1,2,1,96,96]{4,3,2,1,0:T(8,128)S(1)}, f32[1,2,1,96,96]{4,3,2,1,0:T(8,128)}, u32[]{:S(2)}) copy-start(f32[1,2,1,96,96]{4,3,2,1,0:T(8,128)} %param.12) | copy-start | bytes 221188
  5.8 35.4 %all-to-all-start = ((f32[32,51,1,128]{3,2,1,0:T(1,128)}), f32[32,51,1,128]{3,2,1,0:T(1,128)S(1)}, u32[]{:S(2)}, u32[]{:S(2)}) async-start(f32[32,51,1,128]{3,2,1,0:T(1,128)} %bitcast.29), calls=%async_computation | async-start | bytes 1671168 | tf_op jit(solution)/shard_map/all_to_all | solution.py:416
  17.3 23.9 %copy-start.2 = (bf16[3,192,192]{2,1,0:T(8,128)(2,1)S(1)}, bf16[3,192,192]{2,1,0:T(8,128)(2,1)}, u32[]{:S(2)}) copy-start(bf16[3,192,192]{2,1,0:T(8,128)(2,1)} %constant.10.clone.table_ref) | copy-start | bytes 663556
  75.4 4.9 %copy-start = (f32[1,96,1152]{2,1,0:T(8,128)S(1)}, f32[1,96,1152]{2,1,0:T(8,128)}, u32[]{:S(2)}) copy-start(f32[1,96,1152]{2,1,0:T(8,128)} %param.10) | copy-start | bytes 1327108
  75.4 4.9 %copy-start.1 = (bf16[2,384,384]{2,1,0:T(8,128)(2,1)S(1)}, bf16[2,384,384]{2,1,0:T(8,128)(2,1)}, u32[]{:S(2)}) copy-start(bf16[2,384,384]{2,1,0:T(8,128)(2,1)} %constant.11.clone.pair_ref) | copy-start | bytes 1769476
  76.2 13.5 %all-to-all-start.2 = ((f32[16,24,128]{2,1,0:T(8,128)}), f32[16,24,128]{2,1,0:T(8,128)S(1)}, u32[]{:S(2)}, u32[]{:S(2)}) async-start(f32[16,24,128]{2,1,0:T(8,128)} %bitcast.12), calls=%async_computation.2 | async-start | bytes 393216 | tf_op jit(solution)/shard_map/all_to_all | solution.py:449

commit v6 on v5

--- a/solution.py
+++ b/solution.py
@@ -21,6 +21,7 @@
 BLOCK_IN, EXTRA_IN = 51, 17
 BLOCK_OUT, EXTRA_OUT = 48, 16
 SHRINK = 0.3
+WIDE = 256
 BF16 = jnp.bfloat16
 F32 = jnp.float32
 VMEM_LIMIT = 24 * 1024 * 1024
@@ -80,14 +81,21 @@
     return cut(value, 3)
 
 
+def terms(parts):
+    return [(n, order - n) for order in reversed(range(parts)) for n in range(order + 1)]
+
+
 def product(a, b, contract, parts=2):
-    dims = (contract, ((), ()))
-    total = None
-    for order in reversed(range(parts)):
-        for n in range(order + 1):
-            one = lax.dot_general(a[n], b[order - n], dims, preferred_element_type=F32)
-            total = one if total is None else total + one
-    return total
+    (left,), (right,) = contract
+    if isinstance(a, list):
+        a = jnp.concatenate([a[n] for n, _ in terms(parts)], axis=left)
+    b = jnp.concatenate([b[n] for _, n in terms(parts)], axis=right)
+    return lax.dot_general(a, b, (contract, ((), ())), preferred_element_type=F32)
+
+
+def lay_out(split, parts, width):
+    pad = [(0, 0)] * (split.ndim - 2) + [(0, width - split.shape[-1])]
+    return np.concatenate([np.pad(split[n], pad) for n, _ in terms(parts)], axis=-1)
 
 
 NN = ((1,), (0,))
@@ -137,11 +145,12 @@
 
 def ahead_kernel(
     x_hbm, g_hbm, b_in_hbm, b_out_hbm, w_in_hbm, w_out_hbm, table_hbm,
-    out_ref, x_ref, g_ref, b_in_ref, b_out_ref, w_ref, table_ref, sems,
+    out_hbm, x_ref, g_ref, b_in_ref, b_out_ref, w_ref, table_ref, out_ref, sems,
 ):
     segment, space = lax.axis_index("segment"), lax.axis_index("space")
     pairs = [(table_hbm, table_ref)]
     for src, dst in ((x_hbm, x_ref), (g_hbm, g_ref)):
+        dst[:, pl.ds(ROWS * W, LANES)] = jnp.zeros((CH, LANES), F32)
         for j in range(ROWS // 2):
             lanes = pl.ds(2 * W * j, 2 * W)
             pairs.append((src.at[:, lanes], dst.at[:, lanes]))
@@ -149,25 +158,27 @@
     copies = [pltpu.make_async_copy(src, dst, sems.at[n]) for n, (src, dst) in enumerate(pairs)]
     for copy in copies:
         copy.start()
-    pad = jnp.zeros((LANES - CH, W), F32)
+    pad = jnp.zeros((LANES - CH, WIDE), F32)
     fields = [{} for _ in range(N_SEG)]
     adjoints = {}
 
     def two_rows(ref, r):
-        return jnp.concatenate([ref[:, pl.ds(W * r, W)], pad, ref[:, pl.ds(W * (r + 1), W)], pad], axis=0)
+        return jnp.concatenate([ref[:, pl.ds(W * r, WIDE)], pad, ref[:, pl.ds(W * (r + 1), WIDE)], pad], axis=0)
 
     def cut_out(value, base, rr):
         return value[base : base + N_SPACE, LANES * rr : LANES * (rr + 1)]
 
     copies[0].wait()
-    table = [table_ref[n].reshape(N_SEG * 2 * COLS * N_SPACE, W) for n in range(3)]
+    table = table_ref[...].reshape(N_SEG * 2 * COLS * N_SPACE, 6 * WIDE)
     last = (2 * COLS - 1) * N_SPACE
-    part = [
-        jnp.concatenate([table_ref[n, segment], table_ref[n, 1 - segment, last:, :]], axis=0) for n in range(2)
-    ]
+    short = pl.ds(3 * WIDE, 3 * WIDE)
+    part = jnp.concatenate([table_ref[segment, :, short], table_ref[1 - segment, last:, short]], axis=0)
     others = {}
     for r in range(0, ROWS, 2):
-        copies[1 + r // 2].wait()
+        if r == 0:
+            copies[1].wait()
+        if r + 2 < ROWS:
+            copies[2 + r // 2].wait()
         field = product(table, thirds(two_rows(x_ref, r)), NT, 3)
         for rr in range(2):
             for s in range(N_SEG):
@@ -175,7 +186,10 @@
                     for c in range(COLS):
                         fields[s][slot(of, c, r + rr)] = cut_out(field, ((s * 2 + of) * COLS + c) * N_SPACE, rr)
     for r in range(0, ROWS, 2):
-        copies[1 + ROWS // 2 + r // 2].wait()
+        if r == 0:
+            copies[1 + ROWS // 2].wait()
+        if r + 2 < ROWS:
+            copies[2 + ROWS // 2 + r // 2].wait()
         adjoint = product(part, halves(two_rows(g_ref, r)), NT)
         for rr in range(2):
             for of in range(2):
@@ -201,6 +215,7 @@
     for j in range(SHARE):
         others[WEIGHT_ROW + j] = to_all(weights[j : j + 1])
 
+    sends = []
     for s in range(N_SEG):
         values = dict(fields[s])
         for q in range(N_FIELD, N_FIELD + OWN):
@@ -210,12 +225,16 @@
             out_ref[pl.ds(s * N_SPACE * BLOCK_IN + q, N_SPACE, stride=BLOCK_IN), :] = value
 
         pack_rows(put, N_SPACE, values, BLOCK_IN, EXTRA_IN)
-
-
-def middle_kernel(got_ref, own_w_ref, own_b_ref, table_ref, out_ref, grads_ref, w_ref, b_ref):
+        half = pl.ds(s * N_SPACE * BLOCK_IN, N_SPACE * BLOCK_IN)
+        sends.append(pltpu.make_async_copy(out_ref.at[half], out_hbm.at[half], sems.at[len(copies) + s]))
+        sends[-1].start()
+    for send in sends:
+        send.wait()
+
+
+def middle_kernel(got_ref, own_w_ref, own_b_ref, long_ref, short_ref, out_ref, grads_ref, w_ref, b_ref):
     segment, space = lax.axis_index("segment"), lax.axis_index("space")
     is_special = (segment == 0) & (space == 0)
-    table = [table_ref[n] for n in range(3)]
     scale = jnp.where(is_special, 1.0, 0.5).astype(F32)
 
     def row(source, q):
@@ -261,6 +280,7 @@
         return [jnp.concatenate([v[:H], v[H:]], axis=1) for v in (one, mirror)]
 
     def transform(columns, parts):
+        table = long_ref[...] if parts == 3 else short_ref[...]
         return product(table, cut(jnp.concatenate(columns, axis=1), parts), NN, parts)
 
     adjoint_first = adjoint_column(0)
@@ -397,19 +417,25 @@
     block_input, given = acts[0, 0], cotangent[0]
 
     by_owner = width_table().reshape(2, COLS, N_SEG, N_SPACE, W).transpose(2, 0, 1, 3, 4)
-    table_parts = split_table(by_owner.reshape(N_SEG, 2 * COLS * N_SPACE, W), 3)
+    width_parts = split_table(by_owner.reshape(N_SEG, 2 * COLS * N_SPACE, W), 3)
+    width_terms = lay_out(width_parts, 3, WIDE)
     pair_parts = split_table(row_pair_table(), 2)
     height_parts = split_table(height_table(), 3)
-
-    given_arrays = (block_input, given, b_in[0], b_out[0], w_in[0, :, 0], w_out[0, :, 0], table_parts)
-    copied = [(CH, ROWS * W), (CH, ROWS * W), (2, CH), (2, CH), (4, CH, CH)]
+    height_terms = [lay_out(height_parts, parts, 2 * H) for parts in (3, 2)]
+
+    given_arrays = (block_input, given, b_in[0], b_out[0], w_in[0, :, 0], w_out[0, :, 0], width_terms)
+    copied = [(CH, ROWS * W + LANES), (CH, ROWS * W + LANES), (2, CH), (2, CH), (4, CH, CH)]
     sent = pl.pallas_call(
         ahead_kernel,
         out_shape=jax.ShapeDtypeStruct((N_DEST * BLOCK_IN, LANES), F32),
         in_specs=[pl.BlockSpec(memory_space=pl.ANY)] * len(given_arrays),
-        out_specs=pl.BlockSpec(memory_space=pltpu.VMEM),
+        out_specs=pl.BlockSpec(memory_space=pl.ANY),
         scratch_shapes=[pltpu.VMEM(shape, F32) for shape in copied]
-        + [pltpu.VMEM(table_parts.shape, BF16), pltpu.SemaphoreType.DMA((1 + ROWS + 4,))],
+        + [
+            pltpu.VMEM(width_terms.shape, BF16),
+            pltpu.VMEM((N_DEST * BLOCK_IN, LANES), F32),
+            pltpu.SemaphoreType.DMA((1 + ROWS + 4 + N_SEG,)),
+        ],
         compiler_params=pltpu.CompilerParams(vmem_limit_bytes=AHEAD_VMEM),
         name="ahead",
     )(*given_arrays)
@@ -422,7 +448,7 @@
     sent = pl.pallas_call(
         middle_kernel,
         out_shape=jax.ShapeDtypeStruct((N_DEST * BLOCK_OUT, LANES), F32),
-        in_specs=vmem(4),
+        in_specs=vmem(5),
         out_specs=pl.BlockSpec(memory_space=pltpu.VMEM),
         scratch_shapes=[
             pltpu.VMEM((4 * CH, LANES), F32),
@@ -431,7 +457,7 @@
         ],
         compiler_params=PARAMS,
         name="middle",
-    )(got.reshape(N_DEST * BLOCK_IN, LANES), own_w, own_b, height_parts)
+    )(got.reshape(N_DEST * BLOCK_IN, LANES), own_w, own_b, *height_terms)
     got = lax.all_to_all(sent.reshape(N_DEST, BLOCK_OUT, LANES), everyone, 0, 0, tiled=True)
     got = got.reshape(N_DEST * BLOCK_OUT, LANES)
 

time: 90.7 us -> 89.8 us (0.990)
  Pallas kernels: 14.9 us -> 13.9 us
where the time goes in v6:
time: 89.8 us; the launch traced here: 89.5 us
  waiting for transfers between devices  31.1 us (35%)
  blocking collectives  26.9 us (30%)
  starting transfers between devices  15.5 us (17%)
  Pallas kernels  13.9 us (15%)
  local copies, waits for them, and re-layouts  1.3 us (1%)
    all_to_all x1, blocking collectives, shards(): lax.all_to_all(sent.reshape(N_DEST, BLOCK_OUT, LANES), everyone, 0, 0, ti...  26.9 us
    all_to_all x1, waiting for transfers between devices, shards(): lax.all_to_all(sent.reshape(N_DEST, BLOCK_IN, 1, LANES), everyone, 0, 0,...  23.8 us
    all_to_all x1, starting transfers between devices, shards(): lax.all_to_all(sent.reshape(N_DEST, BLOCK_IN, 1, LANES), everyone, 0, 0,...  11.5 us
    all_to_all x1, waiting for transfers between devices, shards(): lax.all_to_all(mine.reshape(N_SPACE, SHARE, LANES), 'space', 0, 0, tiled=...  7.27 us
    pallas_call x1, Pallas kernels, shards(): pl.pallas_call(middle_kernel, out_shape=jax.ShapeDtypeStruct((N_DEST * BL...  6.88 us
    pallas_call x1, Pallas kernels, shards(): pl.pallas_call(ahead_kernel, out_shape=jax.ShapeDtypeStruct((N_DEST * BLO...  4.63 us
    all_to_all x1, starting transfers between devices, shards(): lax.all_to_all(mine.reshape(N_SPACE, SHARE, LANES), 'space', 0, 0, tiled=...  4.03 us
  transfers between devices with their start and end apart: 2, of which 2 were waited for; matrix products, arithmetic and copies ran while one was open for 1% of the time, Pallas kernels for 2%

profile of v6, /device:TPU:8, one launch (start us, length us, event | category | flops | bytes accessed | tf_op | source)
XLA Modules:
  0.0 89.5 jit_solution(3126944284275777471)
XLA Ops:
  0.6 4.6 %ahead.1 = f32[1632,128]{1,0:T(8,128)} custom-call(f32[96,1152]{1,0:T(8,128)} %bitcast.31, f32[96,1152]{1,0:T(8,128)} %bitcast.26, f32[2,96]{1,0:T(2,128)} %bitcast.37, f32[2,96]{1,0:T(2,128)} %bitcast.39, f32[2,96,96]{2,1,0:T(8,128)} %bitcast.33, f32[2,96,96]{2,1,0:T(8,128)} %bitcast.35, bf16[2,96,1536]{2,1,0:T(8,128)(2,1)} %constant.11.clone.table_hbm), custom_call_target="tpu_custom_call" | custom-call | tf_op jit(solution)/shard_map/ahead/pallas_call | solution.py:428
  5.3 0.0 copy-start.6
  5.3 0.0 copy-start.7
  5.3 0.0 copy-start.4
  5.3 0.0 copy-start.5
  5.3 0.0 copy-start.2
  5.3 11.5 %all-to-all-start = ((f32[32,51,1,128]{3,2,1,0:T(1,128)}), f32[32,51,1,128]{3,2,1,0:T(1,128)S(1)}, u32[]{:S(2)}, u32[]{:S(2)}) async-start(f32[32,51,1,128]{3,2,1,0:T(1,128)} %bitcast.29), calls=%async_computation | async-start | bytes 1671168 | tf_op jit(solution)/shard_map/all_to_all | solution.py:442
  16.8 0.0 copy-done.6
  16.8 0.0 copy-done.7
  16.8 0.0 copy-start.3
  16.8 0.0 copy-done.4
  16.9 0.0 copy-done.5
  16.9 23.8 %all-to-all-done = f32[32,51,1,128]{3,2,1,0:T(1,128)S(1)} async-done(((f32[32,51,1,128]{3,2,1,0:T(1,128)}), f32[32,51,1,128]{3,2,1,0:T(1,128)S(1)}, u32[]{:S(2)}, u32[]{:S(2)}) %all-to-all-start) | async-done | bytes 835616 | tf_op jit(solution)/shard_map/all_to_all | solution.py:442
  40.7 0.0 copy-done.2
  40.7 0.0 copy-done.3
  40.7 6.9 %middle.1 = f32[1536,128]{1,0:T(8,128)S(1)} custom-call(f32[1632,128]{1,0:T(8,128)S(1)} %bitcast.24, f32[384,128]{1,0:T(8,128)S(1)} %bitcast.28, f32[8,128]{1,0:T(8,128)S(1)} %select_maximum_fusion.1.own_b_ref, bf16[192,1152]{1,0:T(8,128)(2,1)S(1)} %copy-done.2, bf16[192,576]{1,0:T(8,128)(2,1)S(1)} %copy-done.3), custom_call_target="tpu_custom_call" | custom-call | tf_op jit(solution)/shard_map/middle/pallas_call | solution.py:448
  47.6 26.9 %all_to_all.15 = f32[32,48,128]{2,1,0:T(8,128)S(1)} all-to-all(f32[32,48,128]{2,1,0:T(8,128)S(1)} %bitcast.25), channel_id=1, replica_groups=mesh['segment'=2,'space'=16,'chan'=8] {'segment','space'}, dimensions={0} | all-to-all | bytes 1572864 | tf_op jit(solution)/shard_map/all_to_all | solution.py:461
  74.5 0.0 copy-start
  74.5 0.0 copy-start.1
  74.5 0.8 total.1
  75.3 4.0 %all-to-all-start.2 = ((f32[16,24,128]{2,1,0:T(8,128)}), f32[16,24,128]{2,1,0:T(8,128)S(1)}, u32[]{:S(2)}, u32[]{:S(2)}) async-start(f32[16,24,128]{2,1,0:T(8,128)} %bitcast.12), calls=%async_computation.2 | async-start | bytes 393216 | tf_op jit(solution)/shard_map/all_to_all | solution.py:475
  79.3 0.0 copy-done
  79.4 0.0 copy-done.1
  79.4 1.6 %after.1 = f32[96,1152]{1,0:T(8,128)} custom-call(f32[1536,128]{1,0:T(8,128)S(1)} %bitcast.23, f32[96,1152]{1,0:T(8,128)S(1)} %bitcast.27, bf16[2,384,384]{2,1,0:T(8,128)(2,1)S(1)} %copy-done.1), custom_call_target="tpu_custom_call" | custom-call | tf_op jit(solution)/shard_map/after/pallas_call | solution.py:477
  81.0 0.6 slice_bitcast_fusion.2
  81.5 7.3 %all-to-all-done.2 = f32[16,24,128]{2,1,0:T(8,128)S(1)} async-done(((f32[16,24,128]{2,1,0:T(8,128)}), f32[16,24,128]{2,1,0:T(8,128)S(1)}, u32[]{:S(2)}, u32[]{:S(2)}) %all-to-all-start.2) | async-done | bytes 196640 | tf_op jit(solution)/shard_map/all_to_all | solution.py:475
  88.8 0.7 slice_bitcast_fusion
  (2 shorter events, 0.0 us)
Async XLA Ops:
  5.3 11.5 %copy-start.6 = (f32[1,2,96]{2,1,0:T(2,128)S(1)}, f32[1,2,96]{2,1,0:T(2,128)}, u32[]{:S(2)}) copy-start(f32[1,2,96]{2,1,0:T(2,128)} %param.14) | copy-start | bytes 2308
  5.3 11.5 %copy-start.7 = (f32[1,2,96]{2,1,0:T(2,128)S(1)}, f32[1,2,96]{2,1,0:T(2,128)}, u32[]{:S(2)}) copy-start(f32[1,2,96]{2,1,0:T(2,128)} %param.15) | copy-start | bytes 2308
  5.3 11.6 %copy-start.4 = (f32[1,2,1,96,96]{4,3,2,1,0:T(8,128)S(1)}, f32[1,2,1,96,96]{4,3,2,1,0:T(8,128)}, u32[]{:S(2)}) copy-start(f32[1,2,1,96,96]{4,3,2,1,0:T(8,128)} %param.12) | copy-start | bytes 221188
  5.3 11.6 %copy-start.5 = (f32[1,2,1,96,96]{4,3,2,1,0:T(8,128)S(1)}, f32[1,2,1,96,96]{4,3,2,1,0:T(8,128)}, u32[]{:S(2)}) copy-start(f32[1,2,1,96,96]{4,3,2,1,0:T(8,128)} %param.13) | copy-start | bytes 221188
  5.3 35.4 %copy-start.2 = (bf16[192,1152]{1,0:T(8,128)(2,1)S(1)}, bf16[192,1152]{1,0:T(8,128)(2,1)}, u32[]{:S(2)}) copy-start(bf16[192,1152]{1,0:T(8,128)(2,1)} %constant.12.clone.long_ref) | copy-start | bytes 1327108
  5.3 35.4 %all-to-all-start = ((f32[32,51,1,128]{3,2,1,0:T(1,128)}), f32[32,51,1,128]{3,2,1,0:T(1,128)S(1)}, u32[]{:S(2)}, u32[]{:S(2)}) async-start(f32[32,51,1,128]{3,2,1,0:T(1,128)} %bitcast.29), calls=%async_computation | async-start | bytes 1671168 | tf_op jit(solution)/shard_map/all_to_all | solution.py:442
  16.8 23.9 %copy-start.3 = (bf16[192,576]{1,0:T(8,128)(2,1)S(1)}, bf16[192,576]{1,0:T(8,128)(2,1)}, u32[]{:S(2)}) copy-start(bf16[192,576]{1,0:T(8,128)(2,1)} %constant.13.clone.short_ref) | copy-start | bytes 663556
  74.5 4.9 %copy-start = (f32[1,96,1152]{2,1,0:T(8,128)S(1)}, f32[1,96,1152]{2,1,0:T(8,128)}, u32[]{:S(2)}) copy-start(f32[1,96,1152]{2,1,0:T(8,128)} %param.11) | copy-start | bytes 1327108
  74.5 4.9 %copy-start.1 = (bf16[2,384,384]{2,1,0:T(8,128)(2,1)S(1)}, bf16[2,384,384]{2,1,0:T(8,128)(2,1)}, u32[]{:S(2)}) copy-start(bf16[2,384,384]{2,1,0:T(8,128)(2,1)} %constant.14.clone.pair_ref) | copy-start | bytes 1769476
  75.3 13.5 %all-to-all-start.2 = ((f32[16,24,128]{2,1,0:T(8,128)}), f32[16,24,128]{2,1,0:T(8,128)S(1)}, u32[]{:S(2)}, u32[]{:S(2)}) async-start(f32[16,24,128]{2,1,0:T(8,128)} %bitcast.12), calls=%async_computation.2 | async-start | bytes 393216 | tf_op jit(solution)/shard_map/all_to_all | solution.py:475

commit v7 on v6

--- a/solution.py
+++ b/solution.py
@@ -162,11 +162,13 @@
     fields = [{} for _ in range(N_SEG)]
     adjoints = {}
 
-    def two_rows(ref, r):
-        return jnp.concatenate([ref[:, pl.ds(W * r, WIDE)], pad, ref[:, pl.ds(W * (r + 1), WIDE)], pad], axis=0)
-
-    def cut_out(value, base, rr):
-        return value[base : base + N_SPACE, LANES * rr : LANES * (rr + 1)]
+    def all_rows(ref):
+        return jnp.concatenate(
+            [piece for r in range(ROWS) for piece in (ref[:, pl.ds(W * r, WIDE)], pad)], axis=0
+        )
+
+    def cut_out(value, base, r):
+        return value[base : base + N_SPACE, LANES * r : LANES * (r + 1)]
 
     copies[0].wait()
     table = table_ref[...].reshape(N_SEG * 2 * COLS * N_SPACE, 6 * WIDE)
@@ -174,31 +176,22 @@
     short = pl.ds(3 * WIDE, 3 * WIDE)
     part = jnp.concatenate([table_ref[segment, :, short], table_ref[1 - segment, last:, short]], axis=0)
     others = {}
-    for r in range(0, ROWS, 2):
-        if r == 0:
-            copies[1].wait()
-        if r + 2 < ROWS:
-            copies[2 + r // 2].wait()
-        field = product(table, thirds(two_rows(x_ref, r)), NT, 3)
-        for rr in range(2):
-            for s in range(N_SEG):
-                for of in range(2):
-                    for c in range(COLS):
-                        fields[s][slot(of, c, r + rr)] = cut_out(field, ((s * 2 + of) * COLS + c) * N_SPACE, rr)
-    for r in range(0, ROWS, 2):
-        if r == 0:
-            copies[1 + ROWS // 2].wait()
-        if r + 2 < ROWS:
-            copies[2 + ROWS // 2 + r // 2].wait()
-        adjoint = product(part, halves(two_rows(g_ref, r)), NT)
-        for rr in range(2):
-            for of in range(2):
-                for c in range(COLS):
-                    at = slot(of, c, r + rr)
-                    if at < OWN:
-                        adjoints[N_FIELD + at] = cut_out(adjoint, (of * COLS + c) * N_SPACE, rr)
-                    else:
-                        others[N_FIELD + at - OWN] = cut_out(adjoint, last + N_SPACE, rr)
+    for copy in copies[1 : 1 + ROWS // 2]:
+        copy.wait()
+    field = product(table, thirds(all_rows(x_ref)), NT, 3)
+    for copy in copies[1 + ROWS // 2 : 1 + ROWS]:
+        copy.wait()
+    adjoint = product(part, halves(all_rows(g_ref)), NT)
+    for r in range(ROWS):
+        for of in range(2):
+            for c in range(COLS):
+                at = slot(of, c, r)
+                for s in range(N_SEG):
+                    fields[s][at] = cut_out(field, ((s * 2 + of) * COLS + c) * N_SPACE, r)
+                if at < OWN:
+                    adjoints[N_FIELD + at] = cut_out(adjoint, (of * COLS + c) * N_SPACE, r)
+                else:
+                    others[N_FIELD + at - OWN] = cut_out(adjoint, last + N_SPACE, r)
     for copy in copies[1 + ROWS :]:
         copy.wait()
 

time: 89.8 us -> 89.5 us (level)
  no operation moved by 1% of the time
where the time goes in v7:
time: 89.5 us; the launch traced here: 89.1 us
  waiting for transfers between devices  31.1 us (35%)
  blocking collectives  26.9 us (30%)
  starting transfers between devices  15.5 us (17%)
  Pallas kernels  13.5 us (15%)
  local copies, waits for them, and re-layouts  1.3 us (1%)
    all_to_all x1, blocking collectives, shards(): lax.all_to_all(sent.reshape(N_DEST, BLOCK_OUT, LANES), everyone, 0, 0, ti...  26.9 us
    all_to_all x1, waiting for transfers between devices, shards(): lax.all_to_all(sent.reshape(N_DEST, BLOCK_IN, 1, LANES), everyone, 0, 0,...  23.8 us
    all_to_all x1, starting transfers between devices, shards(): lax.all_to_all(sent.reshape(N_DEST, BLOCK_IN, 1, LANES), everyone, 0, 0,...  11.5 us
    all_to_all x1, waiting for transfers between devices, shards(): lax.all_to_all(mine.reshape(N_SPACE, SHARE, LANES), 'space', 0, 0, tiled=...  7.27 us
    pallas_call x1, Pallas kernels, shards(): pl.pallas_call(middle_kernel, out_shape=jax.ShapeDtypeStruct((N_DEST * BL...  6.88 us
    pallas_call x1, Pallas kernels, shards(): pl.pallas_call(ahead_kernel, out_shape=jax.ShapeDtypeStruct((N_DEST * BLO...  4.25 us
    all_to_all x1, starting transfers between devices, shards(): lax.all_to_all(mine.reshape(N_SPACE, SHARE, LANES), 'space', 0, 0, tiled=...  4.04 us
  transfers between devices with their start and end apart: 2, of which 2 were waited for; matrix products, arithmetic and copies ran while one was open for 1% of the time, Pallas kernels for 2%

profile of v7, /device:TPU:8, one launch (start us, length us, event | category | flops | bytes accessed | tf_op | source)
XLA Modules:
  0.0 89.1 jit_solution(6555936220574942898)
XLA Ops:
  0.6 4.3 %ahead.1 = f32[1632,128]{1,0:T(8,128)} custom-call(f32[96,1152]{1,0:T(8,128)} %bitcast.31, f32[96,1152]{1,0:T(8,128)} %bitcast.26, f32[2,96]{1,0:T(2,128)} %bitcast.37, f32[2,96]{1,0:T(2,128)} %bitcast.39, f32[2,96,96]{2,1,0:T(8,128)} %bitcast.33, f32[2,96,96]{2,1,0:T(8,128)} %bitcast.35, bf16[2,96,1536]{2,1,0:T(8,128)(2,1)} %constant.11.clone.table_hbm), custom_call_target="tpu_custom_call" | custom-call | tf_op jit(solution)/shard_map/ahead/pallas_call | solution.py:421
  4.9 0.0 copy-start.6
  4.9 0.0 copy-start.7
  4.9 0.0 copy-start.4
  4.9 0.0 copy-start.5
  4.9 0.0 copy-start.2
  5.0 11.5 %all-to-all-start = ((f32[32,51,1,128]{3,2,1,0:T(1,128)}), f32[32,51,1,128]{3,2,1,0:T(1,128)S(1)}, u32[]{:S(2)}, u32[]{:S(2)}) async-start(f32[32,51,1,128]{3,2,1,0:T(1,128)} %bitcast.29), calls=%async_computation | async-start | bytes 1671168 | tf_op jit(solution)/shard_map/all_to_all | solution.py:435
  16.4 0.0 copy-done.6
  16.4 0.0 copy-done.7
  16.4 0.0 copy-start.3
  16.5 0.0 copy-done.4
  16.5 0.0 copy-done.5
  16.5 23.8 %all-to-all-done = f32[32,51,1,128]{3,2,1,0:T(1,128)S(1)} async-done(((f32[32,51,1,128]{3,2,1,0:T(1,128)}), f32[32,51,1,128]{3,2,1,0:T(1,128)S(1)}, u32[]{:S(2)}, u32[]{:S(2)}) %all-to-all-start) | async-done | bytes 835616 | tf_op jit(solution)/shard_map/all_to_all | solution.py:435
  40.4 0.0 copy-done.2
  40.4 0.0 copy-done.3
  40.4 6.9 %middle.1 = f32[1536,128]{1,0:T(8,128)S(1)} custom-call(f32[1632,128]{1,0:T(8,128)S(1)} %bitcast.24, f32[384,128]{1,0:T(8,128)S(1)} %bitcast.28, f32[8,128]{1,0:T(8,128)S(1)} %select_maximum_fusion.1.own_b_ref, bf16[192,1152]{1,0:T(8,128)(2,1)S(1)} %copy-done.2, bf16[192,576]{1,0:T(8,128)(2,1)S(1)} %copy-done.3), custom_call_target="tpu_custom_call" | custom-call | tf_op jit(solution)/shard_map/middle/pallas_call | solution.py:441
  47.2 26.9 %all_to_all.15 = f32[32,48,128]{2,1,0:T(8,128)S(1)} all-to-all(f32[32,48,128]{2,1,0:T(8,128)S(1)} %bitcast.25), channel_id=1, replica_groups=mesh['segment'=2,'space'=16,'chan'=8] {'segment','space'}, dimensions={0} | all-to-all | bytes 1572864 | tf_op jit(solution)/shard_map/all_to_all | solution.py:454
  74.1 0.0 copy-start
  74.1 0.0 copy-start.1
  74.1 0.8 total.1
  74.9 4.0 %all-to-all-start.2 = ((f32[16,24,128]{2,1,0:T(8,128)}), f32[16,24,128]{2,1,0:T(8,128)S(1)}, u32[]{:S(2)}, u32[]{:S(2)}) async-start(f32[16,24,128]{2,1,0:T(8,128)} %bitcast.12), calls=%async_computation.2 | async-start | bytes 393216 | tf_op jit(solution)/shard_map/all_to_all | solution.py:468
  79.0 0.0 copy-done
  79.0 0.0 copy-done.1
  79.0 1.6 %after.1 = f32[96,1152]{1,0:T(8,128)} custom-call(f32[1536,128]{1,0:T(8,128)S(1)} %bitcast.23, f32[96,1152]{1,0:T(8,128)S(1)} %bitcast.27, bf16[2,384,384]{2,1,0:T(8,128)(2,1)S(1)} %copy-done.1), custom_call_target="tpu_custom_call" | custom-call | tf_op jit(solution)/shard_map/after/pallas_call | solution.py:470
  80.6 0.6 slice_bitcast_fusion.2
  81.2 7.3 %all-to-all-done.2 = f32[16,24,128]{2,1,0:T(8,128)S(1)} async-done(((f32[16,24,128]{2,1,0:T(8,128)}), f32[16,24,128]{2,1,0:T(8,128)S(1)}, u32[]{:S(2)}, u32[]{:S(2)}) %all-to-all-start.2) | async-done | bytes 196640 | tf_op jit(solution)/shard_map/all_to_all | solution.py:468
  88.4 0.7 slice_bitcast_fusion
  (2 shorter events, 0.0 us)
Async XLA Ops:
  4.9 11.5 %copy-start.6 = (f32[1,2,96]{2,1,0:T(2,128)S(1)}, f32[1,2,96]{2,1,0:T(2,128)}, u32[]{:S(2)}) copy-start(f32[1,2,96]{2,1,0:T(2,128)} %param.14) | copy-start | bytes 2308
  4.9 11.5 %copy-start.7 = (f32[1,2,96]{2,1,0:T(2,128)S(1)}, f32[1,2,96]{2,1,0:T(2,128)}, u32[]{:S(2)}) copy-start(f32[1,2,96]{2,1,0:T(2,128)} %param.15) | copy-start | bytes 2308
  4.9 11.6 %copy-start.4 = (f32[1,2,1,96,96]{4,3,2,1,0:T(8,128)S(1)}, f32[1,2,1,96,96]{4,3,2,1,0:T(8,128)}, u32[]{:S(2)}) copy-start(f32[1,2,1,96,96]{4,3,2,1,0:T(8,128)} %param.12) | copy-start | bytes 221188
  4.9 11.6 %copy-start.5 = (f32[1,2,1,96,96]{4,3,2,1,0:T(8,128)S(1)}, f32[1,2,1,96,96]{4,3,2,1,0:T(8,128)}, u32[]{:S(2)}) copy-start(f32[1,2,1,96,96]{4,3,2,1,0:T(8,128)} %param.13) | copy-start | bytes 221188
  4.9 35.4 %copy-start.2 = (bf16[192,1152]{1,0:T(8,128)(2,1)S(1)}, bf16[192,1152]{1,0:T(8,128)(2,1)}, u32[]{:S(2)}) copy-start(bf16[192,1152]{1,0:T(8,128)(2,1)} %constant.12.clone.long_ref) | copy-start | bytes 1327108
  5.0 35.4 %all-to-all-start = ((f32[32,51,1,128]{3,2,1,0:T(1,128)}), f32[32,51,1,128]{3,2,1,0:T(1,128)S(1)}, u32[]{:S(2)}, u32[]{:S(2)}) async-start(f32[32,51,1,128]{3,2,1,0:T(1,128)} %bitcast.29), calls=%async_computation | async-start | bytes 1671168 | tf_op jit(solution)/shard_map/all_to_all | solution.py:435
  16.4 23.9 %copy-start.3 = (bf16[192,576]{1,0:T(8,128)(2,1)S(1)}, bf16[192,576]{1,0:T(8,128)(2,1)}, u32[]{:S(2)}) copy-start(bf16[192,576]{1,0:T(8,128)(2,1)} %constant.13.clone.short_ref) | copy-start | bytes 663556
  74.1 4.9 %copy-start = (f32[1,96,1152]{2,1,0:T(8,128)S(1)}, f32[1,96,1152]{2,1,0:T(8,128)}, u32[]{:S(2)}) copy-start(f32[1,96,1152]{2,1,0:T(8,128)} %param.11) | copy-start | bytes 1327108
  74.1 4.9 %copy-start.1 = (bf16[2,384,384]{2,1,0:T(8,128)(2,1)S(1)}, bf16[2,384,384]{2,1,0:T(8,128)(2,1)}, u32[]{:S(2)}) copy-start(bf16[2,384,384]{2,1,0:T(8,128)(2,1)} %constant.14.clone.pair_ref) | copy-start | bytes 1769476
  74.9 13.5 %all-to-all-start.2 = ((f32[16,24,128]{2,1,0:T(8,128)}), f32[16,24,128]{2,1,0:T(8,128)S(1)}, u32[]{:S(2)}, u32[]{:S(2)}) async-start(f32[16,24,128]{2,1,0:T(8,128)} %bitcast.12), calls=%async_computation.2 | async-start | bytes 393216 | tf_op jit(solution)/shard_map/all_to_all | solution.py:468

commit v8 on v7

--- a/solution.py
+++ b/solution.py
@@ -171,10 +171,11 @@
         return value[base : base + N_SPACE, LANES * r : LANES * (r + 1)]
 
     copies[0].wait()
-    table = table_ref[...].reshape(N_SEG * 2 * COLS * N_SPACE, 6 * WIDE)
+    table = [table_ref[n].reshape(N_SEG * 2 * COLS * N_SPACE, WIDE) for n in range(3)]
     last = (2 * COLS - 1) * N_SPACE
-    short = pl.ds(3 * WIDE, 3 * WIDE)
-    part = jnp.concatenate([table_ref[segment, :, short], table_ref[1 - segment, last:, short]], axis=0)
+    part = [
+        jnp.concatenate([table_ref[n, segment], table_ref[n, 1 - segment, last:, :]], axis=0) for n in range(2)
+    ]
     others = {}
     for copy in copies[1 : 1 + ROWS // 2]:
         copy.wait()
@@ -411,7 +412,7 @@
 
     by_owner = width_table().reshape(2, COLS, N_SEG, N_SPACE, W).transpose(2, 0, 1, 3, 4)
     width_parts = split_table(by_owner.reshape(N_SEG, 2 * COLS * N_SPACE, W), 3)
-    width_terms = lay_out(width_parts, 3, WIDE)
+    width_terms = np.pad(width_parts, ((0, 0), (0, 0), (0, 0), (0, WIDE - W)))
     pair_parts = split_table(row_pair_table(), 2)
     height_parts = split_table(height_table(), 3)
     height_terms = [lay_out(height_parts, parts, 2 * H) for parts in (3, 2)]

time: 89.5 us -> 89.4 us (level)
  no operation moved by 1% of the time
where the time goes in v8:
time: 89.4 us; the launch traced here: 89.1 us
  waiting for transfers between devices  31.1 us (35%)
  blocking collectives  26.8 us (30%)
  starting transfers between devices  15.5 us (17%)
  Pallas kernels  13.5 us (15%)
  local copies, waits for them, and re-layouts  1.3 us (1%)
    all_to_all x1, blocking collectives, shards(): lax.all_to_all(sent.reshape(N_DEST, BLOCK_OUT, LANES), everyone, 0, 0, ti...  26.8 us
    all_to_all x1, waiting for transfers between devices, shards(): lax.all_to_all(sent.reshape(N_DEST, BLOCK_IN, 1, LANES), everyone, 0, 0,...  23.9 us
    all_to_all x1, starting transfers between devices, shards(): lax.all_to_all(sent.reshape(N_DEST, BLOCK_IN, 1, LANES), everyone, 0, 0,...  11.5 us
    all_to_all x1, waiting for transfers between devices, shards(): lax.all_to_all(mine.reshape(N_SPACE, SHARE, LANES), 'space', 0, 0, tiled=...  7.27 us
    pallas_call x1, Pallas kernels, shards(): pl.pallas_call(middle_kernel, out_shape=jax.ShapeDtypeStruct((N_DEST * BL...  6.88 us
    pallas_call x1, Pallas kernels, shards(): pl.pallas_call(ahead_kernel, out_shape=jax.ShapeDtypeStruct((N_DEST * BLO...  4.22 us
    all_to_all x1, starting transfers between devices, shards(): lax.all_to_all(mine.reshape(N_SPACE, SHARE, LANES), 'space', 0, 0, tiled=...  4.03 us
  transfers between devices with their start and end apart: 2, of which 2 were waited for; matrix products, arithmetic and copies ran while one was open for 1% of the time, Pallas kernels for 2%

profile of v8, /device:TPU:8, one launch (start us, length us, event | category | flops | bytes accessed | tf_op | source)
XLA Modules:
  0.0 89.1 jit_solution(15241369069061700013)
XLA Ops:
  0.6 4.2 %ahead.1 = f32[1632,128]{1,0:T(8,128)} custom-call(f32[96,1152]{1,0:T(8,128)} %bitcast.31, f32[96,1152]{1,0:T(8,128)} %bitcast.26, f32[2,96]{1,0:T(2,128)} %bitcast.37, f32[2,96]{1,0:T(2,128)} %bitcast.39, f32[2,96,96]{2,1,0:T(8,128)} %bitcast.33, f32[2,96,96]{2,1,0:T(8,128)} %bitcast.35, bf16[3,2,96,256]{3,2,1,0:T(8,128)(2,1)} %constant.11.clone.table_hbm), custom_call_target="tpu_custom_call" | custom-call | tf_op jit(solution)/shard_map/ahead/pallas_call | solution.py:422
  4.9 0.0 copy-start.6
  4.9 0.0 copy-start.7
  4.9 0.0 copy-start.4
  4.9 0.0 copy-start.5
  4.9 0.0 copy-start.2
  4.9 11.5 %all-to-all-start = ((f32[32,51,1,128]{3,2,1,0:T(1,128)}), f32[32,51,1,128]{3,2,1,0:T(1,128)S(1)}, u32[]{:S(2)}, u32[]{:S(2)}) async-start(f32[32,51,1,128]{3,2,1,0:T(1,128)} %bitcast.29), calls=%async_computation | async-start | bytes 1671168 | tf_op jit(solution)/shard_map/all_to_all | solution.py:436
  16.4 0.0 copy-done.6
  16.4 0.0 copy-done.7
  16.4 0.0 copy-start.3
  16.4 0.0 copy-done.4
  16.4 0.0 copy-done.5
  16.5 23.9 %all-to-all-done = f32[32,51,1,128]{3,2,1,0:T(1,128)S(1)} async-done(((f32[32,51,1,128]{3,2,1,0:T(1,128)}), f32[32,51,1,128]{3,2,1,0:T(1,128)S(1)}, u32[]{:S(2)}, u32[]{:S(2)}) %all-to-all-start) | async-done | bytes 835616 | tf_op jit(solution)/shard_map/all_to_all | solution.py:436
  40.3 0.0 copy-done.2
  40.3 0.0 copy-done.3
  40.4 6.9 %middle.1 = f32[1536,128]{1,0:T(8,128)S(1)} custom-call(f32[1632,128]{1,0:T(8,128)S(1)} %bitcast.24, f32[384,128]{1,0:T(8,128)S(1)} %bitcast.28, f32[8,128]{1,0:T(8,128)S(1)} %select_maximum_fusion.1.own_b_ref, bf16[192,1152]{1,0:T(8,128)(2,1)S(1)} %copy-done.2, bf16[192,576]{1,0:T(8,128)(2,1)S(1)} %copy-done.3), custom_call_target="tpu_custom_call" | custom-call | tf_op jit(solution)/shard_map/middle/pallas_call | solution.py:442
  47.2 26.8 %all_to_all.15 = f32[32,48,128]{2,1,0:T(8,128)S(1)} all-to-all(f32[32,48,128]{2,1,0:T(8,128)S(1)} %bitcast.25), channel_id=1, replica_groups=mesh['segment'=2,'space'=16,'chan'=8] {'segment','space'}, dimensions={0} | all-to-all | bytes 1572864 | tf_op jit(solution)/shard_map/all_to_all | solution.py:455
  74.1 0.0 copy-start
  74.1 0.0 copy-start.1
  74.1 0.8 total.1
  74.9 4.0 %all-to-all-start.2 = ((f32[16,24,128]{2,1,0:T(8,128)}), f32[16,24,128]{2,1,0:T(8,128)S(1)}, u32[]{:S(2)}, u32[]{:S(2)}) async-start(f32[16,24,128]{2,1,0:T(8,128)} %bitcast.12), calls=%async_computation.2 | async-start | bytes 393216 | tf_op jit(solution)/shard_map/all_to_all | solution.py:469
  78.9 0.0 copy-done
  79.0 0.0 copy-done.1
  79.0 1.6 %after.1 = f32[96,1152]{1,0:T(8,128)} custom-call(f32[1536,128]{1,0:T(8,128)S(1)} %bitcast.23, f32[96,1152]{1,0:T(8,128)S(1)} %bitcast.27, bf16[2,384,384]{2,1,0:T(8,128)(2,1)S(1)} %copy-done.1), custom_call_target="tpu_custom_call" | custom-call | tf_op jit(solution)/shard_map/after/pallas_call | solution.py:471
  80.6 0.6 slice_bitcast_fusion.2
  81.1 7.3 %all-to-all-done.2 = f32[16,24,128]{2,1,0:T(8,128)S(1)} async-done(((f32[16,24,128]{2,1,0:T(8,128)}), f32[16,24,128]{2,1,0:T(8,128)S(1)}, u32[]{:S(2)}, u32[]{:S(2)}) %all-to-all-start.2) | async-done | bytes 196640 | tf_op jit(solution)/shard_map/all_to_all | solution.py:469
  88.4 0.7 slice_bitcast_fusion
  (2 shorter events, 0.0 us)
Async XLA Ops:
  4.9 11.5 %copy-start.6 = (f32[1,2,96]{2,1,0:T(2,128)S(1)}, f32[1,2,96]{2,1,0:T(2,128)}, u32[]{:S(2)}) copy-start(f32[1,2,96]{2,1,0:T(2,128)} %param.14) | copy-start | bytes 2308
  4.9 11.5 %copy-start.7 = (f32[1,2,96]{2,1,0:T(2,128)S(1)}, f32[1,2,96]{2,1,0:T(2,128)}, u32[]{:S(2)}) copy-start(f32[1,2,96]{2,1,0:T(2,128)} %param.15) | copy-start | bytes 2308
  4.9 11.6 %copy-start.4 = (f32[1,2,1,96,96]{4,3,2,1,0:T(8,128)S(1)}, f32[1,2,1,96,96]{4,3,2,1,0:T(8,128)}, u32[]{:S(2)}) copy-start(f32[1,2,1,96,96]{4,3,2,1,0:T(8,128)} %param.12) | copy-start | bytes 221188
  4.9 11.6 %copy-start.5 = (f32[1,2,1,96,96]{4,3,2,1,0:T(8,128)S(1)}, f32[1,2,1,96,96]{4,3,2,1,0:T(8,128)}, u32[]{:S(2)}) copy-start(f32[1,2,1,96,96]{4,3,2,1,0:T(8,128)} %param.13) | copy-start | bytes 221188
  4.9 35.4 %copy-start.2 = (bf16[192,1152]{1,0:T(8,128)(2,1)S(1)}, bf16[192,1152]{1,0:T(8,128)(2,1)}, u32[]{:S(2)}) copy-start(bf16[192,1152]{1,0:T(8,128)(2,1)} %constant.12.clone.long_ref) | copy-start | bytes 1327108
  4.9 35.4 %all-to-all-start = ((f32[32,51,1,128]{3,2,1,0:T(1,128)}), f32[32,51,1,128]{3,2,1,0:T(1,128)S(1)}, u32[]{:S(2)}, u32[]{:S(2)}) async-start(f32[32,51,1,128]{3,2,1,0:T(1,128)} %bitcast.29), calls=%async_computation | async-start | bytes 1671168 | tf_op jit(solution)/shard_map/all_to_all | solution.py:436
  16.4 23.9 %copy-start.3 = (bf16[192,576]{1,0:T(8,128)(2,1)S(1)}, bf16[192,576]{1,0:T(8,128)(2,1)}, u32[]{:S(2)}) copy-start(bf16[192,576]{1,0:T(8,128)(2,1)} %constant.13.clone.short_ref) | copy-start | bytes 663556
  74.1 4.9 %copy-start = (f32[1,96,1152]{2,1,0:T(8,128)S(1)}, f32[1,96,1152]{2,1,0:T(8,128)}, u32[]{:S(2)}) copy-start(f32[1,96,1152]{2,1,0:T(8,128)} %param.11) | copy-start | bytes 1327108
  74.1 4.9 %copy-start.1 = (bf16[2,384,384]{2,1,0:T(8,128)(2,1)S(1)}, bf16[2,384,384]{2,1,0:T(8,128)(2,1)}, u32[]{:S(2)}) copy-start(bf16[2,384,384]{2,1,0:T(8,128)(2,1)} %constant.14.clone.pair_ref) | copy-start | bytes 1769476
  74.9 13.5 %all-to-all-start.2 = ((f32[16,24,128]{2,1,0:T(8,128)}), f32[16,24,128]{2,1,0:T(8,128)S(1)}, u32[]{:S(2)}, u32[]{:S(2)}) async-start(f32[16,24,128]{2,1,0:T(8,128)} %bitcast.12), calls=%async_computation.2 | async-start | bytes 393216 | tf_op jit(solution)/shard_map/all_to_all | solution.py:469
